TPU v7x, 256 devices: a whole 4x4x8 slice. The times are simulated.
256 devices in a mesh: ctx: 32 (over y, x, core), tp: 8 (over z).
Axes of the slice: x: 4, y: 4, z: 8, core: 2. Of those that a mesh axis runs over, the one named last changes fastest.
Arguments:
- hidden: bfloat16 [256, 8192], P('ctx', 'tp')
- norm_gain: float32 [8192], replicated, may hold values from 0.5 to 1.5
- head_weight: bfloat16 [128256, 8192], P(('ctx', 'tp'))
- targets: int32 [256], replicated, may hold values from 0 to 128255
- ref_logprobs: float32 [256], P('ctx'), may hold values from -22 to -10
- block_order: int32 [64], P('ctx'), may hold values from 0 to 63, each once
- lengths: int32 [2], replicated, may hold values from 32 to 128
Outputs:
- loss: float32 [], replicated
- hidden_grad: bfloat16 [256, 8192], P('ctx', 'tp')
Inputs may be any that keep to these rules, and one draw needn't show every extreme that they name: `block_order`: each block number appears once.
All inputs are finite; a program needn't handle non-finite values.
Results may differ from a plain program's by a relative error of at most 0.0034.
Values may be sent and summed in bfloat16 or wider, within the bound.
No kernel may reach another device: no remote copies, remote signals or barrier semaphores. Data moves between devices by JAX's collectives and lax.ppermute only.
A program may use at most 64 MiB of HBM per device.

v0:
```python
import jax
import jax.numpy as jnp
from jax import lax
from jax.sharding import PartitionSpec as P

EPSILON = 1e-05
DPO_BETA = 0.05
LOSS_SCALE = 4096.0


def on_device(hidden, norm_gain, head_weight, targets, ref_logprobs, block_order, lengths):
    tok_dev = hidden.shape[0]
    part_width = hidden.shape[1]
    voc_dev = head_weight.shape[0]
    tp_size = lax.axis_size("tp")
    tp_index = lax.axis_index("tp")
    ctx_index = lax.axis_index("ctx")
    full_width = part_width * tp_size
    own_gain = lax.dynamic_slice_in_dim(norm_gain, tp_index * part_width, part_width)
    hidden_f32 = hidden.astype(jnp.float32)
    features = lax.all_gather(hidden, "tp", axis=1, tiled=True)
    full_rows = features.astype(jnp.float32)
    inv_rms = lax.rsqrt(jnp.mean(full_rows * full_rows, axis=1) + EPSILON)
    normed = (full_rows * inv_rms[:, None] * norm_gain[None, :]).astype(jnp.bfloat16)
    logits = lax.dot_general(
        lax.all_gather(normed, "ctx", axis=0, tiled=True),
        head_weight,
        (((1,), (1,)), ((), ())),
        preferred_element_type=jnp.float32,
    )
    vocab_start = (ctx_index * tp_size + tp_index) * voc_dev
    columns = vocab_start + lax.broadcasted_iota(jnp.int32, (1, voc_dev), 1)
    onehot = targets[:, None] == columns
    picked_part = jnp.sum(jnp.where(onehot, logits, 0.0), axis=1)
    local_top = jnp.max(logits, axis=1)
    row_top = lax.pmax(local_top, ("ctx", "tp"))
    local_total = jnp.sum(jnp.exp(logits - row_top[:, None]), axis=1)
    row_total, picked = lax.psum((local_total, picked_part), ("ctx", "tp"))
    log_total = row_top + jnp.log(row_total)
    shifted = (onehot.astype(jnp.float32) - jnp.exp(logits - log_total[:, None])).astype(
        jnp.bfloat16
    )
    own_logprobs = lax.dynamic_slice_in_dim(picked - log_total, ctx_index * tok_dev, tok_dev)
    block_len = tok_dev // 4
    within = jnp.arange(tok_dev, dtype=jnp.int32)
    seq_index = within // (2 * block_len)
    half_index = within // block_len % 2
    block_start = jnp.where(half_index == 0, block_order[0], block_order[1])
    position = block_start * block_len + within % block_len
    limit = jnp.where(seq_index == 0, lengths[0], lengths[1])
    live_mask = (position < limit).astype(jnp.float32)
    seq_sign = 1.0 - 2.0 * seq_index.astype(jnp.float32)
    log_ratio = (own_logprobs - ref_logprobs) * live_mask
    chosen_part = jnp.sum(jnp.where(seq_index == 0, log_ratio, 0.0))
    rejected_part = jnp.sum(jnp.where(seq_index == 1, log_ratio, 0.0))
    seq_sums = lax.psum(jnp.stack([chosen_part, rejected_part]), "ctx")
    margin = seq_sums[0] - seq_sums[1]
    loss = jax.nn.softplus(-DPO_BETA * margin)
    slope_coef = -DPO_BETA * jax.nn.sigmoid(-DPO_BETA * margin)
    row_grad = slope_coef * seq_sign * live_mask
    full_term = jnp.dot(shifted, head_weight, preferred_element_type=jnp.float32)
    feature_part = lax.psum_scatter(full_term, "tp", scatter_dimension=1, tiled=True)
    grad_part = lax.psum_scatter(feature_part, "ctx", scatter_dimension=0, tiled=True)
    scaled_grad = row_grad[:, None] * grad_part * own_gain[None, :]
    row_dot = lax.psum(jnp.sum(hidden_f32 * scaled_grad, axis=1), "tp") / full_width
    input_grad = (
        inv_rms[:, None] * scaled_grad
        - hidden_f32 * (inv_rms * inv_rms * inv_rms * row_dot)[:, None]
    )
    hidden_grad = (LOSS_SCALE * input_grad).astype(jnp.bfloat16)
    return (loss, hidden_grad)


def solution(mesh):
    placed = (P("ctx", "tp"), P(), P(("ctx", "tp"), None), P(), P("ctx"), P("ctx"), P())
    return jax.shard_map(
        on_device, mesh=mesh, in_specs=placed, out_specs=(P(), P("ctx", "tp")), check_vma=False
    )
```

profile of v0, /device:TPU:1, one launch (start us, length us, event | category | flops | bytes accessed | tf_op | source)
XLA Modules:
  0.0 455.7 jit_solution(10155374028993488482)
XLA Ops:
  7.2 0.0 all-gather.2.cloned.1.call-start
  7.2 23.2 %all_gather.6 = bf16[8,8192]{1,0:T(8,128)(2,1)S(1)} all-gather(bf16[8,1024]{1,0:T(8,128)(2,1)} %param.7), channel_id=1, replica_groups=mesh['ctx'=32,'tp'=8] {'tp'}, dimensions={1}, use_global_device_ids=true | all-gather | bytes 147456 | tf_op jit(solution)/shard_map/all_gather | solution.py:21
  30.5 0.2 fusion.3
  30.6 1.5 fusion.5
  32.2 0.0 all-gather.2.cloned.1.call-update
  32.2 0.0 reduce-scatter.3.cloned.1.call-start
  32.2 0.0 copy-start.1
  32.3 56.9 %all-gather.2.cloned.1.call-done = bf16[256,8192]{1,0:T(8,128)(2,1)} async-done(((bf16[8,8192]{1,0:T(8,128)(2,1)}), bf16[256,8192]{1,0:T(8,128)(2,1)}) %all-gather.2.cloned.1.call-update) | async-done | bytes 4194320 | tf_op jit(solution)/shard_map/all_gather | solution.py:26
  89.2 6.3 %fusion.27 = (f32[256]{0:T(256)S(1)}, f32[256,501]{0,1:T(8,128)S(1)}) fusion(bf16[256,8192]{1,0:T(8,128)(2,1)} %all-gather.2.cloned.1.call-done, bf16[501,8192]{1,0:T(8,128)(2,1)} %param.9), kind=kOutput, calls=%fused_computation.55 | convolution fusion | flops 2101474304 | bytes 12916736 | tf_op jit(solution)/shard_map/dot_general | solution.py:25
  95.5 75.5 %pmax.7 = f32[256]{0:T(256)S(1)} all-reduce(f32[256]{0:T(256)S(1)} %get-tuple-element.18), channel_id=1, replica_groups=mesh['ctx'=32,'tp'=8] {'ctx','tp'}, use_global_device_ids=true, to_apply=%region_4.5 | all-reduce | flops 256 | bytes 2048 | tf_op jit(solution)/shard_map/pmax | solution.py:36
  170.9 0.0 copy-done.1
  171.0 0.2 exponential_reduce_fusion
  171.1 74.3 %all-reduce = (f32[256]{0:T(256)S(1)}, f32[256]{0:T(256)S(1)}) all-reduce(f32[256]{0:T(256)S(1)} %get-tuple-element.3, f32[256]{0:T(256)S(1)} %get-tuple-element.2), channel_id=1, replica_groups=mesh['ctx'=32,'tp'=8] {'ctx','tp'}, use_global_device_ids=true, to_apply=%region_2.3 | all-reduce | flops 512 | bytes 4096 | tf_op jit(solution)/shard_map/psum | solution.py:38
  245.4 9.1 %fusion.6 = f32[256,8192]{1,0:T(8,128)} fusion(bf16[501,8192]{1,0:T(8,128)(2,1)} %param.9, f32[256,501]{0,1:T(8,128)S(1)} %get-tuple-element.19, f32[256]{0:T(256)S(1)} %get-tuple-element.11, s32[256]{0:T(256)S(1)} %copy-done.1, s32[501]{0:T(512)S(1)} %iota_add_fusion), kind=kOutput, calls=%fused_computation.11 | convolution fusion | flops 2101987584 | bytes 17114068 | tf_op jit(solution)/shard_map/dot_general | solution.py:61
  254.5 0.0 copy-start.2
  254.5 0.0 copy-start.3
  254.5 0.0 copy-start.4
  254.5 0.0 copy-start
  254.5 0.0 reduce-scatter.3.cloned.1.call-update
  254.5 0.0 reduce-scatter.5.cloned.1.call-start
  254.6 91.4 %reduce-scatter.3.cloned.1.call-done = f32[256,1024]{1,0:T(8,128)} async-done(((f32[256,8192]{1,0:T(8,128)}), f32[256,1024]{1,0:T(8,128)}) %reduce-scatter.3.cloned.1.call-update) | async-done | bytes 1048592 | tf_op jit(solution)/shard_map/reduce_scatter | solution.py:62
  346.0 0.0 reduce-scatter.5.cloned.1.call-update
  346.0 0.0 copy-done.2
  346.0 0.6 fusion.25
  346.7 0.0 copy-done.3
  346.7 0.6 fusion.26
  347.3 0.0 copy-done.4
  347.3 2.6 subtract_select_fusion
  349.9 0.6 fusion.18
  350.5 1.4 pad_maximum_fusion
  351.9 0.7 dynamic_slice.7
  352.6 62.7 %psum.30 = f32[2]{0:T(128)S(1)} all-reduce(f32[2]{0:T(128)S(1)} %pad_maximum_fusion), channel_id=1, replica_groups=mesh['ctx'=32,'tp'=8] {'ctx'}, use_global_device_ids=true, to_apply=%region_9.10 | all-reduce | flops 2 | bytes 16 | tf_op jit(solution)/shard_map/psum | solution.py:56
  415.2 0.6 fusion.24
  417.3 14.7 %reduce-scatter.5.cloned.1.call-done = f32[8,1024]{1,0:T(8,128)} async-done(((f32[256,1024]{1,0:T(8,128)}), f32[8,1024]{1,0:T(8,128)}) %reduce-scatter.5.cloned.1.call-update) | async-done | bytes 32784 | tf_op jit(solution)/shard_map/reduce_scatter | solution.py:63
  432.0 0.0 copy-done
  432.0 0.9 fusion.11
  432.9 13.7 %psum.31 = f32[8]{0:T(128)S(1)} all-reduce(f32[8]{0:T(128)S(1)} %fusion.11), channel_id=1, replica_groups=mesh['ctx'=32,'tp'=8] {'tp'}, use_global_device_ids=true, to_apply=%region_13.14 | all-reduce | flops 8 | bytes 64 | tf_op jit(solution)/shard_map/psum | solution.py:65
  446.6 1.4 fusion.14
  (5 shorter events, 0.0 us)
Async XLA Ops:
  7.2 82.0 %all-gather.2.cloned.1.call-start = ((), (), s32[]{:S(2)}) async-start(), calls=%async_computation.2 | async-start | bytes 4325376 | tf_op jit(solution)/shard_map/all_gather | solution.py:26
  32.2 313.8 %reduce-scatter.3.cloned.1.call-start = ((), (), s32[]{:S(2)}) async-start(), calls=%async_computation.3 | async-start | bytes 9437184 | tf_op jit(solution)/shard_map/reduce_scatter | solution.py:62
  32.2 138.7 %copy-start.1 = (s32[256]{0:T(256)S(1)}, s32[256]{0:T(256)}, u32[]{:S(2)}) copy-start(s32[256]{0:T(256)} %param.10) | copy-start | bytes 3076
  254.5 91.5 %copy-start.2 = (s32[2]{0:T(128)S(1)}, s32[2]{0:T(128)}, u32[]{:S(2)}) copy-start(s32[2]{0:T(128)} %param.12) | copy-start | bytes 28
  254.5 92.2 %copy-start.3 = (s32[2]{0:T(128)S(1)}, s32[2]{0:T(128)}, u32[]{:S(2)}) copy-start(s32[2]{0:T(128)} %param.13) | copy-start | bytes 28
  254.5 92.7 %copy-start.4 = (f32[8]{0:T(128)S(1)}, f32[8]{0:T(128)}, u32[]{:S(2)}) copy-start(f32[8]{0:T(128)} %param.11) | copy-start | bytes 100
  254.5 177.4 %copy-start = (bf16[8,1024]{1,0:T(8,128)(2,1)S(1)}, bf16[8,1024]{1,0:T(8,128)(2,1)}, u32[]{:S(2)}) copy-start(bf16[8,1024]{1,0:T(8,128)(2,1)} %param.7) | copy-start | bytes 49156
  254.5 177.4 %reduce-scatter.5.cloned.1.call-start = ((), (), s32[]{:S(2)}) async-start(), calls=%async_computation.4 | async-start | bytes 1081344 | tf_op jit(solution)/shard_map/reduce_scatter | solution.py:63
Sparse Core Ops, SparseCore 0:
  32.3 56.8 all-gather.1
  254.7 91.2 reduce-scatter.2
  349.8 82.1 reduce-scatter.4
where the time goes:
time: 461 us; the launch traced here: 456 us
  blocking collectives  249 us (54%)
  waiting for transfers between devices  163 us (35%)
  between operations  16.4 us (4%)
  matrix products  15.3 us (3%)
  other arithmetic  8.88 us (2%)
    reduce_scatter x1, waiting for transfers between devices, on_device(): lax.psum_scatter(full_term, 'tp', scatter_dimension=1, tiled=True)  91.4 us
    pmax x1, blocking collectives, on_device(): row_top = lax.pmax(local_top, ('ctx', 'tp'))  75.5 us
    psum x1, blocking collectives, on_device(): row_total, picked = lax.psum((local_total, picked_part), ('ctx', 'tp'))  74.3 us
    psum x1, blocking collectives, on_device(): seq_sums = lax.psum(jnp.stack([chosen_part, rejected_part]), 'ctx')  62.7 us
    all_gather x1, waiting for transfers between devices, on_device(): lax.all_gather(normed, 'ctx', axis=0, tiled=True)  56.9 us
    all_gather x1, blocking collectives, on_device(): features = lax.all_gather(hidden, 'tp', axis=1, tiled=True)  23.2 us
    reduce_scatter x1, waiting for transfers between devices, on_device(): lax.psum_scatter(feature_part, 'ctx', scatter_dimension=0, tiled=True)  14.7 us
    psum x1, blocking collectives, on_device(): lax.psum(jnp.sum(hidden_f32 * scaled_grad, axis=1), 'tp') / full_width  13.7 us
  transfers between devices with their start and end apart: 3, of which 3 were waited for; matrix products, arithmetic and copies ran while one was open for 2% of the time, Pallas kernels for 0%

commit v1 on v0

v1 whole, which is shorter than its diff:
```python
import jax
import jax.numpy as jnp
from jax import lax
from jax.sharding import Mesh, PartitionSpec as P

EPSILON = 1e-05
DPO_BETA = 0.05
LOSS_SCALE = 4096.0
PLANE = ("y", "x")
CTX = ("y", "x", "c")


def spread(value, axes, count):
    return lax.all_to_all(
        jnp.broadcast_to(value[None], (count,) + value.shape), axes, 0, 0, tiled=True
    )


def other_core(value):
    return lax.ppermute(value, "c", [(0, 1), (1, 0)])


def merge_stats(stats):
    top = jnp.max(stats[:, 0], axis=0)
    total = jnp.sum(stats[:, 1] * jnp.exp(stats[:, 0] - top), axis=0)
    return jnp.stack([top, total, jnp.sum(stats[:, 2], axis=0)])


def on_device(hidden, norm_gain, head_weight, targets, ref_logprobs, block_order, lengths):
    tok_dev, part_width = hidden.shape
    voc_dev, full_width = head_weight.shape
    n_plane = lax.axis_size(PLANE)
    n_ctx = lax.axis_size(CTX)
    n_z = lax.axis_size("z")
    core = lax.axis_index("c")
    z_index = lax.axis_index("z")
    ctx_index = lax.axis_index(CTX)
    rows = tok_dev * n_ctx
    bf16, f32 = jnp.bfloat16, jnp.float32

    features = spread(hidden, "z", n_z).transpose(1, 0, 2).reshape(tok_dev, full_width)
    full_rows = features.astype(f32)
    inv_rms = lax.rsqrt(jnp.mean(full_rows * full_rows, axis=1) + EPSILON)
    normed = (full_rows * inv_rms[:, None] * norm_gain[None, :]).astype(bf16)
    own_rows = spread(normed, PLANE, n_plane).reshape(rows // 2, full_width)
    all_rows = jnp.concatenate([own_rows, other_core(own_rows)], axis=0)

    logits = lax.dot_general(
        all_rows, head_weight, (((1,), (1,)), ((), ())), preferred_element_type=f32
    )
    by_core = targets.reshape(n_plane, 2, tok_dev).transpose(1, 0, 2).reshape(2, rows // 2)
    own_first = jnp.where(core == 0, by_core, by_core[::-1]).reshape(rows)
    vocab_start = (ctx_index * n_z + z_index) * voc_dev
    columns = vocab_start + lax.broadcasted_iota(jnp.int32, (1, voc_dev), 1)
    onehot = own_first[:, None] == columns
    picked_part = jnp.sum(jnp.where(onehot, logits, 0.0), axis=1)
    local_top = jnp.max(logits, axis=1)
    local_total = jnp.sum(jnp.exp(logits - local_top[:, None]), axis=1)

    local = jnp.stack([local_top, local_total, picked_part]).reshape(3, 2, rows // 2)
    local = jnp.where(core == 0, local, local[:, ::-1]).reshape(3, rows)
    within = jnp.arange(tok_dev, dtype=jnp.int32)
    block_len = tok_dev // 4
    seq_own = within // (2 * block_len)
    half_index = within // block_len % 2
    block_start = jnp.where(half_index == 0, block_order[0], block_order[1])
    position = block_start * block_len + within % block_len
    limit = jnp.where(seq_own == 0, lengths[0], lengths[1])
    live_own = (position < limit).astype(f32)
    sign_own = 1.0 - 2.0 * seq_own.astype(f32)
    extra = jnp.concatenate([ref_logprobs, live_own * sign_own, jnp.zeros((rows - 2 * tok_dev,), f32)])
    sent = jnp.concatenate([local, extra[None]], axis=0)
    got = spread(sent, CTX, n_ctx)
    over_ctx = merge_stats(got[:, :3])
    aux = got[:, 3, : 2 * tok_dev].reshape(n_plane, 2, 2, tok_dev).transpose(2, 1, 0, 3).reshape(2, rows)
    top, row_total, picked = merge_stats(spread(over_ctx, "z", n_z))
    log_total = top + jnp.log(row_total)
    margin = jnp.sum((picked - log_total - aux[0]) * aux[1])
    loss = jax.nn.softplus(-DPO_BETA * margin)
    slope_coef = -DPO_BETA * jax.nn.sigmoid(-DPO_BETA * margin)
    row_grad = slope_coef * sign_own * live_own

    halves = log_total.reshape(2, rows // 2)
    log_total = jnp.where(core == 0, halves, halves[::-1]).reshape(rows)
    shifted = (onehot.astype(f32) - jnp.exp(logits - log_total[:, None])).astype(bf16)
    half = rows // 2
    term_other = jnp.dot(shifted[half:], head_weight, preferred_element_type=f32)
    from_other = other_core(term_other.astype(bf16))
    term_own = jnp.dot(shifted[:half], head_weight, preferred_element_type=f32)
    chip_term = (term_own + from_other.astype(f32)).astype(bf16)
    pieces = lax.all_to_all(
        chip_term.reshape(n_plane, tok_dev, full_width), PLANE, 0, 0, tiled=True
    )
    scaled = jnp.sum(pieces.astype(f32), axis=0) * norm_gain[None, :]
    dot_part = jnp.sum(full_rows * scaled, axis=1)
    last = jnp.concatenate(
        [
            scaled.reshape(tok_dev, n_z, part_width).transpose(1, 0, 2),
            jnp.broadcast_to(dot_part[None, :, None], (n_z, tok_dev, 128)),
        ],
        axis=2,
    )
    last = jnp.sum(lax.all_to_all(last, "z", 0, 0, tiled=True), axis=0)
    scaled_grad = row_grad[:, None] * last[:, :part_width]
    row_dot = row_grad * last[:, part_width] / full_width
    input_grad = (
        inv_rms[:, None] * scaled_grad
        - hidden.astype(f32) * (inv_rms * inv_rms * inv_rms * row_dot)[:, None]
    )
    return (loss, (LOSS_SCALE * input_grad).astype(bf16))


def solution(mesh):
    fine = Mesh(mesh.devices.reshape(4, 4, 2, 8), ("y", "x", "c", "z"))
    placed = (P(CTX, "z"), P(), P(CTX + ("z",), None), P(), P(CTX), P(CTX), P())
    return jax.shard_map(
        on_device, mesh=fine, in_specs=placed, out_specs=(P(), P(CTX, "z")), check_vma=False
    )
```

time: 461 us -> 161 us (0.35); the launches traced: 456 us -> 160 us
  blocking collectives: 249 us -> 69.3 us
  waiting for transfers between devices: 163 us -> 45.7 us
  between operations: 16.4 us -> 2.82 us
  starting transfers between devices: 0.12 us -> 12.6 us
    psum x3 -> x0, blocking collectives: 151 us -> none  [the longest x1 74.3 us: on_device(): row_total, picked = lax.psum((local_total, picked_part), ('ctx', 'tp'))]
    reduce_scatter x2 -> x0, waiting for transfers between devices: 106 us -> none  [the longest x1 91.4 us: on_device(): lax.psum_scatter(full_term, 'tp', scatter_dimension=1, tiled=True)]
    pmax x1 -> x0, blocking collectives: 75.5 us -> none  [on_device(): row_top = lax.pmax(local_top, ('ctx', 'tp'))]
    all_to_all x0 -> x4, blocking collectives: none -> 69.3 us  [spread(): lax.all_to_all(jnp.broadcast_to(value[None], (count,) + value.shape), axe...]
    all_gather x1 -> x0, waiting for transfers between devices: 56.9 us -> none  [on_device(): lax.all_gather(normed, 'ctx', axis=0, tiled=True)]
    all_to_all x0 -> x2, waiting for transfers between devices: none -> 41.9 us  [the longest x1 33 us: on_device(): lax.all_to_all(chip_term.reshape(n_plane, tok_dev, full_width), PLANE, 0,...]
    all_gather x1 -> x0, blocking collectives: 23.2 us -> none  [on_device(): features = lax.all_gather(hidden, 'tp', axis=1, tiled=True)]
    all_to_all x0 -> x2, starting transfers between devices: none -> 7.27 us  [the longest x1 3.85 us: on_device(): lax.all_to_all(chip_term.reshape(n_plane, tok_dev, full_width), PLANE, 0,...]
  transfers between devices with their start and end apart: 3 -> 4, of which waited for: 3 -> 3; matrix products, arithmetic and copies ran while one was open for 2% -> 3% of each run, Pallas kernels for 0% -> 0%
where the time goes in v1:
time: 161 us; the launch traced here: 160 us
  blocking collectives  69.3 us (43%)
  waiting for transfers between devices  45.7 us (28%)
  matrix products  17.8 us (11%)
  starting transfers between devices  12.6 us (8%)
  other arithmetic  9.34 us (6%)
  local copies, waits for them, and re-layouts  2.85 us (2%)
  between operations  2.82 us (2%)
    all_to_all x4, blocking collectives, spread(): lax.all_to_all(jnp.broadcast_to(value[None], (count,) + value.shape), axe...  69.3 us
    all_to_all x1, waiting for transfers between devices, on_device(): lax.all_to_all(chip_term.reshape(n_plane, tok_dev, full_width), PLANE, 0,...  33 us
    all_to_all x1, waiting for transfers between devices, on_device(): last = jnp.sum(lax.all_to_all(last, 'z', 0, 0, tiled=True), axis=0)  8.85 us
    dot_general x1, matrix products, on_device(): term_own = jnp.dot(shifted[:half], head_weight, preferred_element_type=f32)  6.47 us
    dot_general x1, matrix products, on_device(): lax.dot_general(all_rows, head_weight, (((1,), (1,)), ((), ())), preferre...  6.33 us
    ppermute x2, starting transfers between devices, other_core(): return lax.ppermute(value, 'c', [(0, 1), (1, 0)])  5.31 us
    dot_general x1, matrix products, on_device(): jnp.dot(shifted[half:], head_weight, preferred_element_type=f32)  4.97 us
    all_to_all x1, starting transfers between devices, on_device(): lax.all_to_all(chip_term.reshape(n_plane, tok_dev, full_width), PLANE, 0,...  3.85 us
  transfers between devices with their start and end apart: 4, of which 3 were waited for; matrix products, arithmetic and copies ran while one was open for 3% of the time, Pallas kernels for 0%

profile of v1, /device:TPU:1, one launch (start us, length us, event | category | flops | bytes accessed | tf_op | source)
XLA Modules:
  0.0 160.4 jit_solution(17167513383481282214)
XLA Ops:
  0.6 0.0 copy-start.4
  0.6 0.0 copy-start.2
  0.7 0.0 copy-start.3
  0.7 0.0 copy-start.5
  0.7 0.8 broadcast_in_dim.71
  1.4 16.6 %all_to_all.30 = bf16[8,8,1024]{2,1,0:T(8,128)(2,1)S(1)} all-to-all(bf16[8,8,1024]{2,1,0:T(8,128)(2,1)S(1)} %broadcast_in_dim.71), channel_id=1, replica_groups=mesh['y'=4,'x'=4,'c'=2,'z'=8] {'z'}, dimensions={0} | all-to-all | bytes 262144 | tf_op jit(solution)/shard_map/all_to_all | solution.py:14
  18.0 0.2 fusion.9
  18.2 0.9 multiply_convert_fusion
  19.1 0.2 broadcast_in_dim.72
  19.3 32.6 %all_to_all.31 = bf16[16,8,8192]{2,1,0:T(8,128)(2,1)S(1)} all-to-all(bf16[16,8,8192]{2,1,0:T(8,128)(2,1)S(1)} %broadcast_in_dim.72), channel_id=1, replica_groups=mesh['y'=4,'x'=4,'c'=2,'z'=8] {'y','x'}, dimensions={0} | all-to-all | bytes 4194304 | tf_op jit(solution)/shard_map/all_to_all | solution.py:14
  51.9 3.5 %collective-permute-start = (bf16[128,8192]{1,0:T(8,128)(2,1)S(1)}, bf16[128,8192]{1,0:T(8,128)(2,1)}, u32[]{:S(2)}, u32[]{:S(2)}) collective-permute-start(bf16[128,8192]{1,0:T(8,128)(2,1)S(1)} %bitcast.70), channel_id=1, source_target_pairs={{0,8},{8,0},{1,9},{9,1},{2,10},{10,2},{3,11},{11,3},{4,12},{12,4},... | collective-permute-start | bytes 6291464 | tf_op jit(solution)/shard_map/ppermute | solution.py:20
  55.4 0.0 copy-done.4
  55.4 0.1 reshape.303
  55.5 0.1 reshape.304
  55.6 0.0 copy-done.2
  55.6 0.6 fusion.62
  56.2 0.0 copy-done.3
  56.2 0.6 fusion.61
  56.8 2.5 %broadcast_select_fusion = (f32[8]{0:T(128)S(1)}, pred[8]{0:T(512)(128)(4,1)S(1)}) fusion(s32[]{:T(128)} %bitcast.11, s32[]{:T(128)} %bitcast.10, s32[]{:T(128)} %bitcast.9, s32[]{:T(128)} %bitcast.8), kind=kLoop, calls=%fused_computation.110 | loop fusion | flops 320 | bytes 56 | tf_op jit(solution)/shard_map/mul | solution.py:71
  59.3 0.0 copy-done.5
  59.3 0.1 pad_maximum_fusion.4
  59.4 0.0 collective-permute-done
  59.4 6.3 %fusion.63 = (f32[256]{0:T(256)S(1)}, f32[256,501]{0,1:T(8,128)S(1)}) fusion(bf16[501,8192]{1,0:T(8,128)(2,1)} %param.9, bf16[128,8192]{1,0:T(8,128)(2,1)} %collective-permute-done, bf16[128,8192]{1,0:T(8,128)(2,1)S(1)} %bitcast.71), kind=kOutput, calls=%fused_computation.120 | convolution fusion | flops 2109862912 | bytes 12916736 | tf_op jit(solution)/shard_map/dot_general | solution.py:48
  65.7 0.2 exponential_reduce_fusion
  66.0 10.8 %all_to_all.32 = f32[32,4,256]{2,1,0:T(4,128)S(1)} all-to-all(f32[32,4,256]{2,1,0:T(4,128)S(1)} %broadcast_in_dim.80), channel_id=1, replica_groups=mesh['y'=4,'x'=4,'c'=2,'z'=8] {'y','x','c'}, dimensions={0} | all-to-all | bytes 262144 | tf_op jit(solution)/shard_map/all_to_all | solution.py:14
  76.8 0.1 slice_reduce_fusion.4
  77.0 9.4 %all_to_all.33 = f32[8,3,256]{2,1,0:T(4,128)S(1)} all-to-all(f32[8,3,256]{2,1,0:T(4,128)S(1)} %broadcast_in_dim.81), channel_id=1, replica_groups=mesh['y'=4,'x'=4,'c'=2,'z'=8] {'z'}, dimensions={0} | all-to-all | bytes 49152 | tf_op jit(solution)/shard_map/all_to_all | solution.py:14
  86.4 0.1 fusion.7
  86.6 5.0 %convolution_convert_fusion = bf16[128,8192]{1,0:T(8,128)(2,1)S(1)} fusion(bf16[501,8192]{1,0:T(8,128)(2,1)} %param.9, bf16[256,501]{0,1:T(8,128)(2,1)S(1)} %fusion.7), kind=kOutput, calls=%fused_computation | convolution fusion | flops 1051721728 | bytes 10434560 | tf_op jit(solution)/shard_map/dot_general | solution.py:87
  91.6 1.8 %collective-permute-start.1 = (bf16[128,8192]{1,0:T(8,128)(2,1)S(1)}, bf16[128,8192]{1,0:T(8,128)(2,1)S(1)}, u32[]{:S(2)}, u32[]{:S(2)}) collective-permute-start(bf16[128,8192]{1,0:T(8,128)(2,1)S(1)} %convolution_convert_fusion), channel_id=1, source_target_pairs={{0,8},{8,0},{1,9},{9,1},{2,10},{10,2},{3,11},{11,3},{4,12},{12,4},... | collective-permute-start | bytes 6291464 | tf_op jit(solution)/shard_map/ppermute | solution.py:20
  93.4 3.8 %collective-permute-done.1 = bf16[128,8192]{1,0:T(8,128)(2,1)S(1)} collective-permute-done((bf16[128,8192]{1,0:T(8,128)(2,1)S(1)}, bf16[128,8192]{1,0:T(8,128)(2,1)S(1)}, u32[]{:S(2)}, u32[]{:S(2)}) %collective-permute-start.1) | collective-permute-done | bytes 2097184 | tf_op jit(solution)/shard_map/ppermute | solution.py:20
  97.2 6.5 %fusion.4 = bf16[16,8,8192]{2,1,0:T(8,128)(2,1)} fusion(bf16[128,8192]{1,0:T(8,128)(2,1)S(1)} %collective-permute-done.1, bf16[501,8192]{1,0:T(8,128)(2,1)} %param.9, bf16[256,501]{0,1:T(8,128)(2,1)S(1)} %fusion.7), kind=kOutput, calls=%fused_computation.7 | convolution fusion | flops 1053818880 | bytes 12531712 | tf_op jit(solution)/shard_map/dot_general | solution.py:89
  103.6 3.8 %all-to-all-start.4 = ((bf16[16,8,8192]{2,1,0:T(8,128)(2,1)}), bf16[16,8,8192]{2,1,0:T(8,128)(2,1)S(1)}, u32[]{:S(2)}, u32[]{:S(2)}) async-start(bf16[16,8,8192]{2,1,0:T(8,128)(2,1)} %fusion.4), calls=%async_computation.4 | async-start | bytes 4194304 | tf_op jit(solution)/shard_map/all_to_all | solution.py:91
  107.5 0.0 copy-done
  107.5 33.0 %all-to-all-done.4 = bf16[16,8,8192]{2,1,0:T(8,128)(2,1)S(1)} async-done(((bf16[16,8,8192]{2,1,0:T(8,128)(2,1)}), bf16[16,8,8192]{2,1,0:T(8,128)(2,1)S(1)}, u32[]{:S(2)}, u32[]{:S(2)}) %all-to-all-start.4) | async-done | bytes 2097184 | tf_op jit(solution)/shard_map/all_to_all | solution.py:91
  140.6 0.3 convert_reduce_fusion
  140.9 0.2 multiply_bitcast_fusion
  141.1 0.1 broadcast_in_dim.82
  141.1 0.7 pad_maximum_fusion
  141.9 3.4 %all-to-all-start.5 = ((f32[8,8,1152]{2,1,0:T(8,128)}), f32[8,8,1152]{2,1,0:T(8,128)S(1)}, u32[]{:S(2)}, u32[]{:S(2)}) async-start(f32[8,8,1152]{2,1,0:T(8,128)} %pad_maximum_fusion), calls=%async_computation.5 | async-start | bytes 589824 | tf_op jit(solution)/shard_map/all_to_all | solution.py:103
  145.3 0.1 copy.56
  145.4 0.1 slice_reduce_fusion.1
  145.4 0.1 reshape_squeeze.3
  145.5 0.1 sub.100
  145.6 0.6 fusion.23
  147.1 8.8 %all-to-all-done.5 = f32[8,8,1152]{2,1,0:T(8,128)S(1)} async-done(((f32[8,8,1152]{2,1,0:T(8,128)}), f32[8,8,1152]{2,1,0:T(8,128)S(1)}, u32[]{:S(2)}, u32[]{:S(2)}) %all-to-all-start.5) | async-done | bytes 294944 | tf_op jit(solution)/shard_map/all_to_all | solution.py:103
  155.9 2.6 %fusion.35 = f32[8]{0:T(128)S(1)} fusion(f32[8,1]{1,0:T(8,128)S(1)} %copy.56, f32[8,1152]{1,0:T(8,128)S(1)} %reduce_sum.112, f32[]{:T(128)S(6)} %mul.207, s32[]{:T(128)} %bitcast.11, s32[]{:T(128)} %bitcast.10, s32[]{:T(128)} %bitcast.9, s32[]{:T(128)} %bitcast.8), kind=kLoop, calls=%fused_computation.64 | loop fusion | flops 368 | bytes 116 | tf_op jit(solution)/shard_map/mul | solution.py:108
  158.6 0.7 fusion.18
  (28 shorter events, 0.4 us)
Async XLA Ops:
  0.6 54.7 %copy-start.4 = (s32[256]{0:T(256)S(1)}, s32[256]{0:T(256)}, u32[]{:S(2)}) copy-start(s32[256]{0:T(256)} %param.10) | copy-start | bytes 3076
  0.6 55.0 %copy-start.2 = (s32[2]{0:T(128)S(1)}, s32[2]{0:T(128)}, u32[]{:S(2)}) copy-start(s32[2]{0:T(128)} %param.13) | copy-start | bytes 28
  0.7 55.6 %copy-start.3 = (s32[2]{0:T(128)S(1)}, s32[2]{0:T(128)}, u32[]{:S(2)}) copy-start(s32[2]{0:T(128)} %param.12) | copy-start | bytes 28
  0.7 58.6 %copy-start.5 = (f32[8]{0:T(128)S(1)}, f32[8]{0:T(128)}, u32[]{:S(2)}) copy-start(f32[8]{0:T(128)} %param.11) | copy-start | bytes 100
  51.9 7.5 %collective-permute-start = (bf16[128,8192]{1,0:T(8,128)(2,1)S(1)}, bf16[128,8192]{1,0:T(8,128)(2,1)}, u32[]{:S(2)}, u32[]{:S(2)}) collective-permute-start(bf16[128,8192]{1,0:T(8,128)(2,1)S(1)} %bitcast.70), channel_id=1, source_target_pairs={{0,8},{8,0},{1,9},{9,1},{2,10},{10,2},{3,11},{11,3},{4,12},{12,4},... | collective-permute-start | bytes 6291464 | tf_op jit(solution)/shard_map/ppermute | solution.py:20
  91.6 5.6 %collective-permute-start.1 = (bf16[128,8192]{1,0:T(8,128)(2,1)S(1)}, bf16[128,8192]{1,0:T(8,128)(2,1)S(1)}, u32[]{:S(2)}, u32[]{:S(2)}) collective-permute-start(bf16[128,8192]{1,0:T(8,128)(2,1)S(1)} %convolution_convert_fusion), channel_id=1, source_target_pairs={{0,8},{8,0},{1,9},{9,1},{2,10},{10,2},{3,11},{11,3},{4,12},{12,4},... | collective-permute-start | bytes 6291464 | tf_op jit(solution)/shard_map/ppermute | solution.py:20
  103.6 3.9 %copy-start = (f32[8192]{0:T(1024)S(1)}, f32[8192]{0:T(1024)}, u32[]{:S(2)}) copy-start(f32[8192]{0:T(1024)} %param.8) | copy-start | bytes 98308
  103.6 54.9 %copy-start.1 = (bf16[8,1024]{1,0:T(8,128)(2,1)S(1)}, bf16[8,1024]{1,0:T(8,128)(2,1)}, u32[]{:S(2)}) copy-start(bf16[8,1024]{1,0:T(8,128)(2,1)} %param.7) | copy-start | bytes 49156
  103.6 36.9 %all-to-all-start.4 = ((bf16[16,8,8192]{2,1,0:T(8,128)(2,1)}), bf16[16,8,8192]{2,1,0:T(8,128)(2,1)S(1)}, u32[]{:S(2)}, u32[]{:S(2)}) async-start(bf16[16,8,8192]{2,1,0:T(8,128)(2,1)} %fusion.4), calls=%async_computation.4 | async-start | bytes 4194304 | tf_op jit(solution)/shard_map/all_to_all | solution.py:91
  141.9 14.1 %all-to-all-start.5 = ((f32[8,8,1152]{2,1,0:T(8,128)}), f32[8,8,1152]{2,1,0:T(8,128)S(1)}, u32[]{:S(2)}, u32[]{:S(2)}) async-start(f32[8,8,1152]{2,1,0:T(8,128)} %pad_maximum_fusion), calls=%async_computation.5 | async-start | bytes 589824 | tf_op jit(solution)/shard_map/all_to_all | solution.py:103

commit v2 on v0

v2 whole, which is shorter than its diff:
```python
import functools

import jax
import jax.numpy as jnp
from jax import lax
from jax.experimental import pallas as pl
from jax.experimental.pallas import tpu as pltpu
from jax.sharding import Mesh, PartitionSpec as P

EPSILON = 1e-05
DPO_BETA = 0.05
LOSS_SCALE = 4096.0
PLANE = ("y", "x")
CTX = ("y", "x", "c")
CHUNK = 2048
LANES = 128
STAT_ROWS = 8
VMEM_LIMIT = 16 * 1024 * 1024
CONTRACT_LAST = (((1,), (1,)), ((), ()))
CONTRACT_MIDDLE = (((1,), (0,)), ((), ()))
F32, BF16 = jnp.float32, jnp.bfloat16


def other_core(value):
    return lax.ppermute(value, "c", [(0, 1), (1, 0)])


def exchange(value, axes):
    return lax.all_to_all(value, axes, 0, 0, tiled=True)


IN_VMEM = pl.BlockSpec(memory_space=pltpu.VMEM)
IN_SMEM = pl.BlockSpec(memory_space=pltpu.SMEM)
IN_HBM = pl.BlockSpec(memory_space=pltpu.HBM)


def run(kernel, outputs, scratch, *operands, specs=None, flops=0, moved=0):
    return pl.pallas_call(
        kernel,
        in_specs=specs or [IN_VMEM] * len(operands),
        out_specs=[IN_VMEM] * len(outputs),
        out_shape=[pltpu.VMEM(shape, dtype) for shape, dtype in outputs],
        scratch_shapes=scratch,
        compiler_params=pltpu.CompilerParams(vmem_limit_bytes=VMEM_LIMIT),
        cost_estimate=pl.CostEstimate(flops=flops, bytes_accessed=moved, transcendentals=0),
    )(*operands)


def plane_index():
    return lax.axis_index("y") * lax.axis_size("x") + lax.axis_index("x")


def prepare_kernel(
    hidden_hbm, gain_hbm, targets_hbm, logprobs_hbm, order_hbm, lengths_hbm,
    sent_ref, hidden_out_ref, gain_out_ref, targets_out_ref, live_ref, extra_ref,
    hidden_ref, targets_ref, logprobs_ref, order_ref, lengths_ref, sems,
):
    copies = [
        pltpu.make_async_copy(source, target, sems.at[i])
        for i, (source, target) in enumerate(
            (
                (hidden_hbm, hidden_ref),
                (gain_hbm, gain_out_ref),
                (targets_hbm, targets_ref),
                (logprobs_hbm, logprobs_ref),
                (order_hbm, order_ref),
                (lengths_hbm, lengths_ref),
            )
        )
    ]
    for copy in copies:
        copy.start()
    for copy in copies:
        copy.wait()
    rows = hidden_ref.shape[0]
    core_rows = extra_ref.shape[1]
    hidden = hidden_ref[...].astype(F32)
    hidden_out_ref[...] = hidden
    twice = jnp.concatenate([hidden, hidden], axis=0).astype(sent_ref.dtype)
    for i in range(sent_ref.shape[0] // (2 * rows)):
        sent_ref[i * 2 * rows : (i + 1) * 2 * rows, :] = twice

    def live_sign(row):
        block_len = rows // 4
        rejected = row // (2 * block_len) == 1
        second = row // block_len % 2 == 1
        start = jnp.where(second, order_ref[1], order_ref[0])
        limit = jnp.where(rejected, lengths_ref[1], lengths_ref[0])
        live = start * block_len + row % block_len < limit
        return jnp.where(live, jnp.where(rejected, -1.0, 1.0), 0.0)

    live_ref[...] = live_sign(lax.broadcasted_iota(jnp.int32, live_ref.shape, 0))
    lane = lax.broadcasted_iota(jnp.int32, (1, core_rows), 1)
    mine = lane // rows == plane_index()
    logprobs = jnp.zeros((1, core_rows), F32)
    for t in range(rows):
        logprobs = jnp.where(lane % rows == t, logprobs_ref[t], logprobs)
    extra_ref[...] = jnp.zeros_like(extra_ref)
    extra_ref[3:4, :] = jnp.where(mine, logprobs, 0.0)
    extra_ref[4:5, :] = jnp.where(mine, live_sign(lane % rows), 0.0)
    count = targets_ref.shape[1]
    digit = jnp.minimum(lax.broadcasted_iota(jnp.int32, (STAT_ROWS, count), 0), 3)
    digits = lax.shift_right_logical(
        jnp.broadcast_to(targets_ref[...], (STAT_ROWS, count)), 8 * digit
    ) & 255
    source = lax.broadcasted_iota(jnp.int32, (count, core_rows), 0)
    place = lax.broadcasted_iota(jnp.int32, (count, core_rows), 1)
    wanted = (place // rows * 2 + lax.axis_index("c")) * rows + place % rows
    picked = jnp.dot(
        digits.astype(F32).astype(BF16),
        (source == wanted).astype(F32).astype(BF16),
        preferred_element_type=F32,
    )
    targets = picked[0:1] + 256.0 * picked[1:2] + 65536.0 * picked[2:3]
    targets_out_ref[...] = targets.astype(jnp.int32)


def normed_kernel(features_ref, gain_ref, out_ref, inv_ref):
    parts, rows, width = features_ref.shape
    squares = sum(
        jnp.sum(features_ref[k] * features_ref[k], axis=1, keepdims=True) for k in range(parts)
    )
    inv_rms = lax.rsqrt(squares / (parts * width) + EPSILON)
    inv_ref[...] = jnp.broadcast_to(inv_rms, inv_ref.shape)
    for k in range(parts):
        columns = slice(k * width, (k + 1) * width)
        normed = features_ref[k] * inv_rms * gain_ref[:, columns]
        twice = jnp.concatenate([normed, normed], axis=0).astype(out_ref.dtype)
        for i in range(out_ref.shape[0] // (2 * rows)):
            out_ref[i * 2 * rows : (i + 1) * 2 * rows, columns] = twice


def places_in(targets_ref, n_z, voc_dev, block):
    core = lax.axis_index("c")
    owner = core if block == 0 else 1 - core
    start = ((2 * plane_index() + owner) * n_z + lax.axis_index("z")) * voc_dev
    return targets_ref[...] - start


def is_target(places, shape):
    return lax.broadcasted_iota(jnp.int32, shape, 0) == places


def logits_kernel(
    n_z, rows_ref, own_hbm, sib_ref, targets_ref, extra_ref,
    own_logits_ref, sib_logits_ref, out_ref, own_ref, sem,
):
    copy = pltpu.make_async_copy(own_hbm, own_ref, sem)
    copy.start()
    sib_logits_ref[...] = lax.dot_general(
        sib_ref[...], rows_ref[...], CONTRACT_LAST, preferred_element_type=F32
    )
    copy.wait()
    own_logits_ref[...] = lax.dot_general(
        own_ref[...], rows_ref[...], CONTRACT_LAST, preferred_element_type=F32
    )
    parts = [own_logits_ref[...], sib_logits_ref[...]]
    top = jnp.maximum(*[jnp.max(part, axis=0, keepdims=True) for part in parts])
    total = sum(jnp.sum(jnp.exp(part - top), axis=0, keepdims=True) for part in parts)
    picked = jnp.zeros_like(top)
    for block, part in enumerate(parts):
        hot = is_target(places_in(targets_ref, n_z, part.shape[0], block), part.shape)
        picked += jnp.sum(jnp.where(hot, part, 0.0), axis=0, keepdims=True)
    for k in range(out_ref.shape[0]):
        out_ref[k, 0:1, :] = top
        out_ref[k, 1:2, :] = total
        out_ref[k, 2:3, :] = picked
        out_ref[k, 3:STAT_ROWS, :] = extra_ref[3:STAT_ROWS, :]


def merged(got_ref):
    senders = got_ref.shape[0]
    top = got_ref[0, 0:1, :]
    for k in range(1, senders):
        top = jnp.maximum(top, got_ref[k, 0:1, :])
    total, picked = jnp.zeros_like(top), jnp.zeros_like(top)
    for k in range(senders):
        total += got_ref[k, 1:2, :] * jnp.exp(got_ref[k, 0:1, :] - top)
        picked += got_ref[k, 2:3, :]
    return top, total, picked


def merge_kernel(got_ref, out_ref):
    top, total, picked = merged(got_ref)
    rest = got_ref[0, 3:STAT_ROWS, :]
    for k in range(1, got_ref.shape[0]):
        rest += got_ref[k, 3:STAT_ROWS, :]
    for k in range(out_ref.shape[0]):
        out_ref[k, 0:1, :] = top
        out_ref[k, 1:2, :] = total
        out_ref[k, 2:3, :] = picked
        out_ref[k, 3:STAT_ROWS, :] = rest


def term_kernel(
    n_z, own_logits_ref, sib_logits_ref, got_ref, targets_ref, own_ref, sib_ref,
    out_ref, part_ref, own_coef_ref, sib_coef_ref,
):
    top, total, picked = merged(got_ref)
    log_total = top + jnp.log(total)
    ratio = (picked - log_total - got_ref[0, 3:4, :]) * got_ref[0, 4:5, :]
    part_ref[...] = jnp.broadcast_to(jnp.sum(ratio, axis=1, keepdims=True), part_ref.shape)
    for block, (logits_ref, coef_ref) in enumerate(
        ((own_logits_ref, own_coef_ref), (sib_logits_ref, sib_coef_ref))
    ):
        logits = logits_ref[...]
        hot = is_target(places_in(targets_ref, n_z, logits.shape[0], block), logits.shape)
        shifted = hot.astype(F32) - jnp.exp(logits - log_total)
        coef_ref[...] = shifted.T.astype(coef_ref.dtype)

    def body(i, carry):
        columns = pl.ds(pl.multiple_of(i * CHUNK, CHUNK), CHUNK)
        out_ref[:, columns] = sum(
            lax.dot_general(
                coef_ref[...], weight_ref[:, columns], CONTRACT_MIDDLE, preferred_element_type=F32
            )
            for coef_ref, weight_ref in ((own_coef_ref, own_ref), (sib_coef_ref, sib_ref))
        ).astype(out_ref.dtype)
        return carry

    lax.fori_loop(0, out_ref.shape[1] // CHUNK, body, 0)


def reduce_kernel(pieces_ref, features_ref, gain_ref, out_ref):
    parts, rows, width = features_ref.shape
    dots = jnp.zeros((rows, 1), F32)
    for k in range(parts):
        columns = slice(k * width, (k + 1) * width)
        pairs = pieces_ref[0 : 2 * rows, columns].astype(F32)
        for i in range(1, pieces_ref.shape[0] // (2 * rows)):
            pairs += pieces_ref[i * 2 * rows : (i + 1) * 2 * rows, columns].astype(F32)
        scaled = (pairs[:rows] + pairs[rows:]) * gain_ref[:, columns]
        out_ref[k, :, :width] = scaled
        dots += jnp.sum(scaled * features_ref[k], axis=1, keepdims=True)
    lane = lax.broadcasted_iota(jnp.int32, (rows, LANES), 1)
    rest = jnp.broadcast_to(dots, (rows, LANES))
    terms = jnp.zeros((rows, LANES), F32)
    for i in range(3):
        term = rest.astype(BF16).astype(F32)
        terms = jnp.where(lane == i, term, terms)
        rest -= term
    for k in range(parts):
        out_ref[k, :, width:] = terms


def final_kernel(
    full_width, last_ref, hidden_ref, inv_ref, live_ref, own_part_ref, sib_part_ref, loss_ref, out_ref
):
    rows, width = out_ref.shape
    scaled = last_ref[0].astype(F32)
    for k in range(1, last_ref.shape[0]):
        scaled += last_ref[k].astype(F32)
    value = -DPO_BETA * (own_part_ref[...] + sib_part_ref[...])
    loss = jnp.maximum(value, 0.0) + jnp.log1p(jnp.exp(-jnp.abs(value)))
    loss_ref[...] = loss[:1, :1]
    slope = -DPO_BETA / (1.0 + jnp.exp(-value))
    row_grad = (slope * live_ref[...])[:, :1]
    inv_rms = inv_ref[:, :1]
    row_dot = row_grad * jnp.sum(scaled[:, width:], axis=1, keepdims=True) / full_width
    input_grad = inv_rms * (row_grad * scaled[:, :width]) - hidden_ref[...] * (
        inv_rms * inv_rms * inv_rms * row_dot
    )
    out_ref[...] = (LOSS_SCALE * input_grad).astype(out_ref.dtype)


def on_device(hidden, norm_gain, head_weight, targets, ref_logprobs, block_order, lengths):
    tok_dev, part_width = hidden.shape
    voc_dev, full_width = head_weight.shape
    n_plane = lax.axis_size(PLANE)
    n_z = lax.axis_size("z")
    half = tok_dev * n_plane
    rows_in_all = targets.shape[0]
    flops = 4 * half * voc_dev * full_width
    moved = 4 * (voc_dev + half) * full_width

    sib_weight = other_core(head_weight)
    sent, hidden_f32, gain, targets, live_rows, extra = run(
        prepare_kernel,
        [
            ((n_z * tok_dev, part_width), BF16),
            ((tok_dev, part_width), F32),
            ((1, full_width), F32),
            ((1, half), jnp.int32),
            ((tok_dev, LANES), F32),
            ((STAT_ROWS, half), F32),
        ],
        [
            pltpu.VMEM((tok_dev, part_width), BF16),
            pltpu.VMEM((1, rows_in_all), jnp.int32),
            pltpu.SMEM((tok_dev,), F32),
            pltpu.SMEM((2,), jnp.int32),
            pltpu.SMEM((2,), jnp.int32),
            pltpu.SemaphoreType.DMA((6,)),
        ],
        *[
            pltpu.with_memory_space_constraint(value, pltpu.HBM)
            for value in (
                hidden, norm_gain[None, :], targets[None, :], ref_logprobs, block_order, lengths
            )
        ],
        specs=[IN_HBM] * 6,
        moved=1 << 20,
    )
    sent = sent.reshape(n_z, tok_dev, part_width)

    features = exchange(sent, "z").astype(F32)
    normed, inv_rms = run(
        normed_kernel,
        [((half, full_width), BF16), ((tok_dev, LANES), F32)],
        [],
        features,
        gain,
        moved=2 * half * full_width,
    )
    normed, sib_weight = lax.optimization_barrier((normed, sib_weight))
    sib_weight = pltpu.with_memory_space_constraint(sib_weight, pltpu.VMEM)
    rows = exchange(normed.reshape(n_plane, tok_dev, full_width), PLANE)
    own_logits, sib_logits, stats, own_weight = run(
        functools.partial(logits_kernel, n_z),
        [
            ((voc_dev, half), F32),
            ((voc_dev, half), F32),
            ((n_plane, STAT_ROWS, half), F32),
            ((voc_dev, full_width), BF16),
        ],
        [pltpu.SemaphoreType.DMA],
        rows.reshape(half, full_width),
        pltpu.with_memory_space_constraint(head_weight, pltpu.HBM),
        sib_weight,
        targets,
        extra,
        specs=[IN_VMEM, IN_HBM, IN_VMEM, IN_VMEM, IN_VMEM],
        flops=flops,
        moved=moved,
    )
    (stats,) = run(
        merge_kernel, [((n_z, STAT_ROWS, half), F32)], [], exchange(stats, PLANE), moved=1 << 17
    )
    chip_term, own_part = run(
        functools.partial(term_kernel, n_z),
        [((half, full_width), BF16), ((tok_dev, LANES), F32)],
        [pltpu.VMEM((half, voc_dev), BF16)] * 2,
        own_logits,
        sib_logits,
        exchange(stats, "z"),
        targets,
        own_weight,
        sib_weight,
        flops=flops,
        moved=moved,
    )
    chip_term, sib_part = lax.optimization_barrier((chip_term, other_core(own_part)))
    pieces = exchange(chip_term.reshape(n_plane, tok_dev, full_width), PLANE)
    (last,) = run(
        reduce_kernel,
        [((n_z, tok_dev, part_width + LANES), F32)],
        [],
        pieces.reshape(half, full_width),
        features,
        gain,
        moved=4 * half * full_width,
    )
    last = exchange(last.astype(BF16), "z")
    loss, hidden_grad = pl.pallas_call(
        functools.partial(final_kernel, full_width),
        in_specs=[IN_VMEM] * 6,
        out_specs=[IN_VMEM] * 2,
        out_shape=[
            jax.ShapeDtypeStruct((1, 1), F32),
            jax.ShapeDtypeStruct((tok_dev, part_width), BF16),
        ],
        compiler_params=pltpu.CompilerParams(vmem_limit_bytes=VMEM_LIMIT),
    )(last, hidden_f32, inv_rms, live_rows, own_part, sib_part)
    return (loss[0, 0], hidden_grad)


def solution(mesh):
    fine = Mesh(mesh.devices.reshape(4, 4, 2, 8), ("y", "x", "c", "z"))
    placed = (P(CTX, "z"), P(), P(CTX + ("z",), None), P(), P(CTX), P(CTX), P())
    return jax.shard_map(
        on_device, mesh=fine, in_specs=placed, out_specs=(P(), P(CTX, "z")), check_vma=False
    )
```

time: 461 us -> 137 us (0.30)
  waiting for transfers between devices: 163 us -> 0.83 us
  blocking collectives: 249 us -> 109 us
  Pallas kernels: 0 us -> 17.7 us
  between operations: 16.4 us -> 0.68 us
  matrix products: 15.3 us -> 0 us
  other arithmetic: 8.88 us -> 0.04 us
  starting transfers between devices: 0.12 us -> 7.45 us
    psum x3 -> x0, blocking collectives: 151 us -> none  [the longest x1 74.3 us: on_device(): row_total, picked = lax.psum((local_total, picked_part), ('ctx', 'tp'))]
    all_to_all x0 -> x6, blocking collectives: none -> 109 us  [exchange(): return lax.all_to_all(value, axes, 0, 0, tiled=True)]
    reduce_scatter x2 -> x0, waiting for transfers between devices: 106 us -> none  [the longest x1 91.4 us: on_device(): lax.psum_scatter(full_term, 'tp', scatter_dimension=1, tiled=True)]
    pmax x1 -> x0, blocking collectives: 75.5 us -> none  [on_device(): row_top = lax.pmax(local_top, ('ctx', 'tp'))]
    all_gather x1 -> x0, waiting for transfers between devices: 56.9 us -> none  [on_device(): lax.all_gather(normed, 'ctx', axis=0, tiled=True)]
    all_gather x1 -> x0, blocking collectives: 23.2 us -> none  [on_device(): features = lax.all_gather(hidden, 'tp', axis=1, tiled=True)]
    pallas_call x0 -> x7, Pallas kernels: none -> 17.7 us  [the longest x6 17 us: run(): pl.pallas_call(kernel, in_specs=specs or [IN_VMEM] * len(operands), out_s...]
    dot_general x2 -> x0, matrix products: 15.4 us -> none  [the longest x1 9.08 us: on_device(): jnp.dot(shifted, head_weight, preferred_element_type=jnp.float32)]
  transfers between devices with their start and end apart: 3 -> 2, of which waited for: 3 -> 1; matrix products, arithmetic and copies ran while one was open for 2% -> 0% of each run, Pallas kernels for 0% -> 1%
where the time goes in v2:
time: 137 us; the launch traced here: 136 us
  blocking collectives  109 us (80%)
  Pallas kernels  17.7 us (13%)
  starting transfers between devices  7.45 us (5%)
    all_to_all x6, blocking collectives, exchange(): return lax.all_to_all(value, axes, 0, 0, tiled=True)  109 us
    pallas_call x6, Pallas kernels, run(): pl.pallas_call(kernel, in_specs=specs or [IN_VMEM] * len(operands), out_s...  17 us
    ppermute x2, starting transfers between devices, other_core(): return lax.ppermute(value, 'c', [(0, 1), (1, 0)])  7.45 us
  transfers between devices with their start and end apart: 2, of which 1 were waited for; matrix products, arithmetic and copies ran while one was open for 0% of the time, Pallas kernels for 1%

profile of v2, /device:TPU:1, one launch (start us, length us, event | category | flops | bytes accessed | tf_op | source)
XLA Modules:
  0.0 136.2 jit_solution(7195578719923762720)
XLA Ops:
  0.6 3.3 %collective-permute-start = (bf16[501,8192]{1,0:T(8,128)(2,1)}, bf16[501,8192]{1,0:T(8,128)(2,1)S(1)}, u32[]{:S(2)}, u32[]{:S(2)}) collective-permute-start(bf16[501,8192]{1,0:T(8,128)(2,1)} %own_hbm.1), channel_id=1, source_target_pairs={{0,8},{8,0},{1,9},{9,1},{2,10},{10,2},{3,11},{11,3},{4,12},{12,4},... | collective-permute-start | bytes 24625160 | tf_op jit(solution)/shard_map/ppermute | solution.py:25
  4.0 1.0 shard_map.86
  5.0 14.8 %all_to_all.30 = bf16[8,8,1024]{2,1,0:T(8,128)(2,1)S(1)} all-to-all(bf16[8,8,1024]{2,1,0:T(8,128)(2,1)S(1)} %bitcast.12), channel_id=1, replica_groups=mesh['y'=4,'x'=4,'c'=2,'z'=8] {'z'}, dimensions={0} | all-to-all | bytes 262144 | tf_op jit(solution)/shard_map/all_to_all | solution.py:29
  19.8 0.2 shard_map.87
  20.0 0.0 collective-permute-done.sib_ref
  20.0 33.4 %all_to_all.31 = bf16[16,8,8192]{2,1,0:T(8,128)(2,1)S(1)} all-to-all(bf16[16,8,8192]{2,1,0:T(8,128)(2,1)S(1)} %bitcast.11), channel_id=1, replica_groups=mesh['y'=4,'x'=4,'c'=2,'z'=8] {'y','x'}, dimensions={0} | all-to-all | bytes 4194304 | tf_op jit(solution)/shard_map/all_to_all | solution.py:29
  53.4 12.2 %shard_map.88 = (f32[501,128]{1,0:T(8,128)S(1)}, f32[501,128]{1,0:T(8,128)S(1)}, f32[16,8,128]{2,1,0:T(8,128)S(1)}, bf16[501,8192]{1,0:T(8,128)(2,1)S(1)}) custom-call(bf16[128,8192]{1,0:T(8,128)(2,1)S(1)} %bitcast.8, bf16[501,8192]{1,0:T(8,128)(2,1)} %own_hbm.1, bf16[501,8192]{1,0:T(8,128)(2,1)S(1)} %collective-permute-done.sib_ref, ...), custom_call_target="tpu_custom_call" | custom-call | flops 2101346304 | bytes 20611072 | tf_op jit(solution)/shard_map/pallas_call | solution.py:38
  65.6 9.1 %all_to_all.32.got_ref = f32[16,8,128]{2,1,0:T(8,128)S(1)} all-to-all(f32[16,8,128]{2,1,0:T(8,128)S(1)} %get-tuple-element.31), channel_id=1, replica_groups=mesh['y'=4,'x'=4,'c'=2,'z'=8] {'y','x'}, dimensions={0} | all-to-all | bytes 131072 | tf_op jit(solution)/shard_map/all_to_all | solution.py:29
  74.7 11.3 %all_to_all.33.got_ref = f32[8,8,128]{2,1,0:T(8,128)S(1)} all-to-all(f32[8,8,128]{2,1,0:T(8,128)S(1)} %shard_map.89), channel_id=1, replica_groups=mesh['y'=4,'x'=4,'c'=2,'z'=8] {'z'}, dimensions={0} | all-to-all | bytes 65536 | tf_op jit(solution)/shard_map/all_to_all | solution.py:29
  86.0 3.1 %shard_map.90 = (bf16[128,8192]{1,0:T(8,128)(2,1)S(1)}, f32[8,128]{1,0:T(8,128)S(1)}) custom-call(f32[501,128]{1,0:T(8,128)S(1)} %get-tuple-element.29.own_logits_ref, f32[501,128]{1,0:T(8,128)S(1)} %get-tuple-element.30.sib_logits_ref, f32[8,8,128]{2,1,0:T(8,128)S(1)} %all_to_all.33.got_ref, s32[1,128]{1,0:T(1,128)S(1)} %get-tuple-element.27.targets_ref, ...), custom_call_target="tpu_custom_call" | custom-call | flops 2101346304 | bytes 20611072 | tf_op jit(solution)/shard_map/pallas_call | solution.py:38
  89.1 4.1 %collective-permute-start.1 = (f32[8,128]{1,0:T(8,128)S(1)}, f32[8,128]{1,0:T(8,128)S(1)}, u32[]{:S(2)}, u32[]{:S(2)}) collective-permute-start(f32[8,128]{1,0:T(8,128)S(1)} %get-tuple-element.34.own_part_ref), channel_id=1, source_target_pairs={{0,8},{8,0},{1,9},{9,1},{2,10},{10,2},{3,11},{11,3},{4,12},{12,4},... | collective-permute-start | bytes 12296 | tf_op jit(solution)/shard_map/ppermute | solution.py:25
  93.2 0.8 collective-permute-done.1.sib_part_ref
  94.0 30.4 %all_to_all.34 = bf16[16,8,8192]{2,1,0:T(8,128)(2,1)S(1)} all-to-all(bf16[16,8,8192]{2,1,0:T(8,128)(2,1)S(1)} %bitcast.10), channel_id=1, replica_groups=mesh['y'=4,'x'=4,'c'=2,'z'=8] {'y','x'}, dimensions={0} | all-to-all | bytes 4194304 | tf_op jit(solution)/shard_map/all_to_all | solution.py:29
  124.5 0.4 shard_map.91
  124.9 10.5 %all_to_all.35.last_ref = bf16[8,8,1152]{2,1,0:T(8,128)(2,1)S(1)} all-to-all(bf16[8,8,1152]{2,1,0:T(8,128)(2,1)S(1)} %convert_element_type.7), channel_id=1, replica_groups=mesh['y'=4,'x'=4,'c'=2,'z'=8] {'z'}, dimensions={0} | all-to-all | bytes 294912 | tf_op jit(solution)/shard_map/all_to_all | solution.py:29
  135.4 0.8 shard_map.92
  (3 shorter events, 0.1 us)
Async XLA Ops:
  0.6 19.4 %collective-permute-start = (bf16[501,8192]{1,0:T(8,128)(2,1)}, bf16[501,8192]{1,0:T(8,128)(2,1)S(1)}, u32[]{:S(2)}, u32[]{:S(2)}) collective-permute-start(bf16[501,8192]{1,0:T(8,128)(2,1)} %own_hbm.1), channel_id=1, source_target_pairs={{0,8},{8,0},{1,9},{9,1},{2,10},{10,2},{3,11},{11,3},{4,12},{12,4},... | collective-permute-start | bytes 24625160 | tf_op jit(solution)/shard_map/ppermute | solution.py:25
  89.1 4.9 %collective-permute-start.1 = (f32[8,128]{1,0:T(8,128)S(1)}, f32[8,128]{1,0:T(8,128)S(1)}, u32[]{:S(2)}, u32[]{:S(2)}) collective-permute-start(f32[8,128]{1,0:T(8,128)S(1)} %get-tuple-element.34.own_part_ref), channel_id=1, source_target_pairs={{0,8},{8,0},{1,9},{9,1},{2,10},{10,2},{3,11},{11,3},{4,12},{12,4},... | collective-permute-start | bytes 12296 | tf_op jit(solution)/shard_map/ppermute | solution.py:25

commit v3 on v2

--- a/solution.py
+++ b/solution.py
@@ -15,6 +15,7 @@
 CHUNK = 2048
 LANES = 128
 STAT_ROWS = 8
+SIDE = 4
 VMEM_LIMIT = 16 * 1024 * 1024
 CONTRACT_LAST = (((1,), (1,)), ((), ()))
 CONTRACT_MIDDLE = (((1,), (0,)), ((), ()))
@@ -48,6 +49,50 @@
 
 def plane_index():
     return lax.axis_index("y") * lax.axis_size("x") + lax.axis_index("x")
+
+
+def place_on(y, x, core):
+    return (jnp.where(core == 0, x, y), jnp.where(core == 0, y, x))
+
+
+def own_place():
+    return place_on(lax.axis_index("y"), lax.axis_index("x"), lax.axis_index("c"))
+
+
+def device(y, x, core):
+    return (y * SIDE + x) * 2 + core
+
+
+def from_ahead(value, step, outer):
+    pairs = []
+    for y in range(SIDE):
+        for x in range(SIDE):
+            for core in range(2):
+                if (core == 0) == outer:
+                    source = device(y, (x + step) % SIDE, core)
+                else:
+                    source = device((y + step) % SIDE, x, core)
+                pairs.append((source, device(y, x, core)))
+    return lax.ppermute(value, CTX, pairs)
+
+
+def gather_from(value, outer):
+    far = from_ahead(value, 2, outer)
+    return jnp.concatenate(
+        [value, from_ahead(value, 1, outer), far, from_ahead(value, 3, outer)], axis=0
+    )
+
+
+def in_order(value, rows):
+    lanes = value.shape[1]
+    group = SIDE * rows
+    outer, inner = own_place()
+    lane = lax.broadcasted_iota(jnp.int32, value.shape, 1)
+    shift = inner * rows
+    ahead = pltpu.roll(value, shift, 1)
+    wrapped = pltpu.roll(value, (shift + lanes - group) % lanes, 1)
+    value = jnp.where(lane % group >= shift, ahead, wrapped)
+    return pltpu.roll(value, outer * group, 1)
 
 
 def prepare_kernel(
@@ -91,7 +136,8 @@
 
     live_ref[...] = live_sign(lax.broadcasted_iota(jnp.int32, live_ref.shape, 0))
     lane = lax.broadcasted_iota(jnp.int32, (1, core_rows), 1)
-    mine = lane // rows == plane_index()
+    outer, inner = own_place()
+    mine = lane // rows == outer * SIDE + inner
     logprobs = jnp.zeros((1, core_rows), F32)
     for t in range(rows):
         logprobs = jnp.where(lane % rows == t, logprobs_ref[t], logprobs)
@@ -105,7 +151,9 @@
     ) & 255
     source = lax.broadcasted_iota(jnp.int32, (count, core_rows), 0)
     place = lax.broadcasted_iota(jnp.int32, (count, core_rows), 1)
-    wanted = (place // rows * 2 + lax.axis_index("c")) * rows + place % rows
+    core = lax.axis_index("c")
+    x, y = place_on(place // rows % SIDE, place // (rows * SIDE), core)
+    wanted = device(y, x, core) * rows + place % rows
     picked = jnp.dot(
         digits.astype(F32).astype(BF16),
         (source == wanted).astype(F32).astype(BF16),
@@ -125,9 +173,7 @@
     for k in range(parts):
         columns = slice(k * width, (k + 1) * width)
         normed = features_ref[k] * inv_rms * gain_ref[:, columns]
-        twice = jnp.concatenate([normed, normed], axis=0).astype(out_ref.dtype)
-        for i in range(out_ref.shape[0] // (2 * rows)):
-            out_ref[i * 2 * rows : (i + 1) * 2 * rows, columns] = twice
+        out_ref[:, columns] = normed.astype(out_ref.dtype)
 
 
 def places_in(targets_ref, n_z, voc_dev, block):
@@ -142,18 +188,13 @@
 
 
 def logits_kernel(
-    n_z, rows_ref, own_hbm, sib_ref, targets_ref, extra_ref,
-    own_logits_ref, sib_logits_ref, out_ref, own_ref, sem,
+    n_z, rows_ref, own_ref, sib_ref, targets_ref, extra_ref, own_logits_ref, sib_logits_ref, out_ref
 ):
-    copy = pltpu.make_async_copy(own_hbm, own_ref, sem)
-    copy.start()
-    sib_logits_ref[...] = lax.dot_general(
-        sib_ref[...], rows_ref[...], CONTRACT_LAST, preferred_element_type=F32
-    )
-    copy.wait()
-    own_logits_ref[...] = lax.dot_general(
-        own_ref[...], rows_ref[...], CONTRACT_LAST, preferred_element_type=F32
-    )
+    for weight_ref, logits_ref in ((own_ref, own_logits_ref), (sib_ref, sib_logits_ref)):
+        logits = lax.dot_general(
+            weight_ref[...], rows_ref[...], CONTRACT_LAST, preferred_element_type=F32
+        )
+        logits_ref[...] = in_order(logits, rows_ref.shape[0] // (SIDE * SIDE))
     parts = [own_logits_ref[...], sib_logits_ref[...]]
     top = jnp.maximum(*[jnp.max(part, axis=0, keepdims=True) for part in parts])
     total = sum(jnp.sum(jnp.exp(part - top), axis=0, keepdims=True) for part in parts)
@@ -232,31 +273,24 @@
         scaled = (pairs[:rows] + pairs[rows:]) * gain_ref[:, columns]
         out_ref[k, :, :width] = scaled
         dots += jnp.sum(scaled * features_ref[k], axis=1, keepdims=True)
-    lane = lax.broadcasted_iota(jnp.int32, (rows, LANES), 1)
-    rest = jnp.broadcast_to(dots, (rows, LANES))
-    terms = jnp.zeros((rows, LANES), F32)
-    for i in range(3):
-        term = rest.astype(BF16).astype(F32)
-        terms = jnp.where(lane == i, term, terms)
-        rest -= term
     for k in range(parts):
-        out_ref[k, :, width:] = terms
+        out_ref[k, :, width:] = jnp.broadcast_to(dots, (rows, LANES))
 
 
 def final_kernel(
     full_width, last_ref, hidden_ref, inv_ref, live_ref, own_part_ref, sib_part_ref, loss_ref, out_ref
 ):
     rows, width = out_ref.shape
-    scaled = last_ref[0].astype(F32)
+    scaled = last_ref[0]
     for k in range(1, last_ref.shape[0]):
-        scaled += last_ref[k].astype(F32)
+        scaled += last_ref[k]
     value = -DPO_BETA * (own_part_ref[...] + sib_part_ref[...])
     loss = jnp.maximum(value, 0.0) + jnp.log1p(jnp.exp(-jnp.abs(value)))
     loss_ref[...] = loss[:1, :1]
     slope = -DPO_BETA / (1.0 + jnp.exp(-value))
     row_grad = (slope * live_ref[...])[:, :1]
     inv_rms = inv_ref[:, :1]
-    row_dot = row_grad * jnp.sum(scaled[:, width:], axis=1, keepdims=True) / full_width
+    row_dot = row_grad * scaled[:, width : width + 1] / full_width
     input_grad = inv_rms * (row_grad * scaled[:, :width]) - hidden_ref[...] * (
         inv_rms * inv_rms * inv_rms * row_dot
     )
@@ -306,30 +340,25 @@
     features = exchange(sent, "z").astype(F32)
     normed, inv_rms = run(
         normed_kernel,
-        [((half, full_width), BF16), ((tok_dev, LANES), F32)],
+        [((tok_dev, full_width), BF16), ((tok_dev, LANES), F32)],
         [],
         features,
         gain,
         moved=2 * half * full_width,
     )
     normed, sib_weight = lax.optimization_barrier((normed, sib_weight))
+    own_weight = pltpu.with_memory_space_constraint(other_core(sib_weight), pltpu.VMEM)
     sib_weight = pltpu.with_memory_space_constraint(sib_weight, pltpu.VMEM)
-    rows = exchange(normed.reshape(n_plane, tok_dev, full_width), PLANE)
-    own_logits, sib_logits, stats, own_weight = run(
+    rows = gather_from(gather_from(normed, False), True)
+    own_logits, sib_logits, stats = run(
         functools.partial(logits_kernel, n_z),
-        [
-            ((voc_dev, half), F32),
-            ((voc_dev, half), F32),
-            ((n_plane, STAT_ROWS, half), F32),
-            ((voc_dev, full_width), BF16),
-        ],
-        [pltpu.SemaphoreType.DMA],
-        rows.reshape(half, full_width),
-        pltpu.with_memory_space_constraint(head_weight, pltpu.HBM),
+        [((voc_dev, half), F32), ((voc_dev, half), F32), ((n_plane, STAT_ROWS, half), F32)],
+        [],
+        rows,
+        own_weight,
         sib_weight,
         targets,
         extra,
-        specs=[IN_VMEM, IN_HBM, IN_VMEM, IN_VMEM, IN_VMEM],
         flops=flops,
         moved=moved,
     )
@@ -350,7 +379,17 @@
         moved=moved,
     )
     chip_term, sib_part = lax.optimization_barrier((chip_term, other_core(own_part)))
-    pieces = exchange(chip_term.reshape(n_plane, tok_dev, full_width), PLANE)
+    pieces = lax.all_to_all(
+        chip_term.reshape(n_plane, tok_dev, full_width),
+        CTX,
+        0,
+        0,
+        axis_index_groups=[
+            [device(y, x, 0) for x in range(SIDE) for y in range(SIDE)],
+            [device(y, x, 1) for y in range(SIDE) for x in range(SIDE)],
+        ],
+        tiled=True,
+    )
     (last,) = run(
         reduce_kernel,
         [((n_z, tok_dev, part_width + LANES), F32)],
@@ -360,7 +399,7 @@
         gain,
         moved=4 * half * full_width,
     )
-    last = exchange(last.astype(BF16), "z")
+    last = exchange(last, "z")
     loss, hidden_grad = pl.pallas_call(
         functools.partial(final_kernel, full_width),
         in_specs=[IN_VMEM] * 6,
@@ -375,7 +414,7 @@
 
 
 def solution(mesh):
-    fine = Mesh(mesh.devices.reshape(4, 4, 2, 8), ("y", "x", "c", "z"))
+    fine = Mesh(mesh.devices.reshape(SIDE, SIDE, 2, 8), ("y", "x", "c", "z"))
     placed = (P(CTX, "z"), P(), P(CTX + ("z",), None), P(), P(CTX), P(CTX), P())
     return jax.shard_map(
         on_device, mesh=fine, in_specs=placed, out_specs=(P(), P(CTX, "z")), check_vma=False

time: 137 us -> 127 us (0.927)
  blocking collectives: 109 us -> 77.7 us
  waiting for transfers between devices: 0.83 us -> 17.2 us
  starting transfers between devices: 7.45 us -> 19.3 us
  Pallas kernels: 17.7 us -> 10.3 us
    all_to_all x6 -> x4, blocking collectives: 109 us -> 46.9 us  [exchange(): return lax.all_to_all(value, axes, 0, 0, tiled=True)]
    all_to_all x0 -> x1, blocking collectives: none -> 30.7 us  [on_device(): lax.all_to_all(chip_term.reshape(n_plane, tok_dev, full_width), CTX, 0, 0...]
    ppermute x0 -> x6, waiting for transfers between devices: none -> 16.4 us  [from_ahead(): return lax.ppermute(value, CTX, pairs)]
    ppermute x0 -> x6, starting transfers between devices: none -> 9.27 us  [from_ahead(): return lax.ppermute(value, CTX, pairs)]
    pallas_call x6, Pallas kernels: 17 us -> 9.62 us  [run(): pl.pallas_call(kernel, in_specs=specs or [IN_VMEM] * len(operands), out_s...]
    ppermute x2 -> x3, starting transfers between devices: 7.45 us -> 10.1 us  [other_core(): return lax.ppermute(value, 'c', [(0, 1), (1, 0)])]
  transfers between devices with their start and end apart: 2 -> 9, of which waited for: 1 -> 5; matrix products, arithmetic and copies ran while one was open for 0% -> 0% of each run, Pallas kernels for 1% -> 1%
where the time goes in v3:
time: 127 us; the launch traced here: 125 us
  blocking collectives  77.7 us (61%)
  starting transfers between devices  19.3 us (15%)
  waiting for transfers between devices  17.2 us (14%)
  Pallas kernels  10.3 us (8%)
    all_to_all x4, blocking collectives, exchange(): return lax.all_to_all(value, axes, 0, 0, tiled=True)  46.9 us
    all_to_all x1, blocking collectives, on_device(): lax.all_to_all(chip_term.reshape(n_plane, tok_dev, full_width), CTX, 0, 0...  30.7 us
    ppermute x6, waiting for transfers between devices, from_ahead(): return lax.ppermute(value, CTX, pairs)  16.4 us
    ppermute x3, starting transfers between devices, other_core(): return lax.ppermute(value, 'c', [(0, 1), (1, 0)])  10.1 us
    pallas_call x6, Pallas kernels, run(): pl.pallas_call(kernel, in_specs=specs or [IN_VMEM] * len(operands), out_s...  9.62 us
    ppermute x6, starting transfers between devices, from_ahead(): return lax.ppermute(value, CTX, pairs)  9.27 us
  transfers between devices with their start and end apart: 9, of which 5 were waited for; matrix products, arithmetic and copies ran while one was open for 0% of the time, Pallas kernels for 1%

profile of v3, /device:TPU:1, one launch (start us, length us, event | category | flops | bytes accessed | tf_op | source)
XLA Modules:
  0.0 125.5 jit_solution(15565996465653830196)
XLA Ops:
  0.6 3.3 %collective-permute-start = (bf16[501,8192]{1,0:T(8,128)(2,1)}, bf16[501,8192]{1,0:T(8,128)(2,1)S(1)}, u32[]{:S(2)}, u32[]{:S(2)}) collective-permute-start(bf16[501,8192]{1,0:T(8,128)(2,1)} %param.9), channel_id=1, source_target_pairs={{0,8},{8,0},{1,9},{9,1},{2,10},{10,2},{3,11},{11,3},{4,12},{12,4},... | collective-permute-start | bytes 24625160 | tf_op jit(solution)/shard_map/ppermute | solution.py:26
  4.0 1.0 shard_map.86
  5.0 14.8 %all_to_all.25 = bf16[8,8,1024]{2,1,0:T(8,128)(2,1)S(1)} all-to-all(bf16[8,8,1024]{2,1,0:T(8,128)(2,1)S(1)} %bitcast.8), channel_id=1, replica_groups=mesh['y'=4,'x'=4,'c'=2,'z'=8] {'z'}, dimensions={0} | all-to-all | bytes 262144 | tf_op jit(solution)/shard_map/all_to_all | solution.py:30
  19.8 0.1 shard_map.87
  19.9 0.0 collective-permute-done.sib_ref
  19.9 1.6 %collective-permute-start.7 = (bf16[501,8192]{1,0:T(8,128)(2,1)S(1)}, bf16[501,8192]{1,0:T(8,128)(2,1)S(1)}, u32[]{:S(2)}, u32[]{:S(2)}) collective-permute-start(bf16[501,8192]{1,0:T(8,128)(2,1)S(1)} %collective-permute-done.sib_ref), channel_id=1, source_target_pairs={{0,8},{8,0},{1,9},{9,1},{2,10},{10,2},{3,11},{11,3},{4,12},{12,4},... | collective-permute-start | bytes 24625160 | tf_op jit(solution)/shard_map/ppermute | solution.py:26
  21.5 1.2 collective-permute-start.3
  22.7 2.5 %collective-permute-start.2 = (bf16[8,8192]{1,0:T(8,128)(2,1)S(1)}, bf16[8,8192]{1,0:T(8,128)(2,1)S(1)}, u32[]{:S(2)}, u32[]{:S(2)}) collective-permute-start(bf16[8,8192]{1,0:T(8,128)(2,1)S(1)} %get-tuple-element.24), channel_id=1, source_target_pairs={{128,0},{40,8},{144,16},{56,24},{160,32},{8,40},{176,48},{24,56},{... | collective-permute-start | bytes 393224 | tf_op jit(solution)/shard_map/ppermute | solution.py:76
  25.2 1.2 collective-permute-start.1
  26.4 2.9 %collective-permute-done.1 = bf16[8,8192]{1,0:T(8,128)(2,1)S(1)} collective-permute-done((bf16[8,8192]{1,0:T(8,128)(2,1)S(1)}, bf16[8,8192]{1,0:T(8,128)(2,1)S(1)}, u32[]{:S(2)}, u32[]{:S(2)}) %collective-permute-start.1) | collective-permute-done | bytes 131104 | tf_op jit(solution)/shard_map/ppermute | solution.py:76
  29.3 0.0 collective-permute-done.2
  29.4 0.0 collective-permute-done.3
  29.4 2.8 %collective-permute-start.4 = (bf16[32,8192]{1,0:T(8,128)(2,1)S(1)}, bf16[32,8192]{1,0:T(8,128)(2,1)S(1)}, u32[]{:S(2)}, u32[]{:S(2)}) collective-permute-start(bf16[32,8192]{1,0:T(8,128)(2,1)S(1)} %get-tuple-element.40), channel_id=1, source_target_pairs={{16,0},{72,8},{32,16},{88,24},{48,32},{104,40},{0,48},{120,56},{80... | collective-permute-start | bytes 1572872 | tf_op jit(solution)/shard_map/ppermute | solution.py:76
  32.2 0.0 collective-permute-start.6
  32.2 1.6 %collective-permute-start.5 = (bf16[32,8192]{1,0:T(8,128)(2,1)S(1)}, bf16[32,8192]{1,0:T(8,128)(2,1)S(1)}, u32[]{:S(2)}, u32[]{:S(2)}) collective-permute-start(bf16[32,8192]{1,0:T(8,128)(2,1)S(1)} %get-tuple-element.40), channel_id=1, source_target_pairs={{32,0},{136,8},{48,16},{152,24},{0,32},{168,40},{16,48},{184,56},{... | collective-permute-start | bytes 1572872 | tf_op jit(solution)/shard_map/ppermute | solution.py:76
  33.9 10.1 %collective-permute-done.4 = bf16[32,8192]{1,0:T(8,128)(2,1)S(1)} collective-permute-done((bf16[32,8192]{1,0:T(8,128)(2,1)S(1)}, bf16[32,8192]{1,0:T(8,128)(2,1)S(1)}, u32[]{:S(2)}, u32[]{:S(2)}) %collective-permute-start.4) | collective-permute-done | bytes 524320 | tf_op jit(solution)/shard_map/ppermute | solution.py:76
  44.0 2.4 %collective-permute-done.5 = bf16[32,8192]{1,0:T(8,128)(2,1)S(1)} collective-permute-done((bf16[32,8192]{1,0:T(8,128)(2,1)S(1)}, bf16[32,8192]{1,0:T(8,128)(2,1)S(1)}, u32[]{:S(2)}, u32[]{:S(2)}) %collective-permute-start.5) | collective-permute-done | bytes 524320 | tf_op jit(solution)/shard_map/ppermute | solution.py:76
  46.4 0.9 collective-permute-done.6
  47.4 0.0 collective-permute-done.7.own_ref
  47.4 4.9 %shard_map.88 = (f32[501,128]{1,0:T(8,128)S(1)}, f32[501,128]{1,0:T(8,128)S(1)}, f32[16,8,128]{2,1,0:T(8,128)S(1)}) custom-call(bf16[128,8192]{1,0:T(8,128)(2,1)S(1)} %constant_dynamic-update-slice_fusion.4.rows_ref, bf16[501,8192]{1,0:T(8,128)(2,1)S(1)} %collective-permute-done.7.own_ref, bf16[501,8192]{1,0:T(8,128)(2,1)S(1)} %collective-permute-done.sib_ref, ...), custom_call_target="tpu_custom_call" | custom-call | flops 2101346304 | bytes 20611072 | tf_op jit(solution)/shard_map/pallas_call | solution.py:39
  52.4 10.1 %all_to_all.26.got_ref = f32[16,8,128]{2,1,0:T(8,128)S(1)} all-to-all(f32[16,8,128]{2,1,0:T(8,128)S(1)} %get-tuple-element.30), channel_id=1, replica_groups=mesh['y'=4,'x'=4,'c'=2,'z'=8] {'y','x'}, dimensions={0} | all-to-all | bytes 131072 | tf_op jit(solution)/shard_map/all_to_all | solution.py:30
  62.5 9.2 %all_to_all.27.got_ref = f32[8,8,128]{2,1,0:T(8,128)S(1)} all-to-all(f32[8,8,128]{2,1,0:T(8,128)S(1)} %shard_map.89), channel_id=1, replica_groups=mesh['y'=4,'x'=4,'c'=2,'z'=8] {'z'}, dimensions={0} | all-to-all | bytes 65536 | tf_op jit(solution)/shard_map/all_to_all | solution.py:30
  71.8 3.1 %shard_map.90 = (bf16[128,8192]{1,0:T(8,128)(2,1)S(1)}, f32[8,128]{1,0:T(8,128)S(1)}) custom-call(f32[501,128]{1,0:T(8,128)S(1)} %get-tuple-element.28.own_logits_ref, f32[501,128]{1,0:T(8,128)S(1)} %get-tuple-element.29.sib_logits_ref, f32[8,8,128]{2,1,0:T(8,128)S(1)} %all_to_all.27.got_ref, s32[1,128]{1,0:T(1,128)S(1)} %get-tuple-element.26.targets_ref, ...), custom_call_target="tpu_custom_call" | custom-call | flops 2101346304 | bytes 20611072 | tf_op jit(solution)/shard_map/pallas_call | solution.py:39
  74.9 5.1 %collective-permute-start.8 = (f32[8,128]{1,0:T(8,128)S(1)}, f32[8,128]{1,0:T(8,128)S(1)}, u32[]{:S(2)}, u32[]{:S(2)}) collective-permute-start(f32[8,128]{1,0:T(8,128)S(1)} %get-tuple-element.32.own_part_ref), channel_id=1, source_target_pairs={{0,8},{8,0},{1,9},{9,1},{2,10},{10,2},{3,11},{11,3},{4,12},{12,4},... | collective-permute-start | bytes 12296 | tf_op jit(solution)/shard_map/ppermute | solution.py:26
  80.0 0.8 collective-permute-done.8.sib_part_ref
  80.9 30.7 %all_to_all.28 = bf16[16,8,8192]{2,1,0:T(8,128)(2,1)S(1)} all-to-all(bf16[16,8,8192]{2,1,0:T(8,128)(2,1)S(1)} %bitcast.7), channel_id=1, replica_groups={{0,64,128,192,16,80,144,208,32,96,160,224,48,112,176,240},{8,24,40,56,7..., dimensions={0} | all-to-all | bytes 4194304 | tf_op jit(solution)/shard_map/all_to_all | solution.py:382
  111.6 0.4 shard_map.91
  112.0 12.8 %all_to_all.29.last_ref = f32[8,8,1152]{2,1,0:T(8,128)S(1)} all-to-all(f32[8,8,1152]{2,1,0:T(8,128)S(1)} %shard_map.91), channel_id=1, replica_groups=mesh['y'=4,'x'=4,'c'=2,'z'=8] {'z'}, dimensions={0} | all-to-all | bytes 589824 | tf_op jit(solution)/shard_map/all_to_all | solution.py:30
  124.8 0.7 shard_map.92
  (9 shorter events, 0.2 us)
Async XLA Ops:
  0.6 19.3 %collective-permute-start = (bf16[501,8192]{1,0:T(8,128)(2,1)}, bf16[501,8192]{1,0:T(8,128)(2,1)S(1)}, u32[]{:S(2)}, u32[]{:S(2)}) collective-permute-start(bf16[501,8192]{1,0:T(8,128)(2,1)} %param.9), channel_id=1, source_target_pairs={{0,8},{8,0},{1,9},{9,1},{2,10},{10,2},{3,11},{11,3},{4,12},{12,4},... | collective-permute-start | bytes 24625160 | tf_op jit(solution)/shard_map/ppermute | solution.py:26
  19.9 27.5 %collective-permute-start.7 = (bf16[501,8192]{1,0:T(8,128)(2,1)S(1)}, bf16[501,8192]{1,0:T(8,128)(2,1)S(1)}, u32[]{:S(2)}, u32[]{:S(2)}) collective-permute-start(bf16[501,8192]{1,0:T(8,128)(2,1)S(1)} %collective-permute-done.sib_ref), channel_id=1, source_target_pairs={{0,8},{8,0},{1,9},{9,1},{2,10},{10,2},{3,11},{11,3},{4,12},{12,4},... | collective-permute-start | bytes 24625160 | tf_op jit(solution)/shard_map/ppermute | solution.py:26
  21.5 7.8 %collective-permute-start.3 = (bf16[8,8192]{1,0:T(8,128)(2,1)S(1)}, bf16[8,8192]{1,0:T(8,128)(2,1)S(1)}, u32[]{:S(2)}, u32[]{:S(2)}) collective-permute-start(bf16[8,8192]{1,0:T(8,128)(2,1)S(1)} %get-tuple-element.24), channel_id=1, source_target_pairs={{192,0},{56,8},{208,16},{8,24},{224,32},{24,40},{240,48},{40,56},{... | collective-permute-start | bytes 393224 | tf_op jit(solution)/shard_map/ppermute | solution.py:76
  22.7 6.6 %collective-permute-start.2 = (bf16[8,8192]{1,0:T(8,128)(2,1)S(1)}, bf16[8,8192]{1,0:T(8,128)(2,1)S(1)}, u32[]{:S(2)}, u32[]{:S(2)}) collective-permute-start(bf16[8,8192]{1,0:T(8,128)(2,1)S(1)} %get-tuple-element.24), channel_id=1, source_target_pairs={{128,0},{40,8},{144,16},{56,24},{160,32},{8,40},{176,48},{24,56},{... | collective-permute-start | bytes 393224 | tf_op jit(solution)/shard_map/ppermute | solution.py:76
  25.2 4.1 %collective-permute-start.1 = (bf16[8,8192]{1,0:T(8,128)(2,1)S(1)}, bf16[8,8192]{1,0:T(8,128)(2,1)S(1)}, u32[]{:S(2)}, u32[]{:S(2)}) collective-permute-start(bf16[8,8192]{1,0:T(8,128)(2,1)S(1)} %get-tuple-element.24), channel_id=1, source_target_pairs={{64,0},{24,8},{80,16},{40,24},{96,32},{56,40},{112,48},{8,56},{128... | collective-permute-start | bytes 393224 | tf_op jit(solution)/shard_map/ppermute | solution.py:76
  29.4 14.6 %collective-permute-start.4 = (bf16[32,8192]{1,0:T(8,128)(2,1)S(1)}, bf16[32,8192]{1,0:T(8,128)(2,1)S(1)}, u32[]{:S(2)}, u32[]{:S(2)}) collective-permute-start(bf16[32,8192]{1,0:T(8,128)(2,1)S(1)} %get-tuple-element.40), channel_id=1, source_target_pairs={{16,0},{72,8},{32,16},{88,24},{48,32},{104,40},{0,48},{120,56},{80... | collective-permute-start | bytes 1572872 | tf_op jit(solution)/shard_map/ppermute | solution.py:76
  32.2 15.2 %collective-permute-start.6 = (bf16[32,8192]{1,0:T(8,128)(2,1)S(1)}, bf16[32,8192]{1,0:T(8,128)(2,1)S(1)}, u32[]{:S(2)}, u32[]{:S(2)}) collective-permute-start(bf16[32,8192]{1,0:T(8,128)(2,1)S(1)} %get-tuple-element.40), channel_id=1, source_target_pairs={{48,0},{200,8},{0,16},{216,24},{16,32},{232,40},{32,48},{248,56},{... | collective-permute-start | bytes 1572872 | tf_op jit(solution)/shard_map/ppermute | solution.py:76
  32.2 14.2 %collective-permute-start.5 = (bf16[32,8192]{1,0:T(8,128)(2,1)S(1)}, bf16[32,8192]{1,0:T(8,128)(2,1)S(1)}, u32[]{:S(2)}, u32[]{:S(2)}) collective-permute-start(bf16[32,8192]{1,0:T(8,128)(2,1)S(1)} %get-tuple-element.40), channel_id=1, source_target_pairs={{32,0},{136,8},{48,16},{152,24},{0,32},{168,40},{16,48},{184,56},{... | collective-permute-start | bytes 1572872 | tf_op jit(solution)/shard_map/ppermute | solution.py:76
  74.9 6.0 %collective-permute-start.8 = (f32[8,128]{1,0:T(8,128)S(1)}, f32[8,128]{1,0:T(8,128)S(1)}, u32[]{:S(2)}, u32[]{:S(2)}) collective-permute-start(f32[8,128]{1,0:T(8,128)S(1)} %get-tuple-element.32.own_part_ref), channel_id=1, source_target_pairs={{0,8},{8,0},{1,9},{9,1},{2,10},{10,2},{3,11},{11,3},{4,12},{12,4},... | collective-permute-start | bytes 12296 | tf_op jit(solution)/shard_map/ppermute | solution.py:26

commit v4 on v3

--- a/solution.py
+++ b/solution.py
@@ -81,6 +81,23 @@
     return jnp.concatenate(
         [value, from_ahead(value, 1, outer), far, from_ahead(value, 3, outer)], axis=0
     )
+
+
+def by_distance(value, rows):
+    lanes = value.shape[1]
+    group = SIDE * rows
+    outer, inner = own_place()
+    value = pltpu.roll(value, (lanes - outer * group) % lanes, 1)
+    lane = lax.broadcasted_iota(jnp.int32, value.shape, 1)
+    shift = inner * rows
+    behind = pltpu.roll(value, (lanes - shift) % lanes, 1)
+    wrapped = pltpu.roll(value, (lanes - shift + group) % lanes, 1)
+    return jnp.where(lane % group < group - shift, behind, wrapped)
+
+
+def columns_of(row, rows):
+    lanes = row.shape[1]
+    return jnp.broadcast_to(row, (lanes, lanes)).T[:rows]
 
 
 def in_order(value, rows):
@@ -160,7 +177,8 @@
         preferred_element_type=F32,
     )
     targets = picked[0:1] + 256.0 * picked[1:2] + 65536.0 * picked[2:3]
-    targets_out_ref[...] = targets.astype(jnp.int32)
+    targets = by_distance(jnp.broadcast_to(targets, (STAT_ROWS, core_rows)), rows)
+    targets_out_ref[...] = targets[:1].astype(jnp.int32)
 
 
 def normed_kernel(features_ref, gain_ref, out_ref, inv_ref):
@@ -188,13 +206,13 @@
 
 
 def logits_kernel(
-    n_z, rows_ref, own_ref, sib_ref, targets_ref, extra_ref, own_logits_ref, sib_logits_ref, out_ref
+    n_z, rows_ref, own_ref, sib_ref, targets_ref, extra_ref,
+    own_logits_ref, sib_logits_ref, out_ref, top_ref, own_stats_ref,
 ):
     for weight_ref, logits_ref in ((own_ref, own_logits_ref), (sib_ref, sib_logits_ref)):
-        logits = lax.dot_general(
+        logits_ref[...] = lax.dot_general(
             weight_ref[...], rows_ref[...], CONTRACT_LAST, preferred_element_type=F32
         )
-        logits_ref[...] = in_order(logits, rows_ref.shape[0] // (SIDE * SIDE))
     parts = [own_logits_ref[...], sib_logits_ref[...]]
     top = jnp.maximum(*[jnp.max(part, axis=0, keepdims=True) for part in parts])
     total = sum(jnp.sum(jnp.exp(part - top), axis=0, keepdims=True) for part in parts)
@@ -202,11 +220,47 @@
     for block, part in enumerate(parts):
         hot = is_target(places_in(targets_ref, n_z, part.shape[0], block), part.shape)
         picked += jnp.sum(jnp.where(hot, part, 0.0), axis=0, keepdims=True)
+    top_ref[...] = jnp.broadcast_to(top, top_ref.shape)
+    row = lax.broadcasted_iota(jnp.int32, top_ref.shape, 0)
+    stats = jnp.where(row == 1, total, jnp.where(row == 2, picked, top))
+    stats = in_order(stats, rows_ref.shape[0] // (SIDE * SIDE))
+    stats = jnp.where((row == 3) | (row == 4), extra_ref[...], stats)
+    own_stats_ref[...] = stats
     for k in range(out_ref.shape[0]):
-        out_ref[k, 0:1, :] = top
-        out_ref[k, 1:2, :] = total
-        out_ref[k, 2:3, :] = picked
-        out_ref[k, 3:STAT_ROWS, :] = extra_ref[3:STAT_ROWS, :]
+        out_ref[k] = stats
+
+
+def sums_kernel(
+    n_z, own_logits_ref, sib_logits_ref, top_ref, targets_ref, own_ref, sib_ref,
+    own_power_ref, own_hot_ref, *refs,
+):
+    outs, coefs = refs[: SIDE - 1], refs[SIDE - 1 :]
+    rows = own_logits_ref.shape[1]
+    for block, (logits_ref, coef_ref) in enumerate(zip((own_logits_ref, sib_logits_ref), coefs)):
+        logits = logits_ref[...]
+        hot = is_target(places_in(targets_ref, n_z, logits.shape[0], block), logits.shape)
+        powers = jnp.where(hot, 0.0, jnp.exp(logits - top_ref[0:1, :]))
+        coef_ref[:rows, :] = powers.T.astype(coef_ref.dtype)
+        coef_ref[rows:, :] = hot.astype(F32).T.astype(coef_ref.dtype)
+    size = rows // SIDE
+
+    def body(i, carry):
+        columns = pl.ds(pl.multiple_of(i * CHUNK, CHUNK), CHUNK)
+        sums = sum(
+            lax.dot_general(
+                coef_ref[...], weight_ref[:, columns], CONTRACT_MIDDLE, preferred_element_type=F32
+            )
+            for coef_ref, weight_ref in zip(coefs, (own_ref, sib_ref))
+        )
+        own_power_ref[:, columns] = sums[:size]
+        own_hot_ref[:, columns] = sums[rows : rows + size].astype(BF16)
+        for k in range(1, SIDE):
+            part = slice(k * size, (k + 1) * size)
+            outs[k - 1][:size, columns] = sums[part].astype(BF16)
+            outs[k - 1][size:, columns] = sums[rows:][part].astype(BF16)
+        return carry
+
+    lax.fori_loop(0, own_ref.shape[1] // CHUNK, body, 0)
 
 
 def merged(got_ref):
@@ -221,76 +275,102 @@
     return top, total, picked
 
 
-def merge_kernel(got_ref, out_ref):
+def merge_kernel(got_ref, own_ref, out_ref):
     top, total, picked = merged(got_ref)
-    rest = got_ref[0, 3:STAT_ROWS, :]
-    for k in range(1, got_ref.shape[0]):
-        rest += got_ref[k, 3:STAT_ROWS, :]
+    row = lax.broadcasted_iota(jnp.int32, own_ref.shape, 0)
+    both = jnp.where(row == 0, top, jnp.where(row == 1, total, picked))
+    stats = jnp.where(row < 3, both, own_ref[...])
     for k in range(out_ref.shape[0]):
-        out_ref[k, 0:1, :] = top
-        out_ref[k, 1:2, :] = total
-        out_ref[k, 2:3, :] = picked
-        out_ref[k, 3:STAT_ROWS, :] = rest
-
-
-def term_kernel(
-    n_z, own_logits_ref, sib_logits_ref, got_ref, targets_ref, own_ref, sib_ref,
-    out_ref, part_ref, own_coef_ref, sib_coef_ref,
-):
+        out_ref[k] = stats
+
+
+def outer_kernel(got_ref, own_power_ref, own_hot_ref, *refs):
+    blocks, refs = refs[: SIDE - 1], refs[SIDE - 1 :]
+    power_out_ref, hot_out_ref, outs = refs[0], refs[1], refs[2 : SIDE + 1]
+    factors_ref, part_ref, scale_ref = refs[SIDE + 1 :]
+    size = own_power_ref.shape[0]
+    rows = size // SIDE
+    outer, inner = own_place()
+    core = lax.axis_index("c")
+    senders = got_ref.shape[0]
+    plane = got_ref[0]
+    entries = got_ref[0]
+    for k in range(1, senders):
+        plane = jnp.maximum(plane, got_ref[k])
+        entries += got_ref[k]
+    plane_top = plane[5:6, :]
     top, total, picked = merged(got_ref)
     log_total = top + jnp.log(total)
-    ratio = (picked - log_total - got_ref[0, 3:4, :]) * got_ref[0, 4:5, :]
+    ratio = (picked - log_total - entries[3:4, :]) * entries[4:5, :]
     part_ref[...] = jnp.broadcast_to(jnp.sum(ratio, axis=1, keepdims=True), part_ref.shape)
-    for block, (logits_ref, coef_ref) in enumerate(
-        ((own_logits_ref, own_coef_ref), (sib_logits_ref, sib_coef_ref))
-    ):
-        logits = logits_ref[...]
-        hot = is_target(places_in(targets_ref, n_z, logits.shape[0], block), logits.shape)
-        shifted = hot.astype(F32) - jnp.exp(logits - log_total)
-        coef_ref[...] = shifted.T.astype(coef_ref.dtype)
+    shape = part_ref.shape
+    for i, factor in enumerate((1.0 - jnp.exp(picked - log_total), jnp.exp(plane_top - log_total))):
+        factor = by_distance(jnp.broadcast_to(factor, shape), rows)
+        factors_ref[i] = columns_of(factor[0:1, :], rows)
+    for k in range(SIDE):
+        x, y = place_on(inner, (outer + SIDE - k) % SIDE, core)
+        scale = jnp.exp(got_ref[y * SIDE + x] - plane_top)
+        scale_ref[k] = columns_of(by_distance(scale, rows)[5:6, :], size)
 
     def body(i, carry):
-        columns = pl.ds(pl.multiple_of(i * CHUNK, CHUNK), CHUNK)
-        out_ref[:, columns] = sum(
-            lax.dot_general(
-                coef_ref[...], weight_ref[:, columns], CONTRACT_MIDDLE, preferred_element_type=F32
-            )
-            for coef_ref, weight_ref in ((own_coef_ref, own_ref), (sib_coef_ref, sib_ref))
-        ).astype(out_ref.dtype)
+        for j in range(CHUNK // LANES):
+            columns = pl.ds(pl.multiple_of(i * CHUNK + j * LANES, LANES), LANES)
+            power = scale_ref[0] * own_power_ref[:, columns]
+            hot = own_hot_ref[:, columns].astype(F32)
+            for k in range(1, SIDE):
+                power += scale_ref[k] * blocks[k - 1][:size, columns].astype(F32)
+                hot += blocks[k - 1][size:, columns].astype(F32)
+            power_out_ref[:, columns] = power[:rows]
+            hot_out_ref[:, columns] = hot[:rows]
+            for m in range(1, SIDE):
+                part = slice(m * rows, (m + 1) * rows)
+                both = jnp.concatenate([power[part], hot[part]], axis=0)
+                outs[m - 1][:, columns] = both.astype(BF16)
         return carry
 
-    lax.fori_loop(0, out_ref.shape[1] // CHUNK, body, 0)
-
-
-def reduce_kernel(pieces_ref, features_ref, gain_ref, out_ref):
+    lax.fori_loop(0, own_power_ref.shape[1] // CHUNK, body, 0)
+
+
+def reduce_kernel(factors_ref, features_ref, gain_ref, own_power_ref, own_hot_ref, *refs):
+    blocks, out_ref = refs[: SIDE - 1], refs[SIDE - 1]
     parts, rows, width = features_ref.shape
     dots = jnp.zeros((rows, 1), F32)
     for k in range(parts):
         columns = slice(k * width, (k + 1) * width)
-        pairs = pieces_ref[0 : 2 * rows, columns].astype(F32)
-        for i in range(1, pieces_ref.shape[0] // (2 * rows)):
-            pairs += pieces_ref[i * 2 * rows : (i + 1) * 2 * rows, columns].astype(F32)
-        scaled = (pairs[:rows] + pairs[rows:]) * gain_ref[:, columns]
+        power, hot = own_power_ref[:, columns], own_hot_ref[:, columns]
+        for block in blocks:
+            both = block[:, columns].astype(F32)
+            power += both[:rows]
+            hot += both[rows:]
+        term = factors_ref[0][:, :1] * hot - factors_ref[1][:, :1] * power
+        scaled = term * gain_ref[:, columns]
         out_ref[k, :, :width] = scaled
         dots += jnp.sum(scaled * features_ref[k], axis=1, keepdims=True)
+    lane = lax.broadcasted_iota(jnp.int32, (rows, LANES), 1)
+    rest = jnp.broadcast_to(dots, (rows, LANES))
+    terms = jnp.zeros((rows, LANES), F32)
+    for i in range(3):
+        digits = rest.astype(BF16).astype(F32)
+        terms = jnp.where(lane == i, digits, terms)
+        rest -= digits
     for k in range(parts):
-        out_ref[k, :, width:] = jnp.broadcast_to(dots, (rows, LANES))
+        out_ref[k, :, width:] = terms
 
 
 def final_kernel(
     full_width, last_ref, hidden_ref, inv_ref, live_ref, own_part_ref, sib_part_ref, loss_ref, out_ref
 ):
     rows, width = out_ref.shape
-    scaled = last_ref[0]
+    scaled = last_ref[0].astype(F32)
     for k in range(1, last_ref.shape[0]):
-        scaled += last_ref[k]
+        scaled += last_ref[k].astype(F32)
     value = -DPO_BETA * (own_part_ref[...] + sib_part_ref[...])
     loss = jnp.maximum(value, 0.0) + jnp.log1p(jnp.exp(-jnp.abs(value)))
     loss_ref[...] = loss[:1, :1]
     slope = -DPO_BETA / (1.0 + jnp.exp(-value))
     row_grad = (slope * live_ref[...])[:, :1]
     inv_rms = inv_ref[:, :1]
-    row_dot = row_grad * scaled[:, width : width + 1] / full_width
+    row_dot = row_grad * jnp.sum(scaled[:, width:], axis=1, keepdims=True) / full_width
     input_grad = inv_rms * (row_grad * scaled[:, :width]) - hidden_ref[...] * (
         inv_rms * inv_rms * inv_rms * row_dot
     )
@@ -347,12 +427,20 @@
         moved=2 * half * full_width,
     )
     normed, sib_weight = lax.optimization_barrier((normed, sib_weight))
-    own_weight = pltpu.with_memory_space_constraint(other_core(sib_weight), pltpu.VMEM)
+    own_weight = other_core(sib_weight)
     sib_weight = pltpu.with_memory_space_constraint(sib_weight, pltpu.VMEM)
     rows = gather_from(gather_from(normed, False), True)
-    own_logits, sib_logits, stats = run(
+    own_weight = pltpu.with_memory_space_constraint(own_weight, pltpu.VMEM)
+    block = half // SIDE
+    own_logits, sib_logits, stats, tops, own_stats = run(
         functools.partial(logits_kernel, n_z),
-        [((voc_dev, half), F32), ((voc_dev, half), F32), ((n_plane, STAT_ROWS, half), F32)],
+        [
+            ((voc_dev, half), F32),
+            ((voc_dev, half), F32),
+            ((n_z, STAT_ROWS, half), F32),
+            ((STAT_ROWS, half), F32),
+            ((STAT_ROWS, half), F32),
+        ],
         [],
         rows,
         own_weight,
@@ -362,44 +450,58 @@
         flops=flops,
         moved=moved,
     )
-    (stats,) = run(
-        merge_kernel, [((n_z, STAT_ROWS, half), F32)], [], exchange(stats, PLANE), moved=1 << 17
-    )
-    chip_term, own_part = run(
-        functools.partial(term_kernel, n_z),
-        [((half, full_width), BF16), ((tok_dev, LANES), F32)],
-        [pltpu.VMEM((half, voc_dev), BF16)] * 2,
+    own_power, own_hot, *blocks = run(
+        functools.partial(sums_kernel, n_z),
+        [((block, full_width), F32), ((block, full_width), BF16)]
+        + [((2 * block, full_width), BF16)] * (SIDE - 1),
+        [pltpu.VMEM((2 * half, voc_dev), BF16)] * 2,
         own_logits,
         sib_logits,
-        exchange(stats, "z"),
+        tops,
         targets,
         own_weight,
         sib_weight,
-        flops=flops,
+        flops=2 * flops,
         moved=moved,
     )
-    chip_term, sib_part = lax.optimization_barrier((chip_term, other_core(own_part)))
-    pieces = lax.all_to_all(
-        chip_term.reshape(n_plane, tok_dev, full_width),
-        CTX,
-        0,
-        0,
-        axis_index_groups=[
-            [device(y, x, 0) for x in range(SIDE) for y in range(SIDE)],
-            [device(y, x, 1) for y in range(SIDE) for x in range(SIDE)],
-        ],
-        tiled=True,
-    )
+    stats, *blocks = lax.optimization_barrier((stats, *blocks))
+    blocks = [from_ahead(value, SIDE - 1 - k, True) for k, value in enumerate(blocks)]
+    (stats,) = run(
+        merge_kernel,
+        [((n_plane, STAT_ROWS, half), F32)],
+        [],
+        exchange(stats, "z"),
+        own_stats,
+        moved=1 << 17,
+    )
+    own_power, own_hot, *blocks, factors, own_part = run(
+        outer_kernel,
+        [((tok_dev, full_width), F32)] * 2
+        + [((2 * tok_dev, full_width), BF16)] * (SIDE - 1)
+        + [((2, tok_dev, half), F32), ((tok_dev, LANES), F32)],
+        [pltpu.VMEM((SIDE, block, half), F32)],
+        exchange(stats, PLANE),
+        own_power,
+        own_hot,
+        *blocks,
+        moved=8 * half * full_width,
+    )
+    blocks = [from_ahead(value, SIDE - 1 - k, False) for k, value in enumerate(blocks)]
+    sib_part = other_core(own_part)
     (last,) = run(
         reduce_kernel,
         [((n_z, tok_dev, part_width + LANES), F32)],
         [],
-        pieces.reshape(half, full_width),
+        factors,
         features,
         gain,
+        own_power,
+        own_hot,
+        *blocks,
         moved=4 * half * full_width,
     )
-    last = exchange(last, "z")
+    last, sib_part = lax.optimization_barrier((last, sib_part))
+    last = exchange(last.astype(BF16), "z")
     loss, hidden_grad = pl.pallas_call(
         functools.partial(final_kernel, full_width),
         in_specs=[IN_VMEM] * 6,

time: 127 us -> 115 us (0.906)
  the two profiles are of different devices: /device:TPU:1 before, /device:TPU:6 now
where the time goes in v4:
time: 115 us
  blocking collectives  58.6 us (51%)
  waiting for transfers between devices  23.3 us (20%)
  starting transfers between devices  18 us (16%)
  Pallas kernels  13.8 us (12%)
    all_to_all x4, blocking collectives, exchange(): return lax.all_to_all(value, axes, 0, 0, tiled=True)  58.6 us
    ppermute x12, waiting for transfers between devices, from_ahead(): return lax.ppermute(value, CTX, pairs)  23.3 us
    ppermute x12, starting transfers between devices, from_ahead(): return lax.ppermute(value, CTX, pairs)  17.8 us
    pallas_call x7, Pallas kernels, run(): pl.pallas_call(kernel, in_specs=specs or [IN_VMEM] * len(operands), out_s...  13.1 us
  transfers between devices with their start and end apart: 15, of which 4 were waited for; matrix products, arithmetic and copies ran while one was open for 0% of the time, Pallas kernels for 1%

profile of v4, /device:TPU:6, one launch (start us, length us, event | category | flops | bytes accessed | tf_op | source)
XLA Modules:
  0.0 114.8 jit_solution(11335660403605623598)
XLA Ops:
  0.6 0.1 collective-permute-start
  0.7 1.2 %shard_map.86 = (bf16[64,1024]{1,0:T(8,128)(2,1)S(1)}, f32[8,1024]{1,0:T(8,128)S(1)}, f32[1,8192]{1,0:T(1,128)S(1)}, s32[1,128]{1,0:T(1,128)S(1)}, f32[8,128]{1,0:T(8,128)S(1)}, /*index=5*/f32[8,128]{1,0:T(8,128)S(1)}) custom-call(bf16[8,1024]{1,0:T(8,128)(2,1)} %hidden_hbm.1, f32[1,8192]{1,0:T(1,128)} %bitcast.5, s32[1,256]{1,0:T(1,128)} %bitcast.6, ...), custom_call_target="tpu_custom_call" | custom-call | bytes 1048576 | tf_op jit(solution)/shard_map/pallas_call | solution.py:39
  1.9 18.0 %all_to_all.20 = bf16[8,8,1024]{2,1,0:T(8,128)(2,1)S(1)} all-to-all(bf16[8,8,1024]{2,1,0:T(8,128)(2,1)S(1)} %bitcast.4), channel_id=1, replica_groups=mesh['y'=4,'x'=4,'c'=2,'z'=8] {'z'}, dimensions={0} | all-to-all | bytes 262144 | tf_op jit(solution)/shard_map/all_to_all | solution.py:30
  19.9 0.1 shard_map.87
  20.1 0.0 collective-permute-done.sib_ref
  20.1 0.1 collective-permute-start.7
  20.2 1.7 %collective-permute-start.3 = (bf16[8,8192]{1,0:T(8,128)(2,1)S(1)}, bf16[8,8192]{1,0:T(8,128)(2,1)S(1)}, u32[]{:S(2)}, u32[]{:S(2)}) collective-permute-start(bf16[8,8192]{1,0:T(8,128)(2,1)S(1)} %get-tuple-element.40), channel_id=1, source_target_pairs={{192,0},{56,8},{208,16},{8,24},{224,32},{24,40},{240,48},{40,56},{... | collective-permute-start | bytes 393224 | tf_op jit(solution)/shard_map/ppermute | solution.py:76
  21.8 2.9 %collective-permute-start.2 = (bf16[8,8192]{1,0:T(8,128)(2,1)S(1)}, bf16[8,8192]{1,0:T(8,128)(2,1)S(1)}, u32[]{:S(2)}, u32[]{:S(2)}) collective-permute-start(bf16[8,8192]{1,0:T(8,128)(2,1)S(1)} %get-tuple-element.40), channel_id=1, source_target_pairs={{128,0},{40,8},{144,16},{56,24},{160,32},{8,40},{176,48},{24,56},{... | collective-permute-start | bytes 393224 | tf_op jit(solution)/shard_map/ppermute | solution.py:76
  24.7 1.3 %collective-permute-start.1 = (bf16[8,8192]{1,0:T(8,128)(2,1)S(1)}, bf16[8,8192]{1,0:T(8,128)(2,1)S(1)}, u32[]{:S(2)}, u32[]{:S(2)}) collective-permute-start(bf16[8,8192]{1,0:T(8,128)(2,1)S(1)} %get-tuple-element.40), channel_id=1, source_target_pairs={{64,0},{24,8},{80,16},{40,24},{96,32},{56,40},{112,48},{8,56},{128... | collective-permute-start | bytes 393224 | tf_op jit(solution)/shard_map/ppermute | solution.py:76
  26.1 3.6 %collective-permute-done.1 = bf16[8,8192]{1,0:T(8,128)(2,1)S(1)} collective-permute-done((bf16[8,8192]{1,0:T(8,128)(2,1)S(1)}, bf16[8,8192]{1,0:T(8,128)(2,1)S(1)}, u32[]{:S(2)}, u32[]{:S(2)}) %collective-permute-start.1) | collective-permute-done | bytes 131104 | tf_op jit(solution)/shard_map/ppermute | solution.py:76
  29.7 0.0 collective-permute-done.2
  29.8 0.0 collective-permute-done.3
  29.8 0.9 collective-permute-start.4
  30.7 2.4 %collective-permute-start.6 = (bf16[32,8192]{1,0:T(8,128)(2,1)S(1)}, bf16[32,8192]{1,0:T(8,128)(2,1)S(1)}, u32[]{:S(2)}, u32[]{:S(2)}) collective-permute-start(bf16[32,8192]{1,0:T(8,128)(2,1)S(1)} %get-tuple-element.72), channel_id=1, source_target_pairs={{48,0},{200,8},{0,16},{216,24},{16,32},{232,40},{32,48},{248,56},{... | collective-permute-start | bytes 1572872 | tf_op jit(solution)/shard_map/ppermute | solution.py:76
  33.1 0.2 collective-permute-start.5
  33.3 12.6 %collective-permute-done.4 = bf16[32,8192]{1,0:T(8,128)(2,1)S(1)} collective-permute-done((bf16[32,8192]{1,0:T(8,128)(2,1)S(1)}, bf16[32,8192]{1,0:T(8,128)(2,1)S(1)}, u32[]{:S(2)}, u32[]{:S(2)}) %collective-permute-start.4) | collective-permute-done | bytes 524320 | tf_op jit(solution)/shard_map/ppermute | solution.py:76
  45.9 0.0 collective-permute-done.5
  46.0 0.0 collective-permute-done.6
  46.0 0.0 collective-permute-done.7.own_ref
  46.0 4.7 %shard_map.88 = (f32[501,128]{1,0:T(8,128)S(1)}, f32[501,128]{1,0:T(8,128)S(1)}, f32[8,8,128]{2,1,0:T(8,128)S(1)}, f32[8,128]{1,0:T(8,128)S(1)}, f32[8,128]{1,0:T(8,128)S(1)}) custom-call(bf16[128,8192]{1,0:T(8,128)(2,1)S(1)} %constant_dynamic-update-slice_fusion.4.rows_ref, bf16[501,8192]{1,0:T(8,128)(2,1)S(1)} %collective-permute-done.7.own_ref, ...), custom_call_target="tpu_custom_call" | custom-call | flops 2101346304 | bytes 20611072 | tf_op jit(solution)/shard_map/pallas_call | solution.py:39
  50.8 5.3 %shard_map.89 = (f32[32,8192]{1,0:T(8,128)S(1)}, bf16[32,8192]{1,0:T(8,128)(2,1)S(1)}, bf16[64,8192]{1,0:T(8,128)(2,1)S(1)}, bf16[64,8192]{1,0:T(8,128)(2,1)S(1)}, bf16[64,8192]{1,0:T(8,128)(2,1)S(1)}) custom-call(f32[501,128]{1,0:T(8,128)S(1)} %get-tuple-element.45.own_logits_ref, f32[501,128]{1,0:T(8,128)S(1)} %get-tuple-element.46.sib_logits_ref, ...), custom_call_target="tpu_custom_call" | custom-call | flops 4202692608 | bytes 20611072 | tf_op jit(solution)/shard_map/pallas_call | solution.py:39
  56.0 3.2 %collective-permute-start.8 = (bf16[64,8192]{1,0:T(8,128)(2,1)S(1)}, bf16[64,8192]{1,0:T(8,128)(2,1)S(1)}, u32[]{:S(2)}, u32[]{:S(2)}) collective-permute-start(bf16[64,8192]{1,0:T(8,128)(2,1)S(1)} %get-tuple-element.55), channel_id=1, source_target_pairs={{48,0},{200,8},{0,16},{216,24},{16,32},{232,40},{32,48},{248,56},{... | collective-permute-start | bytes 3145736 | tf_op jit(solution)/shard_map/ppermute | solution.py:76
  59.3 0.0 collective-permute-start.9
  59.3 1.0 collective-permute-start.10
  60.2 10.4 %all_to_all.21.got_ref = f32[8,8,128]{2,1,0:T(8,128)S(1)} all-to-all(f32[8,8,128]{2,1,0:T(8,128)S(1)} %get-tuple-element.51), channel_id=1, replica_groups=mesh['y'=4,'x'=4,'c'=2,'z'=8] {'z'}, dimensions={0} | all-to-all | bytes 65536 | tf_op jit(solution)/shard_map/all_to_all | solution.py:30
  70.6 18.6 %all_to_all.22.got_ref = f32[16,8,128]{2,1,0:T(8,128)S(1)} all-to-all(f32[16,8,128]{2,1,0:T(8,128)S(1)} %shard_map.90), channel_id=1, replica_groups=mesh['y'=4,'x'=4,'c'=2,'z'=8] {'y','x'}, dimensions={0} | all-to-all | bytes 131072 | tf_op jit(solution)/shard_map/all_to_all | solution.py:30
  89.2 0.0 collective-permute-done.8.refs_0_
  89.2 0.0 collective-permute-done.9.refs_1_
  89.2 0.0 collective-permute-done.10.refs_2_
  89.2 1.5 %shard_map.91 = (f32[8,8192]{1,0:T(8,128)S(1)}, f32[8,8192]{1,0:T(8,128)S(1)}, bf16[16,8192]{1,0:T(8,128)(2,1)S(1)}, bf16[16,8192]{1,0:T(8,128)(2,1)S(1)}, bf16[...) custom-call(f32[16,8,128]{2,1,0:T(8,128)S(1)} %all_to_all.22.got_ref, ...), custom_call_target="tpu_custom_call" | custom-call | bytes 8388608 | tf_op jit(solution)/shard_map/pallas_call | solution.py:39
  90.7 1.0 collective-permute-start.11
  91.7 1.7 %collective-permute-start.12 = (bf16[16,8192]{1,0:T(8,128)(2,1)S(1)}, bf16[16,8192]{1,0:T(8,128)(2,1)S(1)}, u32[]{:S(2)}, u32[]{:S(2)}) collective-permute-start(bf16[16,8192]{1,0:T(8,128)(2,1)S(1)} %get-tuple-element.62), channel_id=1, source_target_pairs={{128,0},{40,8},{144,16},{56,24},{160,32},{8,40},{176,48},{24,56},{... | collective-permute-start | bytes 786440 | tf_op jit(solution)/shard_map/ppermute | solution.py:76
  93.4 1.5 %collective-permute-start.13 = (bf16[16,8192]{1,0:T(8,128)(2,1)S(1)}, bf16[16,8192]{1,0:T(8,128)(2,1)S(1)}, u32[]{:S(2)}, u32[]{:S(2)}) collective-permute-start(bf16[16,8192]{1,0:T(8,128)(2,1)S(1)} %get-tuple-element.63), channel_id=1, source_target_pairs={{64,0},{24,8},{80,16},{40,24},{96,32},{56,40},{112,48},{8,56},{128... | collective-permute-start | bytes 786440 | tf_op jit(solution)/shard_map/ppermute | solution.py:76
  95.0 0.0 collective-permute-start.14
  95.0 6.2 %collective-permute-done.11.refs_0_ = bf16[16,8192]{1,0:T(8,128)(2,1)S(1)} collective-permute-done((bf16[16,8192]{1,0:T(8,128)(2,1)S(1)}, bf16[16,8192]{1,0:T(8,128)(2,1)S(1)}, u32[]{:S(2)}, u32[]{:S(2)}) %collective-permute-start.11) | collective-permute-done | bytes 262176 | tf_op jit(solution)/shard_map/ppermute | solution.py:76
  101.2 0.0 collective-permute-done.12.refs_1_
  101.2 0.9 collective-permute-done.13.refs_2_
  102.1 0.3 shard_map.92
  102.4 0.0 collective-permute-done.14.sib_part_ref
  102.4 11.6 %all_to_all.23.last_ref = bf16[8,8,1152]{2,1,0:T(8,128)(2,1)S(1)} all-to-all(bf16[8,8,1152]{2,1,0:T(8,128)(2,1)S(1)} %convert_element_type.7), channel_id=1, replica_groups=mesh['y'=4,'x'=4,'c'=2,'z'=8] {'z'}, dimensions={0} | all-to-all | bytes 294912 | tf_op jit(solution)/shard_map/all_to_all | solution.py:30
  114.0 0.8 shard_map.93
  (10 shorter events, 0.3 us)
Async XLA Ops:
  0.6 19.4 %collective-permute-start = (bf16[501,8192]{1,0:T(8,128)(2,1)}, bf16[501,8192]{1,0:T(8,128)(2,1)S(1)}, u32[]{:S(2)}, u32[]{:S(2)}) collective-permute-start(bf16[501,8192]{1,0:T(8,128)(2,1)} %param.9), channel_id=1, source_target_pairs={{0,8},{8,0},{1,9},{9,1},{2,10},{10,2},{3,11},{11,3},{4,12},{12,4},... | collective-permute-start | bytes 24625160 | tf_op jit(solution)/shard_map/ppermute | solution.py:26
  20.1 26.0 %collective-permute-start.7 = (bf16[501,8192]{1,0:T(8,128)(2,1)S(1)}, bf16[501,8192]{1,0:T(8,128)(2,1)S(1)}, u32[]{:S(2)}, u32[]{:S(2)}) collective-permute-start(bf16[501,8192]{1,0:T(8,128)(2,1)S(1)} %collective-permute-done.sib_ref), channel_id=1, source_target_pairs={{0,8},{8,0},{1,9},{9,1},{2,10},{10,2},{3,11},{11,3},{4,12},{12,4},... | collective-permute-start | bytes 24625160 | tf_op jit(solution)/shard_map/ppermute | solution.py:26
  20.2 9.6 %collective-permute-start.3 = (bf16[8,8192]{1,0:T(8,128)(2,1)S(1)}, bf16[8,8192]{1,0:T(8,128)(2,1)S(1)}, u32[]{:S(2)}, u32[]{:S(2)}) collective-permute-start(bf16[8,8192]{1,0:T(8,128)(2,1)S(1)} %get-tuple-element.40), channel_id=1, source_target_pairs={{192,0},{56,8},{208,16},{8,24},{224,32},{24,40},{240,48},{40,56},{... | collective-permute-start | bytes 393224 | tf_op jit(solution)/shard_map/ppermute | solution.py:76
  21.8 7.9 %collective-permute-start.2 = (bf16[8,8192]{1,0:T(8,128)(2,1)S(1)}, bf16[8,8192]{1,0:T(8,128)(2,1)S(1)}, u32[]{:S(2)}, u32[]{:S(2)}) collective-permute-start(bf16[8,8192]{1,0:T(8,128)(2,1)S(1)} %get-tuple-element.40), channel_id=1, source_target_pairs={{128,0},{40,8},{144,16},{56,24},{160,32},{8,40},{176,48},{24,56},{... | collective-permute-start | bytes 393224 | tf_op jit(solution)/shard_map/ppermute | solution.py:76
  24.7 5.0 %collective-permute-start.1 = (bf16[8,8192]{1,0:T(8,128)(2,1)S(1)}, bf16[8,8192]{1,0:T(8,128)(2,1)S(1)}, u32[]{:S(2)}, u32[]{:S(2)}) collective-permute-start(bf16[8,8192]{1,0:T(8,128)(2,1)S(1)} %get-tuple-element.40), channel_id=1, source_target_pairs={{64,0},{24,8},{80,16},{40,24},{96,32},{56,40},{112,48},{8,56},{128... | collective-permute-start | bytes 393224 | tf_op jit(solution)/shard_map/ppermute | solution.py:76
  29.8 16.1 %collective-permute-start.4 = (bf16[32,8192]{1,0:T(8,128)(2,1)S(1)}, bf16[32,8192]{1,0:T(8,128)(2,1)S(1)}, u32[]{:S(2)}, u32[]{:S(2)}) collective-permute-start(bf16[32,8192]{1,0:T(8,128)(2,1)S(1)} %get-tuple-element.72), channel_id=1, source_target_pairs={{16,0},{72,8},{32,16},{88,24},{48,32},{104,40},{0,48},{120,56},{80... | collective-permute-start | bytes 1572872 | tf_op jit(solution)/shard_map/ppermute | solution.py:76
  30.7 15.3 %collective-permute-start.6 = (bf16[32,8192]{1,0:T(8,128)(2,1)S(1)}, bf16[32,8192]{1,0:T(8,128)(2,1)S(1)}, u32[]{:S(2)}, u32[]{:S(2)}) collective-permute-start(bf16[32,8192]{1,0:T(8,128)(2,1)S(1)} %get-tuple-element.72), channel_id=1, source_target_pairs={{48,0},{200,8},{0,16},{216,24},{16,32},{232,40},{32,48},{248,56},{... | collective-permute-start | bytes 1572872 | tf_op jit(solution)/shard_map/ppermute | solution.py:76
  33.1 12.8 %collective-permute-start.5 = (bf16[32,8192]{1,0:T(8,128)(2,1)S(1)}, bf16[32,8192]{1,0:T(8,128)(2,1)S(1)}, u32[]{:S(2)}, u32[]{:S(2)}) collective-permute-start(bf16[32,8192]{1,0:T(8,128)(2,1)S(1)} %get-tuple-element.72), channel_id=1, source_target_pairs={{32,0},{136,8},{48,16},{152,24},{0,32},{168,40},{16,48},{184,56},{... | collective-permute-start | bytes 1572872 | tf_op jit(solution)/shard_map/ppermute | solution.py:76
  56.0 33.2 %collective-permute-start.8 = (bf16[64,8192]{1,0:T(8,128)(2,1)S(1)}, bf16[64,8192]{1,0:T(8,128)(2,1)S(1)}, u32[]{:S(2)}, u32[]{:S(2)}) collective-permute-start(bf16[64,8192]{1,0:T(8,128)(2,1)S(1)} %get-tuple-element.55), channel_id=1, source_target_pairs={{48,0},{200,8},{0,16},{216,24},{16,32},{232,40},{32,48},{248,56},{... | collective-permute-start | bytes 3145736 | tf_op jit(solution)/shard_map/ppermute | solution.py:76
  59.3 30.0 %collective-permute-start.9 = (bf16[64,8192]{1,0:T(8,128)(2,1)S(1)}, bf16[64,8192]{1,0:T(8,128)(2,1)S(1)}, u32[]{:S(2)}, u32[]{:S(2)}) collective-permute-start(bf16[64,8192]{1,0:T(8,128)(2,1)S(1)} %get-tuple-element.56), channel_id=1, source_target_pairs={{32,0},{136,8},{48,16},{152,24},{0,32},{168,40},{16,48},{184,56},{... | collective-permute-start | bytes 3145736 | tf_op jit(solution)/shard_map/ppermute | solution.py:76
  59.3 30.0 %collective-permute-start.10 = (bf16[64,8192]{1,0:T(8,128)(2,1)S(1)}, bf16[64,8192]{1,0:T(8,128)(2,1)S(1)}, u32[]{:S(2)}, u32[]{:S(2)}) collective-permute-start(bf16[64,8192]{1,0:T(8,128)(2,1)S(1)} %get-tuple-element.57), channel_id=1, source_target_pairs={{16,0},{72,8},{32,16},{88,24},{48,32},{104,40},{0,48},{120,56},{80... | collective-permute-start | bytes 3145736 | tf_op jit(solution)/shard_map/ppermute | solution.py:76
  90.7 10.5 %collective-permute-start.11 = (bf16[16,8192]{1,0:T(8,128)(2,1)S(1)}, bf16[16,8192]{1,0:T(8,128)(2,1)S(1)}, u32[]{:S(2)}, u32[]{:S(2)}) collective-permute-start(bf16[16,8192]{1,0:T(8,128)(2,1)S(1)} %get-tuple-element.61), channel_id=1, source_target_pairs={{192,0},{56,8},{208,16},{8,24},{224,32},{24,40},{240,48},{40,56},{... | collective-permute-start | bytes 786440 | tf_op jit(solution)/shard_map/ppermute | solution.py:76
  91.7 9.5 %collective-permute-start.12 = (bf16[16,8192]{1,0:T(8,128)(2,1)S(1)}, bf16[16,8192]{1,0:T(8,128)(2,1)S(1)}, u32[]{:S(2)}, u32[]{:S(2)}) collective-permute-start(bf16[16,8192]{1,0:T(8,128)(2,1)S(1)} %get-tuple-element.62), channel_id=1, source_target_pairs={{128,0},{40,8},{144,16},{56,24},{160,32},{8,40},{176,48},{24,56},{... | collective-permute-start | bytes 786440 | tf_op jit(solution)/shard_map/ppermute | solution.py:76
  93.4 8.7 %collective-permute-start.13 = (bf16[16,8192]{1,0:T(8,128)(2,1)S(1)}, bf16[16,8192]{1,0:T(8,128)(2,1)S(1)}, u32[]{:S(2)}, u32[]{:S(2)}) collective-permute-start(bf16[16,8192]{1,0:T(8,128)(2,1)S(1)} %get-tuple-element.63), channel_id=1, source_target_pairs={{64,0},{24,8},{80,16},{40,24},{96,32},{56,40},{112,48},{8,56},{128... | collective-permute-start | bytes 786440 | tf_op jit(solution)/shard_map/ppermute | solution.py:76
  95.0 7.4 %collective-permute-start.14 = (f32[8,128]{1,0:T(8,128)S(1)}, f32[8,128]{1,0:T(8,128)S(1)}, u32[]{:S(2)}, u32[]{:S(2)}) collective-permute-start(f32[8,128]{1,0:T(8,128)S(1)} %get-tuple-element.64.own_part_ref), channel_id=1, source_target_pairs={{0,8},{8,0},{1,9},{9,1},{2,10},{10,2},{3,11},{11,3},{4,12},{12,4},... | collective-permute-start | bytes 12296 | tf_op jit(solution)/shard_map/ppermute | solution.py:26

commit v5 on v4

--- a/solution.py
+++ b/solution.py
@@ -205,17 +205,30 @@
     return lax.broadcasted_iota(jnp.int32, shape, 0) == places
 
 
+def first_logits_kernel(rows_ref, own_ref, sib_ref, own_logits_ref, sib_logits_ref):
+    width = rows_ref.shape[1]
+    for weight_ref, logits_ref in ((own_ref, own_logits_ref), (sib_ref, sib_logits_ref)):
+        logits_ref[...] = lax.dot_general(
+            weight_ref[:, :width], rows_ref[...], CONTRACT_LAST, preferred_element_type=F32
+        )
+
+
 def logits_kernel(
-    n_z, rows_ref, own_ref, sib_ref, targets_ref, extra_ref,
+    n_z, rows_ref, own_first_ref, sib_first_ref, own_ref, sib_ref, targets_ref, extra_ref,
     own_logits_ref, sib_logits_ref, out_ref, top_ref, own_stats_ref,
 ):
-    for weight_ref, logits_ref in ((own_ref, own_logits_ref), (sib_ref, sib_logits_ref)):
-        logits_ref[...] = lax.dot_general(
-            weight_ref[...], rows_ref[...], CONTRACT_LAST, preferred_element_type=F32
+    width = rows_ref.shape[1]
+    for weight_ref, first_ref, logits_ref in (
+        (own_ref, own_first_ref, own_logits_ref),
+        (sib_ref, sib_first_ref, sib_logits_ref),
+    ):
+        logits_ref[...] = first_ref[...] + lax.dot_general(
+            weight_ref[:, width:], rows_ref[...], CONTRACT_LAST, preferred_element_type=F32
         )
     parts = [own_logits_ref[...], sib_logits_ref[...]]
     top = jnp.maximum(*[jnp.max(part, axis=0, keepdims=True) for part in parts])
     total = sum(jnp.sum(jnp.exp(part - top), axis=0, keepdims=True) for part in parts)
+    weighted = sum(jnp.sum(jnp.exp(part - top) * part, axis=0, keepdims=True) for part in parts)
     picked = jnp.zeros_like(top)
     for block, part in enumerate(parts):
         hot = is_target(places_in(targets_ref, n_z, part.shape[0], block), part.shape)
@@ -223,6 +236,7 @@
     top_ref[...] = jnp.broadcast_to(top, top_ref.shape)
     row = lax.broadcasted_iota(jnp.int32, top_ref.shape, 0)
     stats = jnp.where(row == 1, total, jnp.where(row == 2, picked, top))
+    stats = jnp.where(row == 6, weighted, stats)
     stats = in_order(stats, rows_ref.shape[0] // (SIDE * SIDE))
     stats = jnp.where((row == 3) | (row == 4), extra_ref[...], stats)
     own_stats_ref[...] = stats
@@ -232,35 +246,42 @@
 
 def sums_kernel(
     n_z, own_logits_ref, sib_logits_ref, top_ref, targets_ref, own_ref, sib_ref,
-    own_power_ref, own_hot_ref, *refs,
+    ahead_ref, behind_ref, own_rest_ref, sib_rest_ref, *coefs,
 ):
-    outs, coefs = refs[: SIDE - 1], refs[SIDE - 1 :]
     rows = own_logits_ref.shape[1]
+    size = rows // SIDE
+    rests = (own_rest_ref, sib_rest_ref)
     for block, (logits_ref, coef_ref) in enumerate(zip((own_logits_ref, sib_logits_ref), coefs)):
         logits = logits_ref[...]
         hot = is_target(places_in(targets_ref, n_z, logits.shape[0], block), logits.shape)
-        powers = jnp.where(hot, 0.0, jnp.exp(logits - top_ref[0:1, :]))
-        coef_ref[:rows, :] = powers.T.astype(coef_ref.dtype)
-        coef_ref[rows:, :] = hot.astype(F32).T.astype(coef_ref.dtype)
-    size = rows // SIDE
-
-    def body(i, carry):
-        columns = pl.ds(pl.multiple_of(i * CHUNK, CHUNK), CHUNK)
-        sums = sum(
-            lax.dot_general(
-                coef_ref[...], weight_ref[:, columns], CONTRACT_MIDDLE, preferred_element_type=F32
-            )
-            for coef_ref, weight_ref in zip(coefs, (own_ref, sib_ref))
+        powers = jnp.where(hot, 0.0, jnp.exp(logits - top_ref[0:1, :])).T
+        hot = hot.astype(F32).T
+        for k in range(SIDE):
+            target_ref = (rests[block], coef_ref)[k % 2]
+            start = k // 2 * 2 * size
+            part = slice(k * size, (k + 1) * size)
+            target_ref[start : start + size, :] = powers[part].astype(BF16)
+            target_ref[start + size : start + 2 * size, :] = hot[part].astype(BF16)
+    sums = products(coefs, (own_ref, sib_ref))
+    ahead_ref[...] = sums[: 2 * size].astype(BF16)
+    behind_ref[...] = sums[2 * size :].astype(BF16)
+
+
+def products(coefs, weights):
+    return sum(
+        lax.dot_general(
+            coef_ref[...], weight_ref[...], CONTRACT_MIDDLE, preferred_element_type=F32
         )
-        own_power_ref[:, columns] = sums[:size]
-        own_hot_ref[:, columns] = sums[rows : rows + size].astype(BF16)
-        for k in range(1, SIDE):
-            part = slice(k * size, (k + 1) * size)
-            outs[k - 1][:size, columns] = sums[part].astype(BF16)
-            outs[k - 1][size:, columns] = sums[rows:][part].astype(BF16)
-        return carry
-
-    lax.fori_loop(0, own_ref.shape[1] // CHUNK, body, 0)
+        for coef_ref, weight_ref in zip(coefs, weights)
+    )
+
+
+def rest_kernel(own_rest_ref, sib_rest_ref, own_ref, sib_ref, own_power_ref, own_hot_ref, far_ref):
+    size = own_power_ref.shape[0]
+    sums = products((own_rest_ref, sib_rest_ref), (own_ref, sib_ref))
+    own_power_ref[...] = sums[:size]
+    own_hot_ref[...] = sums[size : 2 * size].astype(BF16)
+    far_ref[...] = sums[2 * size :].astype(BF16)
 
 
 def merged(got_ref):
@@ -268,113 +289,104 @@
     top = got_ref[0, 0:1, :]
     for k in range(1, senders):
         top = jnp.maximum(top, got_ref[k, 0:1, :])
-    total, picked = jnp.zeros_like(top), jnp.zeros_like(top)
+    total, picked, weighted = [jnp.zeros_like(top)] * 3
     for k in range(senders):
-        total += got_ref[k, 1:2, :] * jnp.exp(got_ref[k, 0:1, :] - top)
+        scale = jnp.exp(got_ref[k, 0:1, :] - top)
+        total += got_ref[k, 1:2, :] * scale
+        weighted += got_ref[k, 6:7, :] * scale
         picked += got_ref[k, 2:3, :]
-    return top, total, picked
+    return top, total, picked, weighted
 
 
 def merge_kernel(got_ref, own_ref, out_ref):
-    top, total, picked = merged(got_ref)
+    top, total, picked, weighted = merged(got_ref)
     row = lax.broadcasted_iota(jnp.int32, own_ref.shape, 0)
-    both = jnp.where(row == 0, top, jnp.where(row == 1, total, picked))
-    stats = jnp.where(row < 3, both, own_ref[...])
+    stats = own_ref[...]
+    for i, value in ((0, top), (1, total), (2, picked), (6, weighted)):
+        stats = jnp.where(row == i, value, stats)
     for k in range(out_ref.shape[0]):
         out_ref[k] = stats
 
 
-def outer_kernel(got_ref, own_power_ref, own_hot_ref, *refs):
-    blocks, refs = refs[: SIDE - 1], refs[SIDE - 1 :]
-    power_out_ref, hot_out_ref, outs = refs[0], refs[1], refs[2 : SIDE + 1]
-    factors_ref, part_ref, scale_ref = refs[SIDE + 1 :]
-    size = own_power_ref.shape[0]
-    rows = size // SIDE
-    outer, inner = own_place()
-    core = lax.axis_index("c")
-    senders = got_ref.shape[0]
-    plane = got_ref[0]
+def totals_kernel(got_ref, part_ref, dots_ref):
+    rows, lanes = part_ref.shape
+    top, total, picked, weighted = merged(got_ref)
     entries = got_ref[0]
-    for k in range(1, senders):
-        plane = jnp.maximum(plane, got_ref[k])
+    for k in range(1, got_ref.shape[0]):
         entries += got_ref[k]
-    plane_top = plane[5:6, :]
-    top, total, picked = merged(got_ref)
     log_total = top + jnp.log(total)
     ratio = (picked - log_total - entries[3:4, :]) * entries[4:5, :]
     part_ref[...] = jnp.broadcast_to(jnp.sum(ratio, axis=1, keepdims=True), part_ref.shape)
-    shape = part_ref.shape
-    for i, factor in enumerate((1.0 - jnp.exp(picked - log_total), jnp.exp(plane_top - log_total))):
-        factor = by_distance(jnp.broadcast_to(factor, shape), rows)
-        factors_ref[i] = columns_of(factor[0:1, :], rows)
+    dots = jnp.broadcast_to(picked - weighted / total, (STAT_ROWS, lanes))
+    dots_ref[...] = columns_of(by_distance(dots, rows)[0:1, :], rows)
+
+
+def outer_kernel(got_ref, own_power_ref, own_hot_ref, *refs):
+    blocks, (out_ref, scale_ref, total_ref) = refs[: SIDE - 1], refs[SIDE - 1 :]
+    size = own_power_ref.shape[0]
+    rows = size // SIDE
+    parts = out_ref.shape[0] // SIDE
+    width = out_ref.shape[2]
+    outer, inner = own_place()
+    core = lax.axis_index("c")
+    top, total, picked, _ = merged(got_ref)
+    log_total = top + jnp.log(total)
+    shape = got_ref.shape[1:]
+    hot_factor = by_distance(jnp.broadcast_to(1.0 - jnp.exp(picked - log_total), shape), rows)
+    scale_ref[SIDE] = columns_of(hot_factor[0:1, :], size)
     for k in range(SIDE):
         x, y = place_on(inner, (outer + SIDE - k) % SIDE, core)
-        scale = jnp.exp(got_ref[y * SIDE + x] - plane_top)
+        scale = jnp.exp(got_ref[y * SIDE + x] - log_total)
         scale_ref[k] = columns_of(by_distance(scale, rows)[5:6, :], size)
-
-    def body(i, carry):
-        for j in range(CHUNK // LANES):
-            columns = pl.ds(pl.multiple_of(i * CHUNK + j * LANES, LANES), LANES)
+    for z in range(parts):
+        for j in range(width // LANES):
+            columns = slice(z * width + j * LANES, z * width + (j + 1) * LANES)
             power = scale_ref[0] * own_power_ref[:, columns]
             hot = own_hot_ref[:, columns].astype(F32)
             for k in range(1, SIDE):
                 power += scale_ref[k] * blocks[k - 1][:size, columns].astype(F32)
                 hot += blocks[k - 1][size:, columns].astype(F32)
-            power_out_ref[:, columns] = power[:rows]
-            hot_out_ref[:, columns] = hot[:rows]
-            for m in range(1, SIDE):
-                part = slice(m * rows, (m + 1) * rows)
-                both = jnp.concatenate([power[part], hot[part]], axis=0)
-                outs[m - 1][:, columns] = both.astype(BF16)
-        return carry
-
-    lax.fori_loop(0, own_power_ref.shape[1] // CHUNK, body, 0)
-
-
-def reduce_kernel(factors_ref, features_ref, gain_ref, own_power_ref, own_hot_ref, *refs):
-    blocks, out_ref = refs[: SIDE - 1], refs[SIDE - 1]
-    parts, rows, width = features_ref.shape
-    dots = jnp.zeros((rows, 1), F32)
-    for k in range(parts):
-        columns = slice(k * width, (k + 1) * width)
-        power, hot = own_power_ref[:, columns], own_hot_ref[:, columns]
-        for block in blocks:
-            both = block[:, columns].astype(F32)
-            power += both[:rows]
-            hot += both[rows:]
-        term = factors_ref[0][:, :1] * hot - factors_ref[1][:, :1] * power
-        scaled = term * gain_ref[:, columns]
-        out_ref[k, :, :width] = scaled
-        dots += jnp.sum(scaled * features_ref[k], axis=1, keepdims=True)
-    lane = lax.broadcasted_iota(jnp.int32, (rows, LANES), 1)
-    rest = jnp.broadcast_to(dots, (rows, LANES))
-    terms = jnp.zeros((rows, LANES), F32)
-    for i in range(3):
-        digits = rest.astype(BF16).astype(F32)
-        terms = jnp.where(lane == i, digits, terms)
-        rest -= digits
-    for k in range(parts):
-        out_ref[k, :, width:] = terms
+            total_ref[:, j * LANES : (j + 1) * LANES] = scale_ref[SIDE] * hot - power
+        for m in range(SIDE):
+            term = total_ref[m * rows : (m + 1) * rows, :]
+            out_ref[(inner + m) % SIDE * parts + z] = term.astype(out_ref.dtype)
 
 
 def final_kernel(
-    full_width, last_ref, hidden_ref, inv_ref, live_ref, own_part_ref, sib_part_ref, loss_ref, out_ref
+    full_width, last_ref, hidden_ref, gain_ref, inv_ref, live_ref, dots_ref, own_part_ref,
+    sib_part_ref, loss_ref, out_ref,
 ):
     rows, width = out_ref.shape
-    scaled = last_ref[0].astype(F32)
+    term = last_ref[0].astype(F32)
     for k in range(1, last_ref.shape[0]):
-        scaled += last_ref[k].astype(F32)
+        term += last_ref[k].astype(F32)
+    own = pl.ds(pl.multiple_of(lax.axis_index("z") * width, width), width)
     value = -DPO_BETA * (own_part_ref[...] + sib_part_ref[...])
     loss = jnp.maximum(value, 0.0) + jnp.log1p(jnp.exp(-jnp.abs(value)))
     loss_ref[...] = loss[:1, :1]
     slope = -DPO_BETA / (1.0 + jnp.exp(-value))
     row_grad = (slope * live_ref[...])[:, :1]
     inv_rms = inv_ref[:, :1]
-    row_dot = row_grad * jnp.sum(scaled[:, width:], axis=1, keepdims=True) / full_width
-    input_grad = inv_rms * (row_grad * scaled[:, :width]) - hidden_ref[...] * (
+    row_dot = row_grad * (dots_ref[:, :1] / inv_rms) / full_width
+    input_grad = inv_rms * (row_grad * (term * gain_ref[:, own])) - hidden_ref[...] * (
         inv_rms * inv_rms * inv_rms * row_dot
     )
     out_ref[...] = (LOSS_SCALE * input_grad).astype(out_ref.dtype)
+
+
+def along_inner_and_z(value, n_z):
+    groups = [
+        [
+            device(*((inner, outer) if core == 0 else (outer, inner)), core) * n_z + z
+            for inner in range(SIDE)
+            for z in range(n_z)
+        ]
+        for core in range(2)
+        for outer in range(SIDE)
+    ]
+    return lax.all_to_all(
+        value, CTX + ("z",), 0, 0, axis_index_groups=groups, tiled=True
+    )
 
 
 def on_device(hidden, norm_gain, head_weight, targets, ref_logprobs, block_order, lengths):
@@ -429,9 +441,21 @@
     normed, sib_weight = lax.optimization_barrier((normed, sib_weight))
     own_weight = other_core(sib_weight)
     sib_weight = pltpu.with_memory_space_constraint(sib_weight, pltpu.VMEM)
-    rows = gather_from(gather_from(normed, False), True)
+    nearby = gather_from(normed, False)
+    first = gather_from(nearby[:, : full_width // 2], True)
+    rows = gather_from(nearby[:, full_width // 2 :], True)
     own_weight = pltpu.with_memory_space_constraint(own_weight, pltpu.VMEM)
     block = half // SIDE
+    first_logits = run(
+        first_logits_kernel,
+        [((voc_dev, half), F32)] * 2,
+        [],
+        first,
+        own_weight,
+        sib_weight,
+        flops=flops // 2,
+        moved=moved // 2,
+    )
     own_logits, sib_logits, stats, tops, own_stats = run(
         functools.partial(logits_kernel, n_z),
         [
@@ -443,6 +467,7 @@
         ],
         [],
         rows,
+        *first_logits,
         own_weight,
         sib_weight,
         targets,
@@ -450,22 +475,37 @@
         flops=flops,
         moved=moved,
     )
-    own_power, own_hot, *blocks = run(
+    ahead, behind, own_rest, sib_rest = run(
         functools.partial(sums_kernel, n_z),
-        [((block, full_width), F32), ((block, full_width), BF16)]
-        + [((2 * block, full_width), BF16)] * (SIDE - 1),
-        [pltpu.VMEM((2 * half, voc_dev), BF16)] * 2,
+        [((2 * block, full_width), BF16)] * 2 + [((half, voc_dev), BF16)] * 2,
+        [pltpu.VMEM((half, voc_dev), BF16)] * 2,
         own_logits,
         sib_logits,
         tops,
         targets,
         own_weight,
         sib_weight,
-        flops=2 * flops,
+        flops=flops,
         moved=moved,
     )
-    stats, *blocks = lax.optimization_barrier((stats, *blocks))
-    blocks = [from_ahead(value, SIDE - 1 - k, True) for k, value in enumerate(blocks)]
+    ahead, behind = from_ahead(ahead, 3, True), from_ahead(behind, 1, True)
+    own_power, own_hot, far = run(
+        rest_kernel,
+        [
+            ((block, full_width), F32),
+            ((block, full_width), BF16),
+            ((2 * block, full_width), BF16),
+        ],
+        [],
+        own_rest,
+        sib_rest,
+        own_weight,
+        sib_weight,
+        flops=flops,
+        moved=moved,
+    )
+    stats, far = lax.optimization_barrier((stats, far))
+    blocks = [ahead, from_ahead(far, 2, True), behind]
     (stats,) = run(
         merge_kernel,
         [((n_plane, STAT_ROWS, half), F32)],
@@ -474,44 +514,33 @@
         own_stats,
         moved=1 << 17,
     )
-    own_power, own_hot, *blocks, factors, own_part = run(
+    got = exchange(stats, PLANE)
+    own_part, dots = run(
+        totals_kernel, [((tok_dev, LANES), F32)] * 2, [], got, moved=1 << 17
+    )
+    sib_part = other_core(own_part)
+    (last,) = run(
         outer_kernel,
-        [((tok_dev, full_width), F32)] * 2
-        + [((2 * tok_dev, full_width), BF16)] * (SIDE - 1)
-        + [((2, tok_dev, half), F32), ((tok_dev, LANES), F32)],
-        [pltpu.VMEM((SIDE, block, half), F32)],
-        exchange(stats, PLANE),
+        [((SIDE * n_z, tok_dev, part_width), BF16)],
+        [pltpu.VMEM((SIDE + 1, block, half), F32), pltpu.VMEM((block, part_width), F32)],
+        got,
         own_power,
         own_hot,
         *blocks,
         moved=8 * half * full_width,
     )
-    blocks = [from_ahead(value, SIDE - 1 - k, False) for k, value in enumerate(blocks)]
-    sib_part = other_core(own_part)
-    (last,) = run(
-        reduce_kernel,
-        [((n_z, tok_dev, part_width + LANES), F32)],
-        [],
-        factors,
-        features,
-        gain,
-        own_power,
-        own_hot,
-        *blocks,
-        moved=4 * half * full_width,
-    )
     last, sib_part = lax.optimization_barrier((last, sib_part))
-    last = exchange(last.astype(BF16), "z")
+    last = along_inner_and_z(last, n_z)
     loss, hidden_grad = pl.pallas_call(
         functools.partial(final_kernel, full_width),
-        in_specs=[IN_VMEM] * 6,
+        in_specs=[IN_VMEM] * 8,
         out_specs=[IN_VMEM] * 2,
         out_shape=[
             jax.ShapeDtypeStruct((1, 1), F32),
             jax.ShapeDtypeStruct((tok_dev, part_width), BF16),
         ],
         compiler_params=pltpu.CompilerParams(vmem_limit_bytes=VMEM_LIMIT),
-    )(last, hidden_f32, inv_rms, live_rows, own_part, sib_part)
+    )(last, hidden_f32, gain, inv_rms, live_rows, dots, own_part, sib_part)
     return (loss[0, 0], hidden_grad)
 
 

time: 115 us -> 113 us (0.983)
  the two profiles are of different devices: /device:TPU:6 before, /device:TPU:1 now
where the time goes in v5:
time: 113 us; the launch traced here: 112 us
  blocking collectives  57.4 us (51%)
  starting transfers between devices  30.9 us (27%)
  Pallas kernels  13.1 us (12%)
  waiting for transfers between devices  9.81 us (9%)
    all_to_all x3, blocking collectives, exchange(): return lax.all_to_all(value, axes, 0, 0, tiled=True)  36.8 us
    all_to_all x1, blocking collectives, along_inner_and_z(): lax.all_to_all(value, CTX + ('z',), 0, 0, axis_index_groups=groups, tiled...  20.6 us
    ppermute x12, starting transfers between devices, from_ahead(): return lax.ppermute(value, CTX, pairs)  19.5 us
    pallas_call x9, Pallas kernels, run(): pl.pallas_call(kernel, in_specs=specs or [IN_VMEM] * len(operands), out_s...  12.4 us
    ppermute x3, starting transfers between devices, other_core(): return lax.ppermute(value, 'c', [(0, 1), (1, 0)])  11.4 us
    ppermute x12, waiting for transfers between devices, from_ahead(): return lax.ppermute(value, CTX, pairs)  9.8 us
  transfers between devices with their start and end apart: 15, of which 4 were waited for; matrix products, arithmetic and copies ran while one was open for 0% of the time, Pallas kernels for 2%

profile of v5, /device:TPU:1, one launch (start us, length us, event | category | flops | bytes accessed | tf_op | source)
XLA Modules:
  0.0 112.2 jit_solution(17876598606665357227)
XLA Ops:
  0.6 3.3 %collective-permute-start = (bf16[501,8192]{1,0:T(8,128)(2,1)}, bf16[501,8192]{1,0:T(8,128)(2,1)S(1)}, u32[]{:S(2)}, u32[]{:S(2)}) collective-permute-start(bf16[501,8192]{1,0:T(8,128)(2,1)} %param.9), channel_id=1, source_target_pairs={{0,8},{8,0},{1,9},{9,1},{2,10},{10,2},{3,11},{11,3},{4,12},{12,4},... | collective-permute-start | bytes 24625160 | tf_op jit(solution)/shard_map/ppermute | solution.py:26
  4.0 1.2 %shard_map.86 = (bf16[64,1024]{1,0:T(8,128)(2,1)S(1)}, f32[8,1024]{1,0:T(8,128)S(1)}, f32[1,8192]{1,0:T(1,128)S(1)}, s32[1,128]{1,0:T(1,128)S(1)}, f32[8,128]{1,0:T(8,128)S(1)}, /*index=5*/f32[8,128]{1,0:T(8,128)S(1)}) custom-call(bf16[8,1024]{1,0:T(8,128)(2,1)} %hidden_hbm.1, f32[1,8192]{1,0:T(1,128)} %bitcast.5, s32[1,256]{1,0:T(1,128)} %bitcast.6, ...), custom_call_target="tpu_custom_call" | custom-call | bytes 1048576 | tf_op jit(solution)/shard_map/pallas_call | solution.py:39
  5.1 14.8 %all_to_all.20 = bf16[8,8,1024]{2,1,0:T(8,128)(2,1)S(1)} all-to-all(bf16[8,8,1024]{2,1,0:T(8,128)(2,1)S(1)} %bitcast.4), channel_id=1, replica_groups=mesh['y'=4,'x'=4,'c'=2,'z'=8] {'z'}, dimensions={0} | all-to-all | bytes 262144 | tf_op jit(solution)/shard_map/all_to_all | solution.py:30
  19.9 0.1 shard_map.87
  20.0 0.0 collective-permute-done.sib_ref
  20.1 1.6 %collective-permute-start.10 = (bf16[501,8192]{1,0:T(8,128)(2,1)S(1)}, bf16[501,8192]{1,0:T(8,128)(2,1)S(1)}, u32[]{:S(2)}, u32[]{:S(2)}) collective-permute-start(bf16[501,8192]{1,0:T(8,128)(2,1)S(1)} %collective-permute-done.sib_ref), channel_id=1, source_target_pairs={{0,8},{8,0},{1,9},{9,1},{2,10},{10,2},{3,11},{11,3},{4,12},{12,4},... | collective-permute-start | bytes 24625160 | tf_op jit(solution)/shard_map/ppermute | solution.py:26
  21.7 1.2 %collective-permute-start.3 = (bf16[8,8192]{1,0:T(8,128)(2,1)S(1)}, bf16[8,8192]{1,0:T(8,128)(2,1)S(1)}, u32[]{:S(2)}, u32[]{:S(2)}) collective-permute-start(bf16[8,8192]{1,0:T(8,128)(2,1)S(1)} %get-tuple-element.37), channel_id=1, source_target_pairs={{192,0},{56,8},{208,16},{8,24},{224,32},{24,40},{240,48},{40,56},{... | collective-permute-start | bytes 393224 | tf_op jit(solution)/shard_map/ppermute | solution.py:76
  22.9 2.5 %collective-permute-start.2 = (bf16[8,8192]{1,0:T(8,128)(2,1)S(1)}, bf16[8,8192]{1,0:T(8,128)(2,1)S(1)}, u32[]{:S(2)}, u32[]{:S(2)}) collective-permute-start(bf16[8,8192]{1,0:T(8,128)(2,1)S(1)} %get-tuple-element.37), channel_id=1, source_target_pairs={{128,0},{40,8},{144,16},{56,24},{160,32},{8,40},{176,48},{24,56},{... | collective-permute-start | bytes 393224 | tf_op jit(solution)/shard_map/ppermute | solution.py:76
  25.3 1.2 %collective-permute-start.1 = (bf16[8,8192]{1,0:T(8,128)(2,1)S(1)}, bf16[8,8192]{1,0:T(8,128)(2,1)S(1)}, u32[]{:S(2)}, u32[]{:S(2)}) collective-permute-start(bf16[8,8192]{1,0:T(8,128)(2,1)S(1)} %get-tuple-element.37), channel_id=1, source_target_pairs={{64,0},{24,8},{80,16},{40,24},{96,32},{56,40},{112,48},{8,56},{128... | collective-permute-start | bytes 393224 | tf_op jit(solution)/shard_map/ppermute | solution.py:76
  26.5 2.9 %collective-permute-done.1 = bf16[8,8192]{1,0:T(8,128)(2,1)S(1)} collective-permute-done((bf16[8,8192]{1,0:T(8,128)(2,1)S(1)}, bf16[8,8192]{1,0:T(8,128)(2,1)S(1)}, u32[]{:S(2)}, u32[]{:S(2)}) %collective-permute-start.1) | collective-permute-done | bytes 131104 | tf_op jit(solution)/shard_map/ppermute | solution.py:76
  29.4 0.0 collective-permute-done.2
  29.5 0.0 collective-permute-done.3
  29.6 1.4 %collective-permute-start.9 = (bf16[32,4096]{1,0:T(8,128)(2,1)S(1)}, bf16[32,4096]{1,0:T(8,128)(2,1)S(1)}, u32[]{:S(2)}, u32[]{:S(2)}) collective-permute-start(bf16[32,4096]{1,0:T(8,128)(2,1)S(1)} %get-tuple-element.66), channel_id=1, source_target_pairs={{48,0},{200,8},{0,16},{216,24},{16,32},{232,40},{32,48},{248,56},{... | collective-permute-start | bytes 786440 | tf_op jit(solution)/shard_map/ppermute | solution.py:76
  30.9 2.6 %collective-permute-start.8 = (bf16[32,4096]{1,0:T(8,128)(2,1)S(1)}, bf16[32,4096]{1,0:T(8,128)(2,1)S(1)}, u32[]{:S(2)}, u32[]{:S(2)}) collective-permute-start(bf16[32,4096]{1,0:T(8,128)(2,1)S(1)} %get-tuple-element.66), channel_id=1, source_target_pairs={{32,0},{136,8},{48,16},{152,24},{0,32},{168,40},{16,48},{184,56},{... | collective-permute-start | bytes 786440 | tf_op jit(solution)/shard_map/ppermute | solution.py:76
  33.5 1.1 collective-permute-start.7
  34.6 0.4 collective-permute-start.6
  35.0 1.4 %collective-permute-done.9 = bf16[32,4096]{1,0:T(8,128)(2,1)S(1)} collective-permute-done((bf16[32,4096]{1,0:T(8,128)(2,1)S(1)}, bf16[32,4096]{1,0:T(8,128)(2,1)S(1)}, u32[]{:S(2)}, u32[]{:S(2)}) %collective-permute-start.9) | collective-permute-done | bytes 262176 | tf_op jit(solution)/shard_map/ppermute | solution.py:76
  36.4 4.2 %collective-permute-start.5 = (bf16[32,4096]{1,0:T(8,128)(2,1)S(1)}, bf16[32,4096]{1,0:T(8,128)(2,1)S(1)}, u32[]{:S(2)}, u32[]{:S(2)}) collective-permute-start(bf16[32,4096]{1,0:T(8,128)(2,1)S(1)} %get-tuple-element.67), channel_id=1, source_target_pairs={{32,0},{136,8},{48,16},{152,24},{0,32},{168,40},{16,48},{184,56},{... | collective-permute-start | bytes 786440 | tf_op jit(solution)/shard_map/ppermute | solution.py:76
  40.6 0.0 collective-permute-done.8
  40.6 0.0 collective-permute-start.4
  40.6 0.0 collective-permute-done.7
  40.6 0.1 pad_maximum_fusion.1.rows_ref
  40.7 2.5 %collective-permute-done.6 = bf16[32,4096]{1,0:T(8,128)(2,1)S(1)} collective-permute-done((bf16[32,4096]{1,0:T(8,128)(2,1)S(1)}, bf16[32,4096]{1,0:T(8,128)(2,1)S(1)}, u32[]{:S(2)}, u32[]{:S(2)}) %collective-permute-start.6) | collective-permute-done | bytes 262176 | tf_op jit(solution)/shard_map/ppermute | solution.py:76
  43.2 2.9 %collective-permute-done.5 = bf16[32,4096]{1,0:T(8,128)(2,1)S(1)} collective-permute-done((bf16[32,4096]{1,0:T(8,128)(2,1)S(1)}, bf16[32,4096]{1,0:T(8,128)(2,1)S(1)}, u32[]{:S(2)}, u32[]{:S(2)}) %collective-permute-start.5) | collective-permute-done | bytes 262176 | tf_op jit(solution)/shard_map/ppermute | solution.py:76
  46.1 0.0 collective-permute-done.4
  46.1 0.1 pad_maximum_fusion.rows_ref
  46.2 0.0 collective-permute-done.10.own_ref
  46.2 2.3 %shard_map.88 = (f32[501,128]{1,0:T(8,128)S(1)}, f32[501,128]{1,0:T(8,128)S(1)}) custom-call(bf16[128,4096]{1,0:T(8,128)(2,1)S(1)} %pad_maximum_fusion.1.rows_ref, bf16[501,8192]{1,0:T(8,128)(2,1)S(1)} %collective-permute-done.10.own_ref, bf16[501,8192]{1,0:T(8,128)(2,1)S(1)} %collective-permute-done.sib_ref), custom_call_target="tpu_custom_call" | custom-call | flops 1050673152 | bytes 10305536 | tf_op jit(solution)/shard_map/pallas_call | solution.py:39
  48.5 2.7 %shard_map.89 = (f32[501,128]{1,0:T(8,128)S(1)}, f32[501,128]{1,0:T(8,128)S(1)}, f32[8,8,128]{2,1,0:T(8,128)S(1)}, f32[8,128]{1,0:T(8,128)S(1)}, f32[8,128]{1,0:T(8,128)S(1)}) custom-call(bf16[128,4096]{1,0:T(8,128)(2,1)S(1)} %pad_maximum_fusion.rows_ref, f32[501,128]{1,0:T(8,128)S(1)} %get-tuple-element.39.own_first_ref, ...), custom_call_target="tpu_custom_call" | custom-call | flops 2101346304 | bytes 20611072 | tf_op jit(solution)/shard_map/pallas_call | solution.py:39
  51.2 2.5 %shard_map.90 = (bf16[64,8192]{1,0:T(8,128)(2,1)S(1)}, bf16[64,8192]{1,0:T(8,128)(2,1)S(1)}, bf16[128,501]{1,0:T(8,128)(2,1)S(1)}, bf16[128,501]{1,0:T(8,128)(2,1)S(1)}) custom-call(f32[501,128]{1,0:T(8,128)S(1)} %get-tuple-element.44.own_logits_ref, f32[501,128]{1,0:T(8,128)S(1)} %get-tuple-element.45.sib_logits_ref, ...), custom_call_target="tpu_custom_call" | custom-call | flops 2101346304 | bytes 20611072 | tf_op jit(solution)/shard_map/pallas_call | solution.py:39
  53.7 2.4 %shard_map.91 = (f32[32,8192]{1,0:T(8,128)S(1)}, bf16[32,8192]{1,0:T(8,128)(2,1)S(1)}, bf16[64,8192]{1,0:T(8,128)(2,1)S(1)}) custom-call(bf16[128,501]{1,0:T(8,128)(2,1)S(1)} %get-tuple-element.47.own_rest_ref, bf16[128,501]{1,0:T(8,128)(2,1)S(1)} %get-tuple-element.48.sib_rest_ref, bf16[501,8192]{1,0:T(8,128)(2,1)S(1)} %collective-permute-done.10.own_ref, ...), custom_call_target="tpu_custom_call" | custom-call | flops 2101346304 | bytes 20611072 | tf_op jit(solution)/shard_map/pallas_call | solution.py:39
  56.1 2.4 %collective-permute-start.12 = (bf16[64,8192]{1,0:T(8,128)(2,1)S(1)}, bf16[64,8192]{1,0:T(8,128)(2,1)S(1)}, u32[]{:S(2)}, u32[]{:S(2)}) collective-permute-start(bf16[64,8192]{1,0:T(8,128)(2,1)S(1)} %get-tuple-element.55), channel_id=1, source_target_pairs={{32,0},{136,8},{48,16},{152,24},{0,32},{168,40},{16,48},{184,56},{... | collective-permute-start | bytes 3145736 | tf_op jit(solution)/shard_map/ppermute | solution.py:76
  58.4 0.1 collective-permute-start.11
  58.6 2.5 %collective-permute-start.13 = (bf16[64,8192]{1,0:T(8,128)(2,1)S(1)}, bf16[64,8192]{1,0:T(8,128)(2,1)S(1)}, u32[]{:S(2)}, u32[]{:S(2)}) collective-permute-start(bf16[64,8192]{1,0:T(8,128)(2,1)S(1)} %get-tuple-element.56), channel_id=1, source_target_pairs={{16,0},{72,8},{32,16},{88,24},{48,32},{104,40},{0,48},{120,56},{80... | collective-permute-start | bytes 3145736 | tf_op jit(solution)/shard_map/ppermute | solution.py:76
  61.1 9.2 %all_to_all.21.got_ref = f32[8,8,128]{2,1,0:T(8,128)S(1)} all-to-all(f32[8,8,128]{2,1,0:T(8,128)S(1)} %get-tuple-element.50), channel_id=1, replica_groups=mesh['y'=4,'x'=4,'c'=2,'z'=8] {'z'}, dimensions={0} | all-to-all | bytes 65536 | tf_op jit(solution)/shard_map/all_to_all | solution.py:30
  70.4 12.8 %all_to_all.22.got_ref = f32[16,8,128]{2,1,0:T(8,128)S(1)} all-to-all(f32[16,8,128]{2,1,0:T(8,128)S(1)} %shard_map.92), channel_id=1, replica_groups=mesh['y'=4,'x'=4,'c'=2,'z'=8] {'y','x'}, dimensions={0} | all-to-all | bytes 131072 | tf_op jit(solution)/shard_map/all_to_all | solution.py:30
  83.1 0.2 shard_map.94
  83.4 6.5 %collective-permute-start.14 = (f32[8,128]{1,0:T(8,128)S(1)}, f32[8,128]{1,0:T(8,128)S(1)}, u32[]{:S(2)}, u32[]{:S(2)}) collective-permute-start(f32[8,128]{1,0:T(8,128)S(1)} %get-tuple-element.57.own_part_ref), channel_id=1, source_target_pairs={{0,8},{8,0},{1,9},{9,1},{2,10},{10,2},{3,11},{11,3},{4,12},{12,4},... | collective-permute-start | bytes 12296 | tf_op jit(solution)/shard_map/ppermute | solution.py:26
  89.9 0.0 collective-permute-done.12.refs_1_
  89.9 0.0 collective-permute-done.11.refs_0_
  89.9 0.0 collective-permute-done.13.refs_2_
  89.9 1.0 shard_map.93
  90.9 0.0 collective-permute-done.14.sib_part_ref
  90.9 20.6 %all_to_all.23.last_ref = bf16[32,8,1024]{2,1,0:T(8,128)(2,1)S(1)} all-to-all(bf16[32,8,1024]{2,1,0:T(8,128)(2,1)S(1)} %shard_map.93), channel_id=1, replica_groups={{0,1,2,3,4,5,6,7,64,65,66,67,68,69,70,71,128,129,130,131,132,133,134,13..., dimensions={0} | all-to-all | bytes 1048576 | tf_op jit(solution)/shard_map/all_to_all | solution.py:387
  111.5 0.7 shard_map.95
  (7 shorter events, 0.1 us)
Async XLA Ops:
  0.6 19.4 %collective-permute-start = (bf16[501,8192]{1,0:T(8,128)(2,1)}, bf16[501,8192]{1,0:T(8,128)(2,1)S(1)}, u32[]{:S(2)}, u32[]{:S(2)}) collective-permute-start(bf16[501,8192]{1,0:T(8,128)(2,1)} %param.9), channel_id=1, source_target_pairs={{0,8},{8,0},{1,9},{9,1},{2,10},{10,2},{3,11},{11,3},{4,12},{12,4},... | collective-permute-start | bytes 24625160 | tf_op jit(solution)/shard_map/ppermute | solution.py:26
  20.1 26.1 %collective-permute-start.10 = (bf16[501,8192]{1,0:T(8,128)(2,1)S(1)}, bf16[501,8192]{1,0:T(8,128)(2,1)S(1)}, u32[]{:S(2)}, u32[]{:S(2)}) collective-permute-start(bf16[501,8192]{1,0:T(8,128)(2,1)S(1)} %collective-permute-done.sib_ref), channel_id=1, source_target_pairs={{0,8},{8,0},{1,9},{9,1},{2,10},{10,2},{3,11},{11,3},{4,12},{12,4},... | collective-permute-start | bytes 24625160 | tf_op jit(solution)/shard_map/ppermute | solution.py:26
  21.7 7.8 %collective-permute-start.3 = (bf16[8,8192]{1,0:T(8,128)(2,1)S(1)}, bf16[8,8192]{1,0:T(8,128)(2,1)S(1)}, u32[]{:S(2)}, u32[]{:S(2)}) collective-permute-start(bf16[8,8192]{1,0:T(8,128)(2,1)S(1)} %get-tuple-element.37), channel_id=1, source_target_pairs={{192,0},{56,8},{208,16},{8,24},{224,32},{24,40},{240,48},{40,56},{... | collective-permute-start | bytes 393224 | tf_op jit(solution)/shard_map/ppermute | solution.py:76
  22.9 6.6 %collective-permute-start.2 = (bf16[8,8192]{1,0:T(8,128)(2,1)S(1)}, bf16[8,8192]{1,0:T(8,128)(2,1)S(1)}, u32[]{:S(2)}, u32[]{:S(2)}) collective-permute-start(bf16[8,8192]{1,0:T(8,128)(2,1)S(1)} %get-tuple-element.37), channel_id=1, source_target_pairs={{128,0},{40,8},{144,16},{56,24},{160,32},{8,40},{176,48},{24,56},{... | collective-permute-start | bytes 393224 | tf_op jit(solution)/shard_map/ppermute | solution.py:76
  25.3 4.1 %collective-permute-start.1 = (bf16[8,8192]{1,0:T(8,128)(2,1)S(1)}, bf16[8,8192]{1,0:T(8,128)(2,1)S(1)}, u32[]{:S(2)}, u32[]{:S(2)}) collective-permute-start(bf16[8,8192]{1,0:T(8,128)(2,1)S(1)} %get-tuple-element.37), channel_id=1, source_target_pairs={{64,0},{24,8},{80,16},{40,24},{96,32},{56,40},{112,48},{8,56},{128... | collective-permute-start | bytes 393224 | tf_op jit(solution)/shard_map/ppermute | solution.py:76
  29.6 6.9 %collective-permute-start.9 = (bf16[32,4096]{1,0:T(8,128)(2,1)S(1)}, bf16[32,4096]{1,0:T(8,128)(2,1)S(1)}, u32[]{:S(2)}, u32[]{:S(2)}) collective-permute-start(bf16[32,4096]{1,0:T(8,128)(2,1)S(1)} %get-tuple-element.66), channel_id=1, source_target_pairs={{48,0},{200,8},{0,16},{216,24},{16,32},{232,40},{32,48},{248,56},{... | collective-permute-start | bytes 786440 | tf_op jit(solution)/shard_map/ppermute | solution.py:76
  30.9 9.7 %collective-permute-start.8 = (bf16[32,4096]{1,0:T(8,128)(2,1)S(1)}, bf16[32,4096]{1,0:T(8,128)(2,1)S(1)}, u32[]{:S(2)}, u32[]{:S(2)}) collective-permute-start(bf16[32,4096]{1,0:T(8,128)(2,1)S(1)} %get-tuple-element.66), channel_id=1, source_target_pairs={{32,0},{136,8},{48,16},{152,24},{0,32},{168,40},{16,48},{184,56},{... | collective-permute-start | bytes 786440 | tf_op jit(solution)/shard_map/ppermute | solution.py:76
  33.5 7.0 %collective-permute-start.7 = (bf16[32,4096]{1,0:T(8,128)(2,1)S(1)}, bf16[32,4096]{1,0:T(8,128)(2,1)S(1)}, u32[]{:S(2)}, u32[]{:S(2)}) collective-permute-start(bf16[32,4096]{1,0:T(8,128)(2,1)S(1)} %get-tuple-element.66), channel_id=1, source_target_pairs={{16,0},{72,8},{32,16},{88,24},{48,32},{104,40},{0,48},{120,56},{80... | collective-permute-start | bytes 786440 | tf_op jit(solution)/shard_map/ppermute | solution.py:76
  34.6 8.6 %collective-permute-start.6 = (bf16[32,4096]{1,0:T(8,128)(2,1)S(1)}, bf16[32,4096]{1,0:T(8,128)(2,1)S(1)}, u32[]{:S(2)}, u32[]{:S(2)}) collective-permute-start(bf16[32,4096]{1,0:T(8,128)(2,1)S(1)} %get-tuple-element.67), channel_id=1, source_target_pairs={{48,0},{200,8},{0,16},{216,24},{16,32},{232,40},{32,48},{248,56},{... | collective-permute-start | bytes 786440 | tf_op jit(solution)/shard_map/ppermute | solution.py:76
  36.4 9.6 %collective-permute-start.5 = (bf16[32,4096]{1,0:T(8,128)(2,1)S(1)}, bf16[32,4096]{1,0:T(8,128)(2,1)S(1)}, u32[]{:S(2)}, u32[]{:S(2)}) collective-permute-start(bf16[32,4096]{1,0:T(8,128)(2,1)S(1)} %get-tuple-element.67), channel_id=1, source_target_pairs={{32,0},{136,8},{48,16},{152,24},{0,32},{168,40},{16,48},{184,56},{... | collective-permute-start | bytes 786440 | tf_op jit(solution)/shard_map/ppermute | solution.py:76
  40.6 5.5 %collective-permute-start.4 = (bf16[32,4096]{1,0:T(8,128)(2,1)S(1)}, bf16[32,4096]{1,0:T(8,128)(2,1)S(1)}, u32[]{:S(2)}, u32[]{:S(2)}) collective-permute-start(bf16[32,4096]{1,0:T(8,128)(2,1)S(1)} %get-tuple-element.67), channel_id=1, source_target_pairs={{16,0},{72,8},{32,16},{88,24},{48,32},{104,40},{0,48},{120,56},{80... | collective-permute-start | bytes 786440 | tf_op jit(solution)/shard_map/ppermute | solution.py:76
  56.1 33.8 %collective-permute-start.12 = (bf16[64,8192]{1,0:T(8,128)(2,1)S(1)}, bf16[64,8192]{1,0:T(8,128)(2,1)S(1)}, u32[]{:S(2)}, u32[]{:S(2)}) collective-permute-start(bf16[64,8192]{1,0:T(8,128)(2,1)S(1)} %get-tuple-element.55), channel_id=1, source_target_pairs={{32,0},{136,8},{48,16},{152,24},{0,32},{168,40},{16,48},{184,56},{... | collective-permute-start | bytes 3145736 | tf_op jit(solution)/shard_map/ppermute | solution.py:76
  58.4 31.5 %collective-permute-start.11 = (bf16[64,8192]{1,0:T(8,128)(2,1)S(1)}, bf16[64,8192]{1,0:T(8,128)(2,1)S(1)}, u32[]{:S(2)}, u32[]{:S(2)}) collective-permute-start(bf16[64,8192]{1,0:T(8,128)(2,1)S(1)} %get-tuple-element.54), channel_id=1, source_target_pairs={{48,0},{200,8},{0,16},{216,24},{16,32},{232,40},{32,48},{248,56},{... | collective-permute-start | bytes 3145736 | tf_op jit(solution)/shard_map/ppermute | solution.py:76
  58.6 31.3 %collective-permute-start.13 = (bf16[64,8192]{1,0:T(8,128)(2,1)S(1)}, bf16[64,8192]{1,0:T(8,128)(2,1)S(1)}, u32[]{:S(2)}, u32[]{:S(2)}) collective-permute-start(bf16[64,8192]{1,0:T(8,128)(2,1)S(1)} %get-tuple-element.56), channel_id=1, source_target_pairs={{16,0},{72,8},{32,16},{88,24},{48,32},{104,40},{0,48},{120,56},{80... | collective-permute-start | bytes 3145736 | tf_op jit(solution)/shard_map/ppermute | solution.py:76
  83.4 7.5 %collective-permute-start.14 = (f32[8,128]{1,0:T(8,128)S(1)}, f32[8,128]{1,0:T(8,128)S(1)}, u32[]{:S(2)}, u32[]{:S(2)}) collective-permute-start(f32[8,128]{1,0:T(8,128)S(1)} %get-tuple-element.57.own_part_ref), channel_id=1, source_target_pairs={{0,8},{8,0},{1,9},{9,1},{2,10},{10,2},{3,11},{11,3},{4,12},{12,4},... | collective-permute-start | bytes 12296 | tf_op jit(solution)/shard_map/ppermute | solution.py:26

commit v6 on v5

--- a/solution.py
+++ b/solution.py
@@ -51,16 +51,20 @@
     return lax.axis_index("y") * lax.axis_size("x") + lax.axis_index("x")
 
 
-def place_on(y, x, core):
-    return (jnp.where(core == 0, x, y), jnp.where(core == 0, y, x))
+def own_group():
+    return (lax.axis_index("c") + lax.axis_index("x") + lax.axis_index("y")) % 2
+
+
+def place_on(y, x, group):
+    return (jnp.where(group == 0, x, y), jnp.where(group == 0, y, x))
 
 
 def own_place():
-    return place_on(lax.axis_index("y"), lax.axis_index("x"), lax.axis_index("c"))
-
-
-def device(y, x, core):
-    return (y * SIDE + x) * 2 + core
+    return place_on(lax.axis_index("y"), lax.axis_index("x"), own_group())
+
+
+def device(y, x, group):
+    return (y * SIDE + x) * 2 + (group + x + y) % 2
 
 
 def from_ahead(value, step, outer):
@@ -168,7 +172,7 @@
     ) & 255
     source = lax.broadcasted_iota(jnp.int32, (count, core_rows), 0)
     place = lax.broadcasted_iota(jnp.int32, (count, core_rows), 1)
-    core = lax.axis_index("c")
+    core = own_group()
     x, y = place_on(place // rows % SIDE, place // (rows * SIDE), core)
     wanted = device(y, x, core) * rows + place % rows
     picked = jnp.dot(
@@ -205,25 +209,13 @@
     return lax.broadcasted_iota(jnp.int32, shape, 0) == places
 
 
-def first_logits_kernel(rows_ref, own_ref, sib_ref, own_logits_ref, sib_logits_ref):
-    width = rows_ref.shape[1]
+def logits_kernel(
+    n_z, rows_ref, own_ref, sib_ref, targets_ref, extra_ref,
+    own_logits_ref, sib_logits_ref, out_ref, top_ref, own_stats_ref,
+):
     for weight_ref, logits_ref in ((own_ref, own_logits_ref), (sib_ref, sib_logits_ref)):
         logits_ref[...] = lax.dot_general(
-            weight_ref[:, :width], rows_ref[...], CONTRACT_LAST, preferred_element_type=F32
-        )
-
-
-def logits_kernel(
-    n_z, rows_ref, own_first_ref, sib_first_ref, own_ref, sib_ref, targets_ref, extra_ref,
-    own_logits_ref, sib_logits_ref, out_ref, top_ref, own_stats_ref,
-):
-    width = rows_ref.shape[1]
-    for weight_ref, first_ref, logits_ref in (
-        (own_ref, own_first_ref, own_logits_ref),
-        (sib_ref, sib_first_ref, sib_logits_ref),
-    ):
-        logits_ref[...] = first_ref[...] + lax.dot_general(
-            weight_ref[:, width:], rows_ref[...], CONTRACT_LAST, preferred_element_type=F32
+            weight_ref[...], rows_ref[...], CONTRACT_LAST, preferred_element_type=F32
         )
     parts = [own_logits_ref[...], sib_logits_ref[...]]
     top = jnp.maximum(*[jnp.max(part, axis=0, keepdims=True) for part in parts])
@@ -328,7 +320,7 @@
     parts = out_ref.shape[0] // SIDE
     width = out_ref.shape[2]
     outer, inner = own_place()
-    core = lax.axis_index("c")
+    core = own_group()
     top, total, picked, _ = merged(got_ref)
     log_total = top + jnp.log(total)
     shape = got_ref.shape[1:]
@@ -374,6 +366,13 @@
     out_ref[...] = (LOSS_SCALE * input_grad).astype(out_ref.dtype)
 
 
+def along_plane(value):
+    groups = [
+        [device(y, x, group) for y in range(SIDE) for x in range(SIDE)] for group in range(2)
+    ]
+    return lax.all_to_all(value, CTX, 0, 0, axis_index_groups=groups, tiled=True)
+
+
 def along_inner_and_z(value, n_z):
     groups = [
         [
@@ -395,6 +394,7 @@
     n_plane = lax.axis_size(PLANE)
     n_z = lax.axis_size("z")
     half = tok_dev * n_plane
+    block = half // SIDE
     rows_in_all = targets.shape[0]
     flops = 4 * half * voc_dev * full_width
     moved = 4 * (voc_dev + half) * full_width
@@ -442,20 +442,7 @@
     own_weight = other_core(sib_weight)
     sib_weight = pltpu.with_memory_space_constraint(sib_weight, pltpu.VMEM)
     nearby = gather_from(normed, False)
-    first = gather_from(nearby[:, : full_width // 2], True)
-    rows = gather_from(nearby[:, full_width // 2 :], True)
-    own_weight = pltpu.with_memory_space_constraint(own_weight, pltpu.VMEM)
-    block = half // SIDE
-    first_logits = run(
-        first_logits_kernel,
-        [((voc_dev, half), F32)] * 2,
-        [],
-        first,
-        own_weight,
-        sib_weight,
-        flops=flops // 2,
-        moved=moved // 2,
-    )
+    rows = gather_from(nearby, True)
     own_logits, sib_logits, stats, tops, own_stats = run(
         functools.partial(logits_kernel, n_z),
         [
@@ -467,7 +454,6 @@
         ],
         [],
         rows,
-        *first_logits,
         own_weight,
         sib_weight,
         targets,
@@ -514,7 +500,7 @@
         own_stats,
         moved=1 << 17,
     )
-    got = exchange(stats, PLANE)
+    got = along_plane(stats)
     own_part, dots = run(
         totals_kernel, [((tok_dev, LANES), F32)] * 2, [], got, moved=1 << 17
     )

time: 113 us -> 109 us (0.965)
  starting transfers between devices: 30.9 us -> 21.1 us
  waiting for transfers between devices: 9.81 us -> 17 us
    all_to_all x0 -> x1, blocking collectives: none -> 14.9 us  [along_plane(): lax.all_to_all(value, CTX, 0, 0, axis_index_groups=groups, tiled=True)]
    all_to_all x3 -> x2, blocking collectives: 36.8 us -> 24.1 us  [exchange(): return lax.all_to_all(value, axes, 0, 0, tiled=True)]
    ppermute x12 -> x9, waiting for transfers between devices: 9.8 us -> 17 us  [from_ahead(): return lax.ppermute(value, CTX, pairs)]
    ppermute x12 -> x9, starting transfers between devices: 19.5 us -> 13 us  [from_ahead(): return lax.ppermute(value, CTX, pairs)]
    ppermute x3, starting transfers between devices: 11.4 us -> 8.17 us  [other_core(): return lax.ppermute(value, 'c', [(0, 1), (1, 0)])]
    all_to_all x1, blocking collectives: 20.6 us -> 17.9 us  [along_inner_and_z(): lax.all_to_all(value, CTX + ('z',), 0, 0, axis_index_groups=groups, tiled...]
    pallas_call x9 -> x8, Pallas kernels: 12.4 us -> 12.2 us  [run(): pl.pallas_call(kernel, in_specs=specs or [IN_VMEM] * len(operands), out_s...]
  transfers between devices with their start and end apart: 15 -> 12, of which waited for: 4 -> 4; matrix products, arithmetic and copies ran while one was open for 0% -> 0% of each run, Pallas kernels for 2% -> 2%
where the time goes in v6:
time: 109 us
  blocking collectives  56.9 us (52%)
  starting transfers between devices  21.1 us (19%)
  waiting for transfers between devices  17 us (16%)
  Pallas kernels  12.9 us (12%)
    all_to_all x2, blocking collectives, exchange(): return lax.all_to_all(value, axes, 0, 0, tiled=True)  24.1 us
    all_to_all x1, blocking collectives, along_inner_and_z(): lax.all_to_all(value, CTX + ('z',), 0, 0, axis_index_groups=groups, tiled...  17.9 us
    ppermute x9, waiting for transfers between devices, from_ahead(): return lax.ppermute(value, CTX, pairs)  17 us
    all_to_all x1, blocking collectives, along_plane(): lax.all_to_all(value, CTX, 0, 0, axis_index_groups=groups, tiled=True)  14.9 us
    ppermute x9, starting transfers between devices, from_ahead(): return lax.ppermute(value, CTX, pairs)  13 us
    pallas_call x8, Pallas kernels, run(): pl.pallas_call(kernel, in_specs=specs or [IN_VMEM] * len(operands), out_s...  12.2 us
    ppermute x3, starting transfers between devices, other_core(): return lax.ppermute(value, 'c', [(0, 1), (1, 0)])  8.17 us
  transfers between devices with their start and end apart: 12, of which 4 were waited for; matrix products, arithmetic and copies ran while one was open for 0% of the time, Pallas kernels for 2%

profile of v6, /device:TPU:1, one launch (start us, length us, event | category | flops | bytes accessed | tf_op | source)
XLA Modules:
  0.0 108.8 jit_solution(11696252583000492055)
XLA Ops:
  0.6 3.3 %collective-permute-start = (bf16[501,8192]{1,0:T(8,128)(2,1)}, bf16[501,8192]{1,0:T(8,128)(2,1)S(1)}, u32[]{:S(2)}, u32[]{:S(2)}) collective-permute-start(bf16[501,8192]{1,0:T(8,128)(2,1)} %param.9), channel_id=1, source_target_pairs={{0,8},{8,0},{1,9},{9,1},{2,10},{10,2},{3,11},{11,3},{4,12},{12,4},... | collective-permute-start | bytes 24625160 | tf_op jit(solution)/shard_map/ppermute | solution.py:26
  4.0 1.2 %shard_map.86 = (bf16[64,1024]{1,0:T(8,128)(2,1)S(1)}, f32[8,1024]{1,0:T(8,128)S(1)}, f32[1,8192]{1,0:T(1,128)S(1)}, s32[1,128]{1,0:T(1,128)S(1)}, f32[8,128]{1,0:T(8,128)S(1)}, /*index=5*/f32[8,128]{1,0:T(8,128)S(1)}) custom-call(bf16[8,1024]{1,0:T(8,128)(2,1)} %hidden_hbm.1, f32[1,8192]{1,0:T(1,128)} %bitcast.5, s32[1,256]{1,0:T(1,128)} %bitcast.6, ...), custom_call_target="tpu_custom_call" | custom-call | bytes 1048576 | tf_op jit(solution)/shard_map/pallas_call | solution.py:39
  5.1 14.8 %all_to_all.20 = bf16[8,8,1024]{2,1,0:T(8,128)(2,1)S(1)} all-to-all(bf16[8,8,1024]{2,1,0:T(8,128)(2,1)S(1)} %bitcast.4), channel_id=1, replica_groups=mesh['y'=4,'x'=4,'c'=2,'z'=8] {'z'}, dimensions={0} | all-to-all | bytes 262144 | tf_op jit(solution)/shard_map/all_to_all | solution.py:30
  19.9 0.1 shard_map.87
  20.1 0.0 collective-permute-done.sib_ref
  20.1 1.6 %collective-permute-start.7 = (bf16[501,8192]{1,0:T(8,128)(2,1)S(1)}, bf16[501,8192]{1,0:T(8,128)(2,1)S(1)}, u32[]{:S(2)}, u32[]{:S(2)}) collective-permute-start(bf16[501,8192]{1,0:T(8,128)(2,1)S(1)} %collective-permute-done.sib_ref), channel_id=1, source_target_pairs={{0,8},{8,0},{1,9},{9,1},{2,10},{10,2},{3,11},{11,3},{4,12},{12,4},... | collective-permute-start | bytes 24625160 | tf_op jit(solution)/shard_map/ppermute | solution.py:26
  21.7 1.2 %collective-permute-start.3 = (bf16[8,8192]{1,0:T(8,128)(2,1)S(1)}, bf16[8,8192]{1,0:T(8,128)(2,1)S(1)}, u32[]{:S(2)}, u32[]{:S(2)}) collective-permute-start(bf16[8,8192]{1,0:T(8,128)(2,1)S(1)} %get-tuple-element.35), channel_id=1, source_target_pairs={{200,0},{48,8},{208,24},{8,16},{232,32},{16,40},{240,56},{40,48},{... | collective-permute-start | bytes 393224 | tf_op jit(solution)/shard_map/ppermute | solution.py:80
  22.9 2.5 %collective-permute-start.2 = (bf16[8,8192]{1,0:T(8,128)(2,1)S(1)}, bf16[8,8192]{1,0:T(8,128)(2,1)S(1)}, u32[]{:S(2)}, u32[]{:S(2)}) collective-permute-start(bf16[8,8192]{1,0:T(8,128)(2,1)S(1)} %get-tuple-element.35), channel_id=1, source_target_pairs={{128,0},{40,8},{152,24},{48,16},{160,32},{8,40},{184,56},{16,48},{... | collective-permute-start | bytes 393224 | tf_op jit(solution)/shard_map/ppermute | solution.py:80
  25.3 1.7 %collective-permute-start.1 = (bf16[8,8192]{1,0:T(8,128)(2,1)S(1)}, bf16[8,8192]{1,0:T(8,128)(2,1)S(1)}, u32[]{:S(2)}, u32[]{:S(2)}) collective-permute-start(bf16[8,8192]{1,0:T(8,128)(2,1)S(1)} %get-tuple-element.35), channel_id=1, source_target_pairs={{72,0},{16,8},{80,24},{40,16},{104,32},{48,40},{112,56},{8,48},{12... | collective-permute-start | bytes 393224 | tf_op jit(solution)/shard_map/ppermute | solution.py:80
  27.1 2.9 %collective-permute-done.1 = bf16[8,8192]{1,0:T(8,128)(2,1)S(1)} collective-permute-done((bf16[8,8192]{1,0:T(8,128)(2,1)S(1)}, bf16[8,8192]{1,0:T(8,128)(2,1)S(1)}, u32[]{:S(2)}, u32[]{:S(2)}) %collective-permute-start.1) | collective-permute-done | bytes 131104 | tf_op jit(solution)/shard_map/ppermute | solution.py:80
  30.0 0.0 collective-permute-done.2
  30.1 0.0 collective-permute-done.3
  30.1 3.1 %collective-permute-start.4 = (bf16[32,8192]{1,0:T(8,128)(2,1)S(1)}, bf16[32,8192]{1,0:T(8,128)(2,1)S(1)}, u32[]{:S(2)}, u32[]{:S(2)}) collective-permute-start(bf16[32,8192]{1,0:T(8,128)(2,1)S(1)} %get-tuple-element.62), channel_id=1, source_target_pairs={{24,0},{64,8},{32,24},{88,16},{56,32},{96,40},{0,56},{120,48},{80,... | collective-permute-start | bytes 1572872 | tf_op jit(solution)/shard_map/ppermute | solution.py:80
  33.2 0.0 collective-permute-start.6
  33.2 1.3 %collective-permute-start.5 = (bf16[32,8192]{1,0:T(8,128)(2,1)S(1)}, bf16[32,8192]{1,0:T(8,128)(2,1)S(1)}, u32[]{:S(2)}, u32[]{:S(2)}) collective-permute-start(bf16[32,8192]{1,0:T(8,128)(2,1)S(1)} %get-tuple-element.62), channel_id=1, source_target_pairs={{32,0},{136,8},{56,24},{144,16},{0,32},{168,40},{24,56},{176,48},{... | collective-permute-start | bytes 1572872 | tf_op jit(solution)/shard_map/ppermute | solution.py:80
  34.5 10.4 %collective-permute-done.4 = bf16[32,8192]{1,0:T(8,128)(2,1)S(1)} collective-permute-done((bf16[32,8192]{1,0:T(8,128)(2,1)S(1)}, bf16[32,8192]{1,0:T(8,128)(2,1)S(1)}, u32[]{:S(2)}, u32[]{:S(2)}) %collective-permute-start.4) | collective-permute-done | bytes 524320 | tf_op jit(solution)/shard_map/ppermute | solution.py:80
  45.0 2.1 %collective-permute-done.5 = bf16[32,8192]{1,0:T(8,128)(2,1)S(1)} collective-permute-done((bf16[32,8192]{1,0:T(8,128)(2,1)S(1)}, bf16[32,8192]{1,0:T(8,128)(2,1)S(1)}, u32[]{:S(2)}, u32[]{:S(2)}) %collective-permute-start.5) | collective-permute-done | bytes 524320 | tf_op jit(solution)/shard_map/ppermute | solution.py:80
  47.1 1.5 %collective-permute-done.6 = bf16[32,8192]{1,0:T(8,128)(2,1)S(1)} collective-permute-done((bf16[32,8192]{1,0:T(8,128)(2,1)S(1)}, bf16[32,8192]{1,0:T(8,128)(2,1)S(1)}, u32[]{:S(2)}, u32[]{:S(2)}) %collective-permute-start.6) | collective-permute-done | bytes 524320 | tf_op jit(solution)/shard_map/ppermute | solution.py:80
  48.7 0.0 collective-permute-done.7.own_ref
  48.7 4.8 %shard_map.88 = (f32[501,128]{1,0:T(8,128)S(1)}, f32[501,128]{1,0:T(8,128)S(1)}, f32[8,8,128]{2,1,0:T(8,128)S(1)}, f32[8,128]{1,0:T(8,128)S(1)}, f32[8,128]{1,0:T(8,128)S(1)}) custom-call(bf16[128,8192]{1,0:T(8,128)(2,1)S(1)} %constant_dynamic-update-slice_fusion.4.rows_ref, bf16[501,8192]{1,0:T(8,128)(2,1)S(1)} %collective-permute-done.7.own_ref, ...), custom_call_target="tpu_custom_call" | custom-call | flops 2101346304 | bytes 20611072 | tf_op jit(solution)/shard_map/pallas_call | solution.py:39
  53.5 2.5 %shard_map.89 = (bf16[64,8192]{1,0:T(8,128)(2,1)S(1)}, bf16[64,8192]{1,0:T(8,128)(2,1)S(1)}, bf16[128,501]{1,0:T(8,128)(2,1)S(1)}, bf16[128,501]{1,0:T(8,128)(2,1)S(1)}) custom-call(f32[501,128]{1,0:T(8,128)S(1)} %get-tuple-element.40.own_logits_ref, f32[501,128]{1,0:T(8,128)S(1)} %get-tuple-element.41.sib_logits_ref, ...), custom_call_target="tpu_custom_call" | custom-call | flops 2101346304 | bytes 20611072 | tf_op jit(solution)/shard_map/pallas_call | solution.py:39
  56.0 2.4 %shard_map.90 = (f32[32,8192]{1,0:T(8,128)S(1)}, bf16[32,8192]{1,0:T(8,128)(2,1)S(1)}, bf16[64,8192]{1,0:T(8,128)(2,1)S(1)}) custom-call(bf16[128,501]{1,0:T(8,128)(2,1)S(1)} %get-tuple-element.43.own_rest_ref, bf16[128,501]{1,0:T(8,128)(2,1)S(1)} %get-tuple-element.44.sib_rest_ref, bf16[501,8192]{1,0:T(8,128)(2,1)S(1)} %collective-permute-done.7.own_ref, ...), custom_call_target="tpu_custom_call" | custom-call | flops 2101346304 | bytes 20611072 | tf_op jit(solution)/shard_map/pallas_call | solution.py:39
  58.3 0.2 collective-permute-start.9
  58.5 0.9 collective-permute-start.8
  59.4 2.1 %collective-permute-start.10 = (bf16[64,8192]{1,0:T(8,128)(2,1)S(1)}, bf16[64,8192]{1,0:T(8,128)(2,1)S(1)}, u32[]{:S(2)}, u32[]{:S(2)}) collective-permute-start(bf16[64,8192]{1,0:T(8,128)(2,1)S(1)} %get-tuple-element.52), channel_id=1, source_target_pairs={{24,0},{64,8},{32,24},{88,16},{56,32},{96,40},{0,56},{120,48},{80,... | collective-permute-start | bytes 3145736 | tf_op jit(solution)/shard_map/ppermute | solution.py:80
  61.5 9.3 %all_to_all.21.got_ref = f32[8,8,128]{2,1,0:T(8,128)S(1)} all-to-all(f32[8,8,128]{2,1,0:T(8,128)S(1)} %get-tuple-element.46), channel_id=1, replica_groups=mesh['y'=4,'x'=4,'c'=2,'z'=8] {'z'}, dimensions={0} | all-to-all | bytes 65536 | tf_op jit(solution)/shard_map/all_to_all | solution.py:30
  70.8 14.9 %all_to_all.22.got_ref = f32[16,8,128]{2,1,0:T(8,128)S(1)} all-to-all(f32[16,8,128]{2,1,0:T(8,128)S(1)} %shard_map.91), channel_id=1, replica_groups={{0,24,32,56,72,80,104,112,128,152,160,184,200,208,232,240},{8,16,40,48,..., dimensions={0} | all-to-all | bytes 131072 | tf_op jit(solution)/shard_map/all_to_all | solution.py:373
  85.7 0.2 shard_map.93
  85.9 3.2 %collective-permute-start.11 = (f32[8,128]{1,0:T(8,128)S(1)}, f32[8,128]{1,0:T(8,128)S(1)}, u32[]{:S(2)}, u32[]{:S(2)}) collective-permute-start(f32[8,128]{1,0:T(8,128)S(1)} %get-tuple-element.53.own_part_ref), channel_id=1, source_target_pairs={{0,8},{8,0},{1,9},{9,1},{2,10},{10,2},{3,11},{11,3},{4,12},{12,4},... | collective-permute-start | bytes 12296 | tf_op jit(solution)/shard_map/ppermute | solution.py:26
  89.2 0.0 collective-permute-done.9.refs_1_
  89.2 0.0 collective-permute-done.8.refs_0_
  89.2 0.0 collective-permute-done.10.refs_2_
  89.2 1.0 shard_map.92
  90.2 0.0 collective-permute-done.11.sib_part_ref
  90.2 17.9 %all_to_all.23.last_ref = bf16[32,8,1024]{2,1,0:T(8,128)(2,1)S(1)} all-to-all(bf16[32,8,1024]{2,1,0:T(8,128)(2,1)S(1)} %shard_map.92), channel_id=1, replica_groups={{0,1,2,3,4,5,6,7,72,73,74,75,76,77,78,79,128,129,130,131,132,133,134,13..., dimensions={0} | all-to-all | bytes 1048576 | tf_op jit(solution)/shard_map/all_to_all | solution.py:386
  108.1 0.7 shard_map.94
  (9 shorter events, 0.2 us)
Async XLA Ops:
  0.6 19.4 %collective-permute-start = (bf16[501,8192]{1,0:T(8,128)(2,1)}, bf16[501,8192]{1,0:T(8,128)(2,1)S(1)}, u32[]{:S(2)}, u32[]{:S(2)}) collective-permute-start(bf16[501,8192]{1,0:T(8,128)(2,1)} %param.9), channel_id=1, source_target_pairs={{0,8},{8,0},{1,9},{9,1},{2,10},{10,2},{3,11},{11,3},{4,12},{12,4},... | collective-permute-start | bytes 24625160 | tf_op jit(solution)/shard_map/ppermute | solution.py:26
  20.1 28.6 %collective-permute-start.7 = (bf16[501,8192]{1,0:T(8,128)(2,1)S(1)}, bf16[501,8192]{1,0:T(8,128)(2,1)S(1)}, u32[]{:S(2)}, u32[]{:S(2)}) collective-permute-start(bf16[501,8192]{1,0:T(8,128)(2,1)S(1)} %collective-permute-done.sib_ref), channel_id=1, source_target_pairs={{0,8},{8,0},{1,9},{9,1},{2,10},{10,2},{3,11},{11,3},{4,12},{12,4},... | collective-permute-start | bytes 24625160 | tf_op jit(solution)/shard_map/ppermute | solution.py:26
  21.7 8.4 %collective-permute-start.3 = (bf16[8,8192]{1,0:T(8,128)(2,1)S(1)}, bf16[8,8192]{1,0:T(8,128)(2,1)S(1)}, u32[]{:S(2)}, u32[]{:S(2)}) collective-permute-start(bf16[8,8192]{1,0:T(8,128)(2,1)S(1)} %get-tuple-element.35), channel_id=1, source_target_pairs={{200,0},{48,8},{208,24},{8,16},{232,32},{16,40},{240,56},{40,48},{... | collective-permute-start | bytes 393224 | tf_op jit(solution)/shard_map/ppermute | solution.py:80
  22.9 7.2 %collective-permute-start.2 = (bf16[8,8192]{1,0:T(8,128)(2,1)S(1)}, bf16[8,8192]{1,0:T(8,128)(2,1)S(1)}, u32[]{:S(2)}, u32[]{:S(2)}) collective-permute-start(bf16[8,8192]{1,0:T(8,128)(2,1)S(1)} %get-tuple-element.35), channel_id=1, source_target_pairs={{128,0},{40,8},{152,24},{48,16},{160,32},{8,40},{184,56},{16,48},{... | collective-permute-start | bytes 393224 | tf_op jit(solution)/shard_map/ppermute | solution.py:80
  25.3 4.7 %collective-permute-start.1 = (bf16[8,8192]{1,0:T(8,128)(2,1)S(1)}, bf16[8,8192]{1,0:T(8,128)(2,1)S(1)}, u32[]{:S(2)}, u32[]{:S(2)}) collective-permute-start(bf16[8,8192]{1,0:T(8,128)(2,1)S(1)} %get-tuple-element.35), channel_id=1, source_target_pairs={{72,0},{16,8},{80,24},{40,16},{104,32},{48,40},{112,56},{8,48},{12... | collective-permute-start | bytes 393224 | tf_op jit(solution)/shard_map/ppermute | solution.py:80
  30.1 14.8 %collective-permute-start.4 = (bf16[32,8192]{1,0:T(8,128)(2,1)S(1)}, bf16[32,8192]{1,0:T(8,128)(2,1)S(1)}, u32[]{:S(2)}, u32[]{:S(2)}) collective-permute-start(bf16[32,8192]{1,0:T(8,128)(2,1)S(1)} %get-tuple-element.62), channel_id=1, source_target_pairs={{24,0},{64,8},{32,24},{88,16},{56,32},{96,40},{0,56},{120,48},{80,... | collective-permute-start | bytes 1572872 | tf_op jit(solution)/shard_map/ppermute | solution.py:80
  33.2 15.4 %collective-permute-start.6 = (bf16[32,8192]{1,0:T(8,128)(2,1)S(1)}, bf16[32,8192]{1,0:T(8,128)(2,1)S(1)}, u32[]{:S(2)}, u32[]{:S(2)}) collective-permute-start(bf16[32,8192]{1,0:T(8,128)(2,1)S(1)} %get-tuple-element.62), channel_id=1, source_target_pairs={{56,0},{192,8},{0,24},{216,16},{24,32},{224,40},{32,56},{248,48},{... | collective-permute-start | bytes 1572872 | tf_op jit(solution)/shard_map/ppermute | solution.py:80
  33.2 13.9 %collective-permute-start.5 = (bf16[32,8192]{1,0:T(8,128)(2,1)S(1)}, bf16[32,8192]{1,0:T(8,128)(2,1)S(1)}, u32[]{:S(2)}, u32[]{:S(2)}) collective-permute-start(bf16[32,8192]{1,0:T(8,128)(2,1)S(1)} %get-tuple-element.62), channel_id=1, source_target_pairs={{32,0},{136,8},{56,24},{144,16},{0,32},{168,40},{24,56},{176,48},{... | collective-permute-start | bytes 1572872 | tf_op jit(solution)/shard_map/ppermute | solution.py:80
  58.3 30.8 %collective-permute-start.9 = (bf16[64,8192]{1,0:T(8,128)(2,1)S(1)}, bf16[64,8192]{1,0:T(8,128)(2,1)S(1)}, u32[]{:S(2)}, u32[]{:S(2)}) collective-permute-start(bf16[64,8192]{1,0:T(8,128)(2,1)S(1)} %get-tuple-element.51), channel_id=1, source_target_pairs={{32,0},{136,8},{56,24},{144,16},{0,32},{168,40},{24,56},{176,48},{... | collective-permute-start | bytes 3145736 | tf_op jit(solution)/shard_map/ppermute | solution.py:80
  58.5 30.7 %collective-permute-start.8 = (bf16[64,8192]{1,0:T(8,128)(2,1)S(1)}, bf16[64,8192]{1,0:T(8,128)(2,1)S(1)}, u32[]{:S(2)}, u32[]{:S(2)}) collective-permute-start(bf16[64,8192]{1,0:T(8,128)(2,1)S(1)} %get-tuple-element.50), channel_id=1, source_target_pairs={{56,0},{192,8},{0,24},{216,16},{24,32},{224,40},{32,56},{248,48},{... | collective-permute-start | bytes 3145736 | tf_op jit(solution)/shard_map/ppermute | solution.py:80
  59.4 29.8 %collective-permute-start.10 = (bf16[64,8192]{1,0:T(8,128)(2,1)S(1)}, bf16[64,8192]{1,0:T(8,128)(2,1)S(1)}, u32[]{:S(2)}, u32[]{:S(2)}) collective-permute-start(bf16[64,8192]{1,0:T(8,128)(2,1)S(1)} %get-tuple-element.52), channel_id=1, source_target_pairs={{24,0},{64,8},{32,24},{88,16},{56,32},{96,40},{0,56},{120,48},{80,... | collective-permute-start | bytes 3145736 | tf_op jit(solution)/shard_map/ppermute | solution.py:80
  85.9 4.3 %collective-permute-start.11 = (f32[8,128]{1,0:T(8,128)S(1)}, f32[8,128]{1,0:T(8,128)S(1)}, u32[]{:S(2)}, u32[]{:S(2)}) collective-permute-start(f32[8,128]{1,0:T(8,128)S(1)} %get-tuple-element.53.own_part_ref), channel_id=1, source_target_pairs={{0,8},{8,0},{1,9},{9,1},{2,10},{10,2},{3,11},{11,3},{4,12},{12,4},... | collective-permute-start | bytes 12296 | tf_op jit(solution)/shard_map/ppermute | solution.py:26

commit v7 on v6

--- a/solution.py
+++ b/solution.py
@@ -268,12 +268,15 @@
     )
 
 
-def rest_kernel(own_rest_ref, sib_rest_ref, own_ref, sib_ref, own_power_ref, own_hot_ref, far_ref):
+def rest_kernel(
+    own_rest_ref, sib_rest_ref, own_ref, sib_ref, own_power_ref, own_hot_ref, far_power_ref, far_hot_ref
+):
     size = own_power_ref.shape[0]
     sums = products((own_rest_ref, sib_rest_ref), (own_ref, sib_ref))
     own_power_ref[...] = sums[:size]
     own_hot_ref[...] = sums[size : 2 * size].astype(BF16)
-    far_ref[...] = sums[2 * size :].astype(BF16)
+    far_power_ref[...] = sums[2 * size : 3 * size].astype(BF16)
+    far_hot_ref[...] = sums[3 * size :].astype(BF16)
 
 
 def merged(got_ref):
@@ -313,8 +316,10 @@
     dots_ref[...] = columns_of(by_distance(dots, rows)[0:1, :], rows)
 
 
-def outer_kernel(got_ref, own_power_ref, own_hot_ref, *refs):
-    blocks, (out_ref, scale_ref, total_ref) = refs[: SIDE - 1], refs[SIDE - 1 :]
+def outer_kernel(
+    got_ref, own_power_ref, own_hot_ref, ahead_ref, far_power_ref, far_hot_ref, behind_ref,
+    out_ref, scale_ref, total_ref,
+):
     size = own_power_ref.shape[0]
     rows = size // SIDE
     parts = out_ref.shape[0] // SIDE
@@ -335,9 +340,11 @@
             columns = slice(z * width + j * LANES, z * width + (j + 1) * LANES)
             power = scale_ref[0] * own_power_ref[:, columns]
             hot = own_hot_ref[:, columns].astype(F32)
-            for k in range(1, SIDE):
-                power += scale_ref[k] * blocks[k - 1][:size, columns].astype(F32)
-                hot += blocks[k - 1][size:, columns].astype(F32)
+            for k, block_ref in ((1, ahead_ref), (3, behind_ref)):
+                power += scale_ref[k] * block_ref[:size, columns].astype(F32)
+                hot += block_ref[size:, columns].astype(F32)
+            power += scale_ref[2] * far_power_ref[:, columns].astype(F32)
+            hot += far_hot_ref[:, columns].astype(F32)
             total_ref[:, j * LANES : (j + 1) * LANES] = scale_ref[SIDE] * hot - power
         for m in range(SIDE):
             term = total_ref[m * rows : (m + 1) * rows, :]
@@ -442,7 +449,16 @@
     own_weight = other_core(sib_weight)
     sib_weight = pltpu.with_memory_space_constraint(sib_weight, pltpu.VMEM)
     nearby = gather_from(normed, False)
-    rows = gather_from(nearby, True)
+    rows = jnp.concatenate(
+        [
+            nearby,
+            from_ahead(nearby, 1, True),
+            from_ahead(nearby[: block // 2], 2, True),
+            from_ahead(nearby[block // 2 :], 2, True),
+            from_ahead(nearby, 3, True),
+        ],
+        axis=0,
+    )
     own_logits, sib_logits, stats, tops, own_stats = run(
         functools.partial(logits_kernel, n_z),
         [
@@ -475,13 +491,9 @@
         moved=moved,
     )
     ahead, behind = from_ahead(ahead, 3, True), from_ahead(behind, 1, True)
-    own_power, own_hot, far = run(
+    own_power, own_hot, far_power, far_hot = run(
         rest_kernel,
-        [
-            ((block, full_width), F32),
-            ((block, full_width), BF16),
-            ((2 * block, full_width), BF16),
-        ],
+        [((block, full_width), F32)] + [((block, full_width), BF16)] * 3,
         [],
         own_rest,
         sib_rest,
@@ -490,8 +502,8 @@
         flops=flops,
         moved=moved,
     )
-    stats, far = lax.optimization_barrier((stats, far))
-    blocks = [ahead, from_ahead(far, 2, True), behind]
+    stats, far_power, far_hot = lax.optimization_barrier((stats, far_power, far_hot))
+    far_power, far_hot = [from_ahead(far, 2, True) for far in (far_power, far_hot)]
     (stats,) = run(
         merge_kernel,
         [((n_plane, STAT_ROWS, half), F32)],
@@ -512,7 +524,10 @@
         got,
         own_power,
         own_hot,
-        *blocks,
+        ahead,
+        far_power,
+        far_hot,
+        behind,
         moved=8 * half * full_width,
     )
     last, sib_part = lax.optimization_barrier((last, sib_part))

time: 109 us -> 108 us (level)
  waiting for transfers between devices: 17 us -> 12.5 us
  starting transfers between devices: 21.1 us -> 23.3 us
    ppermute x9 -> x11, starting transfers between devices: 13 us -> 17.9 us  [from_ahead(): return lax.ppermute(value, CTX, pairs)]
    ppermute x9 -> x11, waiting for transfers between devices: 17 us -> 12.4 us  [from_ahead(): return lax.ppermute(value, CTX, pairs)]
    ppermute x3, starting transfers between devices: 8.17 us -> 5.39 us  [other_core(): return lax.ppermute(value, 'c', [(0, 1), (1, 0)])]
    all_to_all x1, blocking collectives: 17.9 us -> 19.8 us  [along_inner_and_z(): lax.all_to_all(value, CTX + ('z',), 0, 0, axis_index_groups=groups, tiled...]
  transfers between devices with their start and end apart: 12 -> 14, of which waited for: 4 -> 3; matrix products, arithmetic and copies ran while one was open for 0% -> 0% of each run, Pallas kernels for 2% -> 5%
where the time goes in v7:
time: 108 us; the launch traced here: 107 us
  blocking collectives  57.7 us (53%)
  starting transfers between devices  23.3 us (22%)
  Pallas kernels  12.9 us (12%)
  waiting for transfers between devices  12.5 us (12%)
    all_to_all x2, blocking collectives, exchange(): return lax.all_to_all(value, axes, 0, 0, tiled=True)  24.1 us
    all_to_all x1, blocking collectives, along_inner_and_z(): lax.all_to_all(value, CTX + ('z',), 0, 0, axis_index_groups=groups, tiled...  19.8 us
    ppermute x11, starting transfers between devices, from_ahead(): return lax.ppermute(value, CTX, pairs)  17.9 us
    all_to_all x1, blocking collectives, along_plane(): lax.all_to_all(value, CTX, 0, 0, axis_index_groups=groups, tiled=True)  13.8 us
    ppermute x11, waiting for transfers between devices, from_ahead(): return lax.ppermute(value, CTX, pairs)  12.4 us
    pallas_call x8, Pallas kernels, run(): pl.pallas_call(kernel, in_specs=specs or [IN_VMEM] * len(operands), out_s...  12.2 us
    ppermute x3, starting transfers between devices, other_core(): return lax.ppermute(value, 'c', [(0, 1), (1, 0)])  5.39 us
  transfers between devices with their start and end apart: 14, of which 3 were waited for; matrix products, arithmetic and copies ran while one was open for 0% of the time, Pallas kernels for 5%

profile of v7, /device:TPU:1, one launch (start us, length us, event | category | flops | bytes accessed | tf_op | source)
XLA Modules:
  0.0 107.4 jit_solution(14347506888068565201)
XLA Ops:
  0.6 3.3 %collective-permute-start = (bf16[501,8192]{1,0:T(8,128)(2,1)}, bf16[501,8192]{1,0:T(8,128)(2,1)S(1)}, u32[]{:S(2)}, u32[]{:S(2)}) collective-permute-start(bf16[501,8192]{1,0:T(8,128)(2,1)} %param.9), channel_id=1, source_target_pairs={{0,8},{8,0},{1,9},{9,1},{2,10},{10,2},{3,11},{11,3},{4,12},{12,4},... | collective-permute-start | bytes 24625160 | tf_op jit(solution)/shard_map/ppermute | solution.py:26
  4.0 1.2 %shard_map.86 = (bf16[64,1024]{1,0:T(8,128)(2,1)S(1)}, f32[8,1024]{1,0:T(8,128)S(1)}, f32[1,8192]{1,0:T(1,128)S(1)}, s32[1,128]{1,0:T(1,128)S(1)}, f32[8,128]{1,0:T(8,128)S(1)}, /*index=5*/f32[8,128]{1,0:T(8,128)S(1)}) custom-call(bf16[8,1024]{1,0:T(8,128)(2,1)} %hidden_hbm.1, f32[1,8192]{1,0:T(1,128)} %bitcast.5, s32[1,256]{1,0:T(1,128)} %bitcast.6, ...), custom_call_target="tpu_custom_call" | custom-call | bytes 1048576 | tf_op jit(solution)/shard_map/pallas_call | solution.py:39
  5.1 14.8 %all_to_all.20 = bf16[8,8,1024]{2,1,0:T(8,128)(2,1)S(1)} all-to-all(bf16[8,8,1024]{2,1,0:T(8,128)(2,1)S(1)} %bitcast.4), channel_id=1, replica_groups=mesh['y'=4,'x'=4,'c'=2,'z'=8] {'z'}, dimensions={0} | all-to-all | bytes 262144 | tf_op jit(solution)/shard_map/all_to_all | solution.py:30
  19.9 0.1 shard_map.87
  20.1 0.0 collective-permute-done.sib_ref
  20.1 2.7 %collective-permute-start.3 = (bf16[8,8192]{1,0:T(8,128)(2,1)S(1)}, bf16[8,8192]{1,0:T(8,128)(2,1)S(1)}, u32[]{:S(2)}, u32[]{:S(2)}) collective-permute-start(bf16[8,8192]{1,0:T(8,128)(2,1)S(1)} %get-tuple-element.37), channel_id=1, source_target_pairs={{200,0},{48,8},{208,24},{8,16},{232,32},{16,40},{240,56},{40,48},{... | collective-permute-start | bytes 393224 | tf_op jit(solution)/shard_map/ppermute | solution.py:80
  22.8 2.5 %collective-permute-start.2 = (bf16[8,8192]{1,0:T(8,128)(2,1)S(1)}, bf16[8,8192]{1,0:T(8,128)(2,1)S(1)}, u32[]{:S(2)}, u32[]{:S(2)}) collective-permute-start(bf16[8,8192]{1,0:T(8,128)(2,1)S(1)} %get-tuple-element.37), channel_id=1, source_target_pairs={{128,0},{40,8},{152,24},{48,16},{160,32},{8,40},{184,56},{16,48},{... | collective-permute-start | bytes 393224 | tf_op jit(solution)/shard_map/ppermute | solution.py:80
  25.2 0.3 collective-permute-start.1
  25.5 1.4 %collective-permute-start.8 = (bf16[501,8192]{1,0:T(8,128)(2,1)S(1)}, bf16[501,8192]{1,0:T(8,128)(2,1)S(1)}, u32[]{:S(2)}, u32[]{:S(2)}) collective-permute-start(bf16[501,8192]{1,0:T(8,128)(2,1)S(1)} %collective-permute-done.sib_ref), channel_id=1, source_target_pairs={{0,8},{8,0},{1,9},{9,1},{2,10},{10,2},{3,11},{11,3},{4,12},{12,4},... | collective-permute-start | bytes 24625160 | tf_op jit(solution)/shard_map/ppermute | solution.py:26
  26.9 2.7 %collective-permute-done.1 = bf16[8,8192]{1,0:T(8,128)(2,1)S(1)} collective-permute-done((bf16[8,8192]{1,0:T(8,128)(2,1)S(1)}, bf16[8,8192]{1,0:T(8,128)(2,1)S(1)}, u32[]{:S(2)}, u32[]{:S(2)}) %collective-permute-start.1) | collective-permute-done | bytes 131104 | tf_op jit(solution)/shard_map/ppermute | solution.py:80
  29.6 0.0 collective-permute-done.2
  29.7 0.0 collective-permute-done.3
  29.7 0.9 collective-permute-start.7
  30.6 2.1 %collective-permute-start.4 = (bf16[32,8192]{1,0:T(8,128)(2,1)S(1)}, bf16[32,8192]{1,0:T(8,128)(2,1)S(1)}, u32[]{:S(2)}, u32[]{:S(2)}) collective-permute-start(bf16[32,8192]{1,0:T(8,128)(2,1)S(1)} %get-tuple-element.66), channel_id=1, source_target_pairs={{24,0},{64,8},{32,24},{88,16},{56,32},{96,40},{0,56},{120,48},{80,... | collective-permute-start | bytes 1572872 | tf_op jit(solution)/shard_map/ppermute | solution.py:80
  32.8 1.8 %collective-permute-start.6 = (bf16[16,8192]{1,0:T(8,128)(2,1)S(1)}, bf16[16,8192]{1,0:T(8,128)(2,1)S(1)}, u32[]{:S(2)}, u32[]{:S(2)}) collective-permute-start(bf16[16,8192]{1,0:T(8,128)(2,1)S(1)} %pad_maximum_fusion.1), channel_id=1, source_target_pairs={{32,0},{136,8},{56,24},{144,16},{0,32},{168,40},{24,56},{176,48},{... | collective-permute-start | bytes 786440 | tf_op jit(solution)/shard_map/ppermute | solution.py:80
  34.6 1.4 %collective-permute-start.5 = (bf16[16,8192]{1,0:T(8,128)(2,1)S(1)}, bf16[16,8192]{1,0:T(8,128)(2,1)S(1)}, u32[]{:S(2)}, u32[]{:S(2)}) collective-permute-start(bf16[16,8192]{1,0:T(8,128)(2,1)S(1)} %pad_maximum_fusion), channel_id=1, source_target_pairs={{32,0},{136,8},{56,24},{144,16},{0,32},{168,40},{24,56},{176,48},{... | collective-permute-start | bytes 786440 | tf_op jit(solution)/shard_map/ppermute | solution.py:80
  35.9 3.9 %collective-permute-done.4 = bf16[32,8192]{1,0:T(8,128)(2,1)S(1)} collective-permute-done((bf16[32,8192]{1,0:T(8,128)(2,1)S(1)}, bf16[32,8192]{1,0:T(8,128)(2,1)S(1)}, u32[]{:S(2)}, u32[]{:S(2)}) %collective-permute-start.4) | collective-permute-done | bytes 524320 | tf_op jit(solution)/shard_map/ppermute | solution.py:80
  39.8 5.9 %collective-permute-done.5 = bf16[16,8192]{1,0:T(8,128)(2,1)S(1)} collective-permute-done((bf16[16,8192]{1,0:T(8,128)(2,1)S(1)}, bf16[16,8192]{1,0:T(8,128)(2,1)S(1)}, u32[]{:S(2)}, u32[]{:S(2)}) %collective-permute-start.5) | collective-permute-done | bytes 262176 | tf_op jit(solution)/shard_map/ppermute | solution.py:80
  45.8 0.0 collective-permute-done.6
  45.8 0.0 collective-permute-done.7
  45.8 0.0 collective-permute-done.8.own_ref
  45.9 4.8 %shard_map.88 = (f32[501,128]{1,0:T(8,128)S(1)}, f32[501,128]{1,0:T(8,128)S(1)}, f32[8,8,128]{2,1,0:T(8,128)S(1)}, f32[8,128]{1,0:T(8,128)S(1)}, f32[8,128]{1,0:T(8,128)S(1)}) custom-call(bf16[128,8192]{1,0:T(8,128)(2,1)S(1)} %constant_dynamic-update-slice_fusion.4.rows_ref, bf16[501,8192]{1,0:T(8,128)(2,1)S(1)} %collective-permute-done.8.own_ref, ...), custom_call_target="tpu_custom_call" | custom-call | flops 2101346304 | bytes 20611072 | tf_op jit(solution)/shard_map/pallas_call | solution.py:39
  50.7 2.5 %shard_map.89 = (bf16[64,8192]{1,0:T(8,128)(2,1)S(1)}, bf16[64,8192]{1,0:T(8,128)(2,1)S(1)}, bf16[128,501]{1,0:T(8,128)(2,1)S(1)}, bf16[128,501]{1,0:T(8,128)(2,1)S(1)}) custom-call(f32[501,128]{1,0:T(8,128)S(1)} %get-tuple-element.42.own_logits_ref, f32[501,128]{1,0:T(8,128)S(1)} %get-tuple-element.43.sib_logits_ref, ...), custom_call_target="tpu_custom_call" | custom-call | flops 2101346304 | bytes 20611072 | tf_op jit(solution)/shard_map/pallas_call | solution.py:39
  53.2 2.0 %collective-permute-start.9 = (bf16[64,8192]{1,0:T(8,128)(2,1)S(1)}, bf16[64,8192]{1,0:T(8,128)(2,1)S(1)}, u32[]{:S(2)}, u32[]{:S(2)}) collective-permute-start(bf16[64,8192]{1,0:T(8,128)(2,1)S(1)} %get-tuple-element.53), channel_id=1, source_target_pairs={{56,0},{192,8},{0,24},{216,16},{24,32},{224,40},{32,56},{248,48},{... | collective-permute-start | bytes 3145736 | tf_op jit(solution)/shard_map/ppermute | solution.py:80
  55.1 1.2 %collective-permute-start.12 = (bf16[64,8192]{1,0:T(8,128)(2,1)S(1)}, bf16[64,8192]{1,0:T(8,128)(2,1)S(1)}, u32[]{:S(2)}, u32[]{:S(2)}) collective-permute-start(bf16[64,8192]{1,0:T(8,128)(2,1)S(1)} %get-tuple-element.56), channel_id=1, source_target_pairs={{24,0},{64,8},{32,24},{88,16},{56,32},{96,40},{0,56},{120,48},{80,... | collective-permute-start | bytes 3145736 | tf_op jit(solution)/shard_map/ppermute | solution.py:80
  56.4 2.3 %shard_map.90 = (f32[32,8192]{1,0:T(8,128)S(1)}, bf16[32,8192]{1,0:T(8,128)(2,1)S(1)}, bf16[32,8192]{1,0:T(8,128)(2,1)S(1)}, bf16[32,8192]{1,0:T(8,128)(2,1)S(1)}) custom-call(bf16[128,501]{1,0:T(8,128)(2,1)S(1)} %get-tuple-element.45.own_rest_ref, bf16[128,501]{1,0:T(8,128)(2,1)S(1)} %get-tuple-element.46.sib_rest_ref, ...), custom_call_target="tpu_custom_call" | custom-call | flops 2101346304 | bytes 20611072 | tf_op jit(solution)/shard_map/pallas_call | solution.py:39
  58.7 0.7 collective-permute-start.10
  59.5 2.3 %collective-permute-start.11 = (bf16[32,8192]{1,0:T(8,128)(2,1)S(1)}, bf16[32,8192]{1,0:T(8,128)(2,1)S(1)}, u32[]{:S(2)}, u32[]{:S(2)}) collective-permute-start(bf16[32,8192]{1,0:T(8,128)(2,1)S(1)} %get-tuple-element.55), channel_id=1, source_target_pairs={{32,0},{136,8},{56,24},{144,16},{0,32},{168,40},{24,56},{176,48},{... | collective-permute-start | bytes 1572872 | tf_op jit(solution)/shard_map/ppermute | solution.py:80
  61.8 9.3 %all_to_all.21.got_ref = f32[8,8,128]{2,1,0:T(8,128)S(1)} all-to-all(f32[8,8,128]{2,1,0:T(8,128)S(1)} %get-tuple-element.49), channel_id=1, replica_groups=mesh['y'=4,'x'=4,'c'=2,'z'=8] {'z'}, dimensions={0} | all-to-all | bytes 65536 | tf_op jit(solution)/shard_map/all_to_all | solution.py:30
  71.2 13.8 %all_to_all.22.got_ref = f32[16,8,128]{2,1,0:T(8,128)S(1)} all-to-all(f32[16,8,128]{2,1,0:T(8,128)S(1)} %shard_map.91), channel_id=1, replica_groups={{0,24,32,56,72,80,104,112,128,152,160,184,200,208,232,240},{8,16,40,48,..., dimensions={0} | all-to-all | bytes 131072 | tf_op jit(solution)/shard_map/all_to_all | solution.py:380
  85.0 0.2 shard_map.93
  85.2 0.7 collective-permute-start.13
  85.9 0.0 collective-permute-done.10.far_power_ref
  85.9 0.0 collective-permute-done.11.far_hot_ref
  85.9 0.0 collective-permute-done.9.ahead_ref
  85.9 0.0 collective-permute-done.12.behind_ref
  85.9 1.0 shard_map.92
  86.9 0.0 collective-permute-done.13.sib_part_ref
  86.9 19.8 %all_to_all.23.last_ref = bf16[32,8,1024]{2,1,0:T(8,128)(2,1)S(1)} all-to-all(bf16[32,8,1024]{2,1,0:T(8,128)(2,1)S(1)} %shard_map.92), channel_id=1, replica_groups={{0,1,2,3,4,5,6,7,72,73,74,75,76,77,78,79,128,129,130,131,132,133,134,13..., dimensions={0} | all-to-all | bytes 1048576 | tf_op jit(solution)/shard_map/all_to_all | solution.py:393
  106.7 0.7 shard_map.94
  (12 shorter events, 0.3 us)
Async XLA Ops:
  0.6 19.4 %collective-permute-start = (bf16[501,8192]{1,0:T(8,128)(2,1)}, bf16[501,8192]{1,0:T(8,128)(2,1)S(1)}, u32[]{:S(2)}, u32[]{:S(2)}) collective-permute-start(bf16[501,8192]{1,0:T(8,128)(2,1)} %param.9), channel_id=1, source_target_pairs={{0,8},{8,0},{1,9},{9,1},{2,10},{10,2},{3,11},{11,3},{4,12},{12,4},... | collective-permute-start | bytes 24625160 | tf_op jit(solution)/shard_map/ppermute | solution.py:26
  20.1 9.6 %collective-permute-start.3 = (bf16[8,8192]{1,0:T(8,128)(2,1)S(1)}, bf16[8,8192]{1,0:T(8,128)(2,1)S(1)}, u32[]{:S(2)}, u32[]{:S(2)}) collective-permute-start(bf16[8,8192]{1,0:T(8,128)(2,1)S(1)} %get-tuple-element.37), channel_id=1, source_target_pairs={{200,0},{48,8},{208,24},{8,16},{232,32},{16,40},{240,56},{40,48},{... | collective-permute-start | bytes 393224 | tf_op jit(solution)/shard_map/ppermute | solution.py:80
  22.8 6.9 %collective-permute-start.2 = (bf16[8,8192]{1,0:T(8,128)(2,1)S(1)}, bf16[8,8192]{1,0:T(8,128)(2,1)S(1)}, u32[]{:S(2)}, u32[]{:S(2)}) collective-permute-start(bf16[8,8192]{1,0:T(8,128)(2,1)S(1)} %get-tuple-element.37), channel_id=1, source_target_pairs={{128,0},{40,8},{152,24},{48,16},{160,32},{8,40},{184,56},{16,48},{... | collective-permute-start | bytes 393224 | tf_op jit(solution)/shard_map/ppermute | solution.py:80
  25.2 4.4 %collective-permute-start.1 = (bf16[8,8192]{1,0:T(8,128)(2,1)S(1)}, bf16[8,8192]{1,0:T(8,128)(2,1)S(1)}, u32[]{:S(2)}, u32[]{:S(2)}) collective-permute-start(bf16[8,8192]{1,0:T(8,128)(2,1)S(1)} %get-tuple-element.37), channel_id=1, source_target_pairs={{72,0},{16,8},{80,24},{40,16},{104,32},{48,40},{112,56},{8,48},{12... | collective-permute-start | bytes 393224 | tf_op jit(solution)/shard_map/ppermute | solution.py:80
  25.5 20.3 %collective-permute-start.8 = (bf16[501,8192]{1,0:T(8,128)(2,1)S(1)}, bf16[501,8192]{1,0:T(8,128)(2,1)S(1)}, u32[]{:S(2)}, u32[]{:S(2)}) collective-permute-start(bf16[501,8192]{1,0:T(8,128)(2,1)S(1)} %collective-permute-done.sib_ref), channel_id=1, source_target_pairs={{0,8},{8,0},{1,9},{9,1},{2,10},{10,2},{3,11},{11,3},{4,12},{12,4},... | collective-permute-start | bytes 24625160 | tf_op jit(solution)/shard_map/ppermute | solution.py:26
  29.7 16.1 %collective-permute-start.7 = (bf16[32,8192]{1,0:T(8,128)(2,1)S(1)}, bf16[32,8192]{1,0:T(8,128)(2,1)S(1)}, u32[]{:S(2)}, u32[]{:S(2)}) collective-permute-start(bf16[32,8192]{1,0:T(8,128)(2,1)S(1)} %get-tuple-element.66), channel_id=1, source_target_pairs={{56,0},{192,8},{0,24},{216,16},{24,32},{224,40},{32,56},{248,48},{... | collective-permute-start | bytes 1572872 | tf_op jit(solution)/shard_map/ppermute | solution.py:80
  30.6 9.2 %collective-permute-start.4 = (bf16[32,8192]{1,0:T(8,128)(2,1)S(1)}, bf16[32,8192]{1,0:T(8,128)(2,1)S(1)}, u32[]{:S(2)}, u32[]{:S(2)}) collective-permute-start(bf16[32,8192]{1,0:T(8,128)(2,1)S(1)} %get-tuple-element.66), channel_id=1, source_target_pairs={{24,0},{64,8},{32,24},{88,16},{56,32},{96,40},{0,56},{120,48},{80,... | collective-permute-start | bytes 1572872 | tf_op jit(solution)/shard_map/ppermute | solution.py:80
  32.8 13.0 %collective-permute-start.6 = (bf16[16,8192]{1,0:T(8,128)(2,1)S(1)}, bf16[16,8192]{1,0:T(8,128)(2,1)S(1)}, u32[]{:S(2)}, u32[]{:S(2)}) collective-permute-start(bf16[16,8192]{1,0:T(8,128)(2,1)S(1)} %pad_maximum_fusion.1), channel_id=1, source_target_pairs={{32,0},{136,8},{56,24},{144,16},{0,32},{168,40},{24,56},{176,48},{... | collective-permute-start | bytes 786440 | tf_op jit(solution)/shard_map/ppermute | solution.py:80
  34.6 11.2 %collective-permute-start.5 = (bf16[16,8192]{1,0:T(8,128)(2,1)S(1)}, bf16[16,8192]{1,0:T(8,128)(2,1)S(1)}, u32[]{:S(2)}, u32[]{:S(2)}) collective-permute-start(bf16[16,8192]{1,0:T(8,128)(2,1)S(1)} %pad_maximum_fusion), channel_id=1, source_target_pairs={{32,0},{136,8},{56,24},{144,16},{0,32},{168,40},{24,56},{176,48},{... | collective-permute-start | bytes 786440 | tf_op jit(solution)/shard_map/ppermute | solution.py:80
  53.2 32.7 %collective-permute-start.9 = (bf16[64,8192]{1,0:T(8,128)(2,1)S(1)}, bf16[64,8192]{1,0:T(8,128)(2,1)S(1)}, u32[]{:S(2)}, u32[]{:S(2)}) collective-permute-start(bf16[64,8192]{1,0:T(8,128)(2,1)S(1)} %get-tuple-element.53), channel_id=1, source_target_pairs={{56,0},{192,8},{0,24},{216,16},{24,32},{224,40},{32,56},{248,48},{... | collective-permute-start | bytes 3145736 | tf_op jit(solution)/shard_map/ppermute | solution.py:80
  55.1 30.7 %collective-permute-start.12 = (bf16[64,8192]{1,0:T(8,128)(2,1)S(1)}, bf16[64,8192]{1,0:T(8,128)(2,1)S(1)}, u32[]{:S(2)}, u32[]{:S(2)}) collective-permute-start(bf16[64,8192]{1,0:T(8,128)(2,1)S(1)} %get-tuple-element.56), channel_id=1, source_target_pairs={{24,0},{64,8},{32,24},{88,16},{56,32},{96,40},{0,56},{120,48},{80,... | collective-permute-start | bytes 3145736 | tf_op jit(solution)/shard_map/ppermute | solution.py:80
  58.7 27.1 %collective-permute-start.10 = (bf16[32,8192]{1,0:T(8,128)(2,1)S(1)}, bf16[32,8192]{1,0:T(8,128)(2,1)S(1)}, u32[]{:S(2)}, u32[]{:S(2)}) collective-permute-start(bf16[32,8192]{1,0:T(8,128)(2,1)S(1)} %get-tuple-element.54), channel_id=1, source_target_pairs={{32,0},{136,8},{56,24},{144,16},{0,32},{168,40},{24,56},{176,48},{... | collective-permute-start | bytes 1572872 | tf_op jit(solution)/shard_map/ppermute | solution.py:80
  59.5 26.4 %collective-permute-start.11 = (bf16[32,8192]{1,0:T(8,128)(2,1)S(1)}, bf16[32,8192]{1,0:T(8,128)(2,1)S(1)}, u32[]{:S(2)}, u32[]{:S(2)}) collective-permute-start(bf16[32,8192]{1,0:T(8,128)(2,1)S(1)} %get-tuple-element.55), channel_id=1, source_target_pairs={{32,0},{136,8},{56,24},{144,16},{0,32},{168,40},{24,56},{176,48},{... | collective-permute-start | bytes 1572872 | tf_op jit(solution)/shard_map/ppermute | solution.py:80
  85.2 1.7 %collective-permute-start.13 = (f32[8,128]{1,0:T(8,128)S(1)}, f32[8,128]{1,0:T(8,128)S(1)}, u32[]{:S(2)}, u32[]{:S(2)}) collective-permute-start(f32[8,128]{1,0:T(8,128)S(1)} %get-tuple-element.57.own_part_ref), channel_id=1, source_target_pairs={{0,8},{8,0},{1,9},{9,1},{2,10},{10,2},{3,11},{11,3},{4,12},{12,4},... | collective-permute-start | bytes 12296 | tf_op jit(solution)/shard_map/ppermute | solution.py:26

commit v8 on v7

--- a/solution.py
+++ b/solution.py
@@ -196,6 +196,19 @@
         columns = slice(k * width, (k + 1) * width)
         normed = features_ref[k] * inv_rms * gain_ref[:, columns]
         out_ref[:, columns] = normed.astype(out_ref.dtype)
+
+
+def load_kernel(weight_hbm, out_ref, sems):
+    copies = []
+    for k in range(sems.shape[0]):
+        columns = pl.ds(k * CHUNK, CHUNK)
+        copies.append(
+            pltpu.make_async_copy(weight_hbm.at[:, columns], out_ref.at[:, columns], sems.at[k])
+        )
+    for copy in copies:
+        copy.start()
+    for copy in copies:
+        copy.wait()
 
 
 def places_in(targets_ref, n_z, voc_dev, block):
@@ -446,13 +459,22 @@
         moved=2 * half * full_width,
     )
     normed, sib_weight = lax.optimization_barrier((normed, sib_weight))
-    own_weight = other_core(sib_weight)
     sib_weight = pltpu.with_memory_space_constraint(sib_weight, pltpu.VMEM)
     nearby = gather_from(normed, False)
+    ahead = from_ahead(nearby, 1, True)
+    ahead, own_weight = lax.optimization_barrier((ahead, head_weight))
+    (own_weight,) = run(
+        load_kernel,
+        [((voc_dev, full_width), BF16)],
+        [pltpu.SemaphoreType.DMA((full_width // CHUNK,))],
+        pltpu.with_memory_space_constraint(own_weight, pltpu.HBM),
+        specs=[IN_HBM],
+        moved=4 * voc_dev * full_width,
+    )
     rows = jnp.concatenate(
         [
             nearby,
-            from_ahead(nearby, 1, True),
+            ahead,
             from_ahead(nearby[: block // 2], 2, True),
             from_ahead(nearby[block // 2 :], 2, True),
             from_ahead(nearby, 3, True),

time: 108 us -> 111 us (1.028)
  Pallas kernels: 12.9 us -> 16.4 us
  starting transfers between devices: 23.3 us -> 21.7 us
  waiting for transfers between devices: 12.5 us -> 13.8 us
    pallas_call x8 -> x9, Pallas kernels: 12.2 us -> 15.7 us  [run(): pl.pallas_call(kernel, in_specs=specs or [IN_VMEM] * len(operands), out_s...]
    ppermute x11, waiting for transfers between devices: 12.4 us -> 13.8 us  [from_ahead(): return lax.ppermute(value, CTX, pairs)]
    ppermute x3 -> x2, starting transfers between devices: 5.39 us -> 3.99 us  [other_core(): return lax.ppermute(value, 'c', [(0, 1), (1, 0)])]
  transfers between devices with their start and end apart: 14 -> 13, of which waited for: 3 -> 3; matrix products, arithmetic and copies ran while one was open for 0% -> 0% of each run, Pallas kernels for 5% -> 8%
where the time goes in v8:
time: 111 us
  blocking collectives  57.7 us (52%)
  starting transfers between devices  21.7 us (20%)
  Pallas kernels  16.4 us (15%)
  waiting for transfers between devices  13.8 us (12%)
    all_to_all x2, blocking collectives, exchange(): return lax.all_to_all(value, axes, 0, 0, tiled=True)  24.1 us
    all_to_all x1, blocking collectives, along_inner_and_z(): lax.all_to_all(value, CTX + ('z',), 0, 0, axis_index_groups=groups, tiled...  19.8 us
    ppermute x11, starting transfers between devices, from_ahead(): return lax.ppermute(value, CTX, pairs)  17.7 us
    pallas_call x9, Pallas kernels, run(): pl.pallas_call(kernel, in_specs=specs or [IN_VMEM] * len(operands), out_s...  15.7 us
    ppermute x11, waiting for transfers between devices, from_ahead(): return lax.ppermute(value, CTX, pairs)  13.8 us
    all_to_all x1, blocking collectives, along_plane(): lax.all_to_all(value, CTX, 0, 0, axis_index_groups=groups, tiled=True)  13.8 us
    ppermute x2, starting transfers between devices, other_core(): return lax.ppermute(value, 'c', [(0, 1), (1, 0)])  3.99 us
  transfers between devices with their start and end apart: 13, of which 3 were waited for; matrix products, arithmetic and copies ran while one was open for 0% of the time, Pallas kernels for 8%

profile of v8, /device:TPU:1, one launch (start us, length us, event | category | flops | bytes accessed | tf_op | source)
XLA Modules:
  0.0 110.7 jit_solution(4762924555980263588)
XLA Ops:
  0.6 3.3 %collective-permute-start = (bf16[501,8192]{1,0:T(8,128)(2,1)}, bf16[501,8192]{1,0:T(8,128)(2,1)S(1)}, u32[]{:S(2)}, u32[]{:S(2)}) collective-permute-start(bf16[501,8192]{1,0:T(8,128)(2,1)} %weight_hbm), channel_id=1, source_target_pairs={{0,8},{8,0},{1,9},{9,1},{2,10},{10,2},{3,11},{11,3},{4,12},{12,4},... | collective-permute-start | bytes 24625160 | tf_op jit(solution)/shard_map/ppermute | solution.py:26
  4.0 1.2 %shard_map.86 = (bf16[64,1024]{1,0:T(8,128)(2,1)S(1)}, f32[8,1024]{1,0:T(8,128)S(1)}, f32[1,8192]{1,0:T(1,128)S(1)}, s32[1,128]{1,0:T(1,128)S(1)}, f32[8,128]{1,0:T(8,128)S(1)}, /*index=5*/f32[8,128]{1,0:T(8,128)S(1)}) custom-call(bf16[8,1024]{1,0:T(8,128)(2,1)} %hidden_hbm.1, f32[1,8192]{1,0:T(1,128)} %bitcast.5, s32[1,256]{1,0:T(1,128)} %bitcast.6, ...), custom_call_target="tpu_custom_call" | custom-call | bytes 1048576 | tf_op jit(solution)/shard_map/pallas_call | solution.py:39
  5.1 14.8 %all_to_all.20 = bf16[8,8,1024]{2,1,0:T(8,128)(2,1)S(1)} all-to-all(bf16[8,8,1024]{2,1,0:T(8,128)(2,1)S(1)} %bitcast.4), channel_id=1, replica_groups=mesh['y'=4,'x'=4,'c'=2,'z'=8] {'z'}, dimensions={0} | all-to-all | bytes 262144 | tf_op jit(solution)/shard_map/all_to_all | solution.py:30
  19.9 0.1 shard_map.87
  20.1 0.0 collective-permute-done.sib_ref
  20.1 2.7 %collective-permute-start.3 = (bf16[8,8192]{1,0:T(8,128)(2,1)S(1)}, bf16[8,8192]{1,0:T(8,128)(2,1)S(1)}, u32[]{:S(2)}, u32[]{:S(2)}) collective-permute-start(bf16[8,8192]{1,0:T(8,128)(2,1)S(1)} %get-tuple-element.39), channel_id=1, source_target_pairs={{200,0},{48,8},{208,24},{8,16},{232,32},{16,40},{240,56},{40,48},{... | collective-permute-start | bytes 393224 | tf_op jit(solution)/shard_map/ppermute | solution.py:80
  22.8 2.5 %collective-permute-start.2 = (bf16[8,8192]{1,0:T(8,128)(2,1)S(1)}, bf16[8,8192]{1,0:T(8,128)(2,1)S(1)}, u32[]{:S(2)}, u32[]{:S(2)}) collective-permute-start(bf16[8,8192]{1,0:T(8,128)(2,1)S(1)} %get-tuple-element.39), channel_id=1, source_target_pairs={{128,0},{40,8},{152,24},{48,16},{160,32},{8,40},{184,56},{16,48},{... | collective-permute-start | bytes 393224 | tf_op jit(solution)/shard_map/ppermute | solution.py:80
  25.2 0.3 collective-permute-start.1
  25.6 4.0 %collective-permute-done.1 = bf16[8,8192]{1,0:T(8,128)(2,1)S(1)} collective-permute-done((bf16[8,8192]{1,0:T(8,128)(2,1)S(1)}, bf16[8,8192]{1,0:T(8,128)(2,1)S(1)}, u32[]{:S(2)}, u32[]{:S(2)}) %collective-permute-start.1) | collective-permute-done | bytes 131104 | tf_op jit(solution)/shard_map/ppermute | solution.py:80
  29.6 0.0 collective-permute-done.2
  29.7 0.0 collective-permute-done.3
  29.7 0.9 collective-permute-start.7
  30.6 2.1 %collective-permute-start.4 = (bf16[32,8192]{1,0:T(8,128)(2,1)S(1)}, bf16[32,8192]{1,0:T(8,128)(2,1)S(1)}, u32[]{:S(2)}, u32[]{:S(2)}) collective-permute-start(bf16[32,8192]{1,0:T(8,128)(2,1)S(1)} %get-tuple-element.70), channel_id=1, source_target_pairs={{24,0},{64,8},{32,24},{88,16},{56,32},{96,40},{0,56},{120,48},{80,... | collective-permute-start | bytes 1572872 | tf_op jit(solution)/shard_map/ppermute | solution.py:80
  32.8 1.8 %collective-permute-start.6 = (bf16[16,8192]{1,0:T(8,128)(2,1)S(1)}, bf16[16,8192]{1,0:T(8,128)(2,1)S(1)}, u32[]{:S(2)}, u32[]{:S(2)}) collective-permute-start(bf16[16,8192]{1,0:T(8,128)(2,1)S(1)} %pad_maximum_fusion.1), channel_id=1, source_target_pairs={{32,0},{136,8},{56,24},{144,16},{0,32},{168,40},{24,56},{176,48},{... | collective-permute-start | bytes 786440 | tf_op jit(solution)/shard_map/ppermute | solution.py:80
  34.6 1.4 %collective-permute-start.5 = (bf16[16,8192]{1,0:T(8,128)(2,1)S(1)}, bf16[16,8192]{1,0:T(8,128)(2,1)S(1)}, u32[]{:S(2)}, u32[]{:S(2)}) collective-permute-start(bf16[16,8192]{1,0:T(8,128)(2,1)S(1)} %pad_maximum_fusion), channel_id=1, source_target_pairs={{32,0},{136,8},{56,24},{144,16},{0,32},{168,40},{24,56},{176,48},{... | collective-permute-start | bytes 786440 | tf_op jit(solution)/shard_map/ppermute | solution.py:80
  35.9 3.9 %collective-permute-done.4 = bf16[32,8192]{1,0:T(8,128)(2,1)S(1)} collective-permute-done((bf16[32,8192]{1,0:T(8,128)(2,1)S(1)}, bf16[32,8192]{1,0:T(8,128)(2,1)S(1)}, u32[]{:S(2)}, u32[]{:S(2)}) %collective-permute-start.4) | collective-permute-done | bytes 524320 | tf_op jit(solution)/shard_map/ppermute | solution.py:80
  39.8 5.9 %collective-permute-done.5 = bf16[16,8192]{1,0:T(8,128)(2,1)S(1)} collective-permute-done((bf16[16,8192]{1,0:T(8,128)(2,1)S(1)}, bf16[16,8192]{1,0:T(8,128)(2,1)S(1)}, u32[]{:S(2)}, u32[]{:S(2)}) %collective-permute-start.5) | collective-permute-done | bytes 262176 | tf_op jit(solution)/shard_map/ppermute | solution.py:80
  45.8 3.5 %shard_map.88.own_ref = bf16[501,8192]{1,0:T(8,128)(2,1)S(1)} custom-call(bf16[501,8192]{1,0:T(8,128)(2,1)} %weight_hbm), custom_call_target="tpu_custom_call" | custom-call | bytes 16416768 | tf_op jit(solution)/shard_map/pallas_call | solution.py:39
  49.2 0.0 collective-permute-done.6
  49.3 0.0 collective-permute-done.7
  49.3 4.8 %shard_map.89 = (f32[501,128]{1,0:T(8,128)S(1)}, f32[501,128]{1,0:T(8,128)S(1)}, f32[8,8,128]{2,1,0:T(8,128)S(1)}, f32[8,128]{1,0:T(8,128)S(1)}, f32[8,128]{1,0:T(8,128)S(1)}) custom-call(bf16[128,8192]{1,0:T(8,128)(2,1)S(1)} %constant_dynamic-update-slice_fusion.4.rows_ref, bf16[501,8192]{1,0:T(8,128)(2,1)S(1)} %shard_map.88.own_ref, ...), custom_call_target="tpu_custom_call" | custom-call | flops 2101346304 | bytes 20611072 | tf_op jit(solution)/shard_map/pallas_call | solution.py:39
  54.1 2.5 %shard_map.90 = (bf16[64,8192]{1,0:T(8,128)(2,1)S(1)}, bf16[64,8192]{1,0:T(8,128)(2,1)S(1)}, bf16[128,501]{1,0:T(8,128)(2,1)S(1)}, bf16[128,501]{1,0:T(8,128)(2,1)S(1)}) custom-call(f32[501,128]{1,0:T(8,128)S(1)} %get-tuple-element.46.own_logits_ref, f32[501,128]{1,0:T(8,128)S(1)} %get-tuple-element.47.sib_logits_ref, ...), custom_call_target="tpu_custom_call" | custom-call | flops 2101346304 | bytes 20611072 | tf_op jit(solution)/shard_map/pallas_call | solution.py:39
  56.6 1.8 %collective-permute-start.8 = (bf16[64,8192]{1,0:T(8,128)(2,1)S(1)}, bf16[64,8192]{1,0:T(8,128)(2,1)S(1)}, u32[]{:S(2)}, u32[]{:S(2)}) collective-permute-start(bf16[64,8192]{1,0:T(8,128)(2,1)S(1)} %get-tuple-element.57), channel_id=1, source_target_pairs={{56,0},{192,8},{0,24},{216,16},{24,32},{224,40},{32,56},{248,48},{... | collective-permute-start | bytes 3145736 | tf_op jit(solution)/shard_map/ppermute | solution.py:80
  58.4 1.2 %collective-permute-start.11 = (bf16[64,8192]{1,0:T(8,128)(2,1)S(1)}, bf16[64,8192]{1,0:T(8,128)(2,1)S(1)}, u32[]{:S(2)}, u32[]{:S(2)}) collective-permute-start(bf16[64,8192]{1,0:T(8,128)(2,1)S(1)} %get-tuple-element.60), channel_id=1, source_target_pairs={{24,0},{64,8},{32,24},{88,16},{56,32},{96,40},{0,56},{120,48},{80,... | collective-permute-start | bytes 3145736 | tf_op jit(solution)/shard_map/ppermute | solution.py:80
  59.7 2.3 %shard_map.91 = (f32[32,8192]{1,0:T(8,128)S(1)}, bf16[32,8192]{1,0:T(8,128)(2,1)S(1)}, bf16[32,8192]{1,0:T(8,128)(2,1)S(1)}, bf16[32,8192]{1,0:T(8,128)(2,1)S(1)}) custom-call(bf16[128,501]{1,0:T(8,128)(2,1)S(1)} %get-tuple-element.49.own_rest_ref, bf16[128,501]{1,0:T(8,128)(2,1)S(1)} %get-tuple-element.50.sib_rest_ref, ...), custom_call_target="tpu_custom_call" | custom-call | flops 2101346304 | bytes 20611072 | tf_op jit(solution)/shard_map/pallas_call | solution.py:39
  62.0 0.9 collective-permute-start.9
  62.9 2.2 %collective-permute-start.10 = (bf16[32,8192]{1,0:T(8,128)(2,1)S(1)}, bf16[32,8192]{1,0:T(8,128)(2,1)S(1)}, u32[]{:S(2)}, u32[]{:S(2)}) collective-permute-start(bf16[32,8192]{1,0:T(8,128)(2,1)S(1)} %get-tuple-element.59), channel_id=1, source_target_pairs={{32,0},{136,8},{56,24},{144,16},{0,32},{168,40},{24,56},{176,48},{... | collective-permute-start | bytes 1572872 | tf_op jit(solution)/shard_map/ppermute | solution.py:80
  65.1 9.3 %all_to_all.21.got_ref = f32[8,8,128]{2,1,0:T(8,128)S(1)} all-to-all(f32[8,8,128]{2,1,0:T(8,128)S(1)} %get-tuple-element.53), channel_id=1, replica_groups=mesh['y'=4,'x'=4,'c'=2,'z'=8] {'z'}, dimensions={0} | all-to-all | bytes 65536 | tf_op jit(solution)/shard_map/all_to_all | solution.py:30
  74.5 13.8 %all_to_all.22.got_ref = f32[16,8,128]{2,1,0:T(8,128)S(1)} all-to-all(f32[16,8,128]{2,1,0:T(8,128)S(1)} %shard_map.92), channel_id=1, replica_groups={{0,24,32,56,72,80,104,112,128,152,160,184,200,208,232,240},{8,16,40,48,..., dimensions={0} | all-to-all | bytes 131072 | tf_op jit(solution)/shard_map/all_to_all | solution.py:393
  88.3 0.2 shard_map.94
  88.5 0.7 collective-permute-start.12
  89.2 0.0 collective-permute-done.9.far_power_ref
  89.2 0.0 collective-permute-done.10.far_hot_ref
  89.2 0.0 collective-permute-done.8.ahead_ref
  89.2 0.0 collective-permute-done.11.behind_ref
  89.2 1.0 shard_map.93
  90.2 0.0 collective-permute-done.12.sib_part_ref
  90.2 19.8 %all_to_all.23.last_ref = bf16[32,8,1024]{2,1,0:T(8,128)(2,1)S(1)} all-to-all(bf16[32,8,1024]{2,1,0:T(8,128)(2,1)S(1)} %shard_map.93), channel_id=1, replica_groups={{0,1,2,3,4,5,6,7,72,73,74,75,76,77,78,79,128,129,130,131,132,133,134,13..., dimensions={0} | all-to-all | bytes 1048576 | tf_op jit(solution)/shard_map/all_to_all | solution.py:406
  110.0 0.7 shard_map.95
  (12 shorter events, 0.3 us)
Async XLA Ops:
  0.6 19.4 %collective-permute-start = (bf16[501,8192]{1,0:T(8,128)(2,1)}, bf16[501,8192]{1,0:T(8,128)(2,1)S(1)}, u32[]{:S(2)}, u32[]{:S(2)}) collective-permute-start(bf16[501,8192]{1,0:T(8,128)(2,1)} %weight_hbm), channel_id=1, source_target_pairs={{0,8},{8,0},{1,9},{9,1},{2,10},{10,2},{3,11},{11,3},{4,12},{12,4},... | collective-permute-start | bytes 24625160 | tf_op jit(solution)/shard_map/ppermute | solution.py:26
  20.1 9.6 %collective-permute-start.3 = (bf16[8,8192]{1,0:T(8,128)(2,1)S(1)}, bf16[8,8192]{1,0:T(8,128)(2,1)S(1)}, u32[]{:S(2)}, u32[]{:S(2)}) collective-permute-start(bf16[8,8192]{1,0:T(8,128)(2,1)S(1)} %get-tuple-element.39), channel_id=1, source_target_pairs={{200,0},{48,8},{208,24},{8,16},{232,32},{16,40},{240,56},{40,48},{... | collective-permute-start | bytes 393224 | tf_op jit(solution)/shard_map/ppermute | solution.py:80
  22.8 6.9 %collective-permute-start.2 = (bf16[8,8192]{1,0:T(8,128)(2,1)S(1)}, bf16[8,8192]{1,0:T(8,128)(2,1)S(1)}, u32[]{:S(2)}, u32[]{:S(2)}) collective-permute-start(bf16[8,8192]{1,0:T(8,128)(2,1)S(1)} %get-tuple-element.39), channel_id=1, source_target_pairs={{128,0},{40,8},{152,24},{48,16},{160,32},{8,40},{184,56},{16,48},{... | collective-permute-start | bytes 393224 | tf_op jit(solution)/shard_map/ppermute | solution.py:80
  25.2 4.4 %collective-permute-start.1 = (bf16[8,8192]{1,0:T(8,128)(2,1)S(1)}, bf16[8,8192]{1,0:T(8,128)(2,1)S(1)}, u32[]{:S(2)}, u32[]{:S(2)}) collective-permute-start(bf16[8,8192]{1,0:T(8,128)(2,1)S(1)} %get-tuple-element.39), channel_id=1, source_target_pairs={{72,0},{16,8},{80,24},{40,16},{104,32},{48,40},{112,56},{8,48},{12... | collective-permute-start | bytes 393224 | tf_op jit(solution)/shard_map/ppermute | solution.py:80
  29.7 19.6 %collective-permute-start.7 = (bf16[32,8192]{1,0:T(8,128)(2,1)S(1)}, bf16[32,8192]{1,0:T(8,128)(2,1)S(1)}, u32[]{:S(2)}, u32[]{:S(2)}) collective-permute-start(bf16[32,8192]{1,0:T(8,128)(2,1)S(1)} %get-tuple-element.70), channel_id=1, source_target_pairs={{56,0},{192,8},{0,24},{216,16},{24,32},{224,40},{32,56},{248,48},{... | collective-permute-start | bytes 1572872 | tf_op jit(solution)/shard_map/ppermute | solution.py:80
  30.6 9.2 %collective-permute-start.4 = (bf16[32,8192]{1,0:T(8,128)(2,1)S(1)}, bf16[32,8192]{1,0:T(8,128)(2,1)S(1)}, u32[]{:S(2)}, u32[]{:S(2)}) collective-permute-start(bf16[32,8192]{1,0:T(8,128)(2,1)S(1)} %get-tuple-element.70), channel_id=1, source_target_pairs={{24,0},{64,8},{32,24},{88,16},{56,32},{96,40},{0,56},{120,48},{80,... | collective-permute-start | bytes 1572872 | tf_op jit(solution)/shard_map/ppermute | solution.py:80
  32.8 16.5 %collective-permute-start.6 = (bf16[16,8192]{1,0:T(8,128)(2,1)S(1)}, bf16[16,8192]{1,0:T(8,128)(2,1)S(1)}, u32[]{:S(2)}, u32[]{:S(2)}) collective-permute-start(bf16[16,8192]{1,0:T(8,128)(2,1)S(1)} %pad_maximum_fusion.1), channel_id=1, source_target_pairs={{32,0},{136,8},{56,24},{144,16},{0,32},{168,40},{24,56},{176,48},{... | collective-permute-start | bytes 786440 | tf_op jit(solution)/shard_map/ppermute | solution.py:80
  34.6 11.2 %collective-permute-start.5 = (bf16[16,8192]{1,0:T(8,128)(2,1)S(1)}, bf16[16,8192]{1,0:T(8,128)(2,1)S(1)}, u32[]{:S(2)}, u32[]{:S(2)}) collective-permute-start(bf16[16,8192]{1,0:T(8,128)(2,1)S(1)} %pad_maximum_fusion), channel_id=1, source_target_pairs={{32,0},{136,8},{56,24},{144,16},{0,32},{168,40},{24,56},{176,48},{... | collective-permute-start | bytes 786440 | tf_op jit(solution)/shard_map/ppermute | solution.py:80
  56.6 32.5 %collective-permute-start.8 = (bf16[64,8192]{1,0:T(8,128)(2,1)S(1)}, bf16[64,8192]{1,0:T(8,128)(2,1)S(1)}, u32[]{:S(2)}, u32[]{:S(2)}) collective-permute-start(bf16[64,8192]{1,0:T(8,128)(2,1)S(1)} %get-tuple-element.57), channel_id=1, source_target_pairs={{56,0},{192,8},{0,24},{216,16},{24,32},{224,40},{32,56},{248,48},{... | collective-permute-start | bytes 3145736 | tf_op jit(solution)/shard_map/ppermute | solution.py:80
  58.4 30.8 %collective-permute-start.11 = (bf16[64,8192]{1,0:T(8,128)(2,1)S(1)}, bf16[64,8192]{1,0:T(8,128)(2,1)S(1)}, u32[]{:S(2)}, u32[]{:S(2)}) collective-permute-start(bf16[64,8192]{1,0:T(8,128)(2,1)S(1)} %get-tuple-element.60), channel_id=1, source_target_pairs={{24,0},{64,8},{32,24},{88,16},{56,32},{96,40},{0,56},{120,48},{80,... | collective-permute-start | bytes 3145736 | tf_op jit(solution)/shard_map/ppermute | solution.py:80
  62.0 27.1 %collective-permute-start.9 = (bf16[32,8192]{1,0:T(8,128)(2,1)S(1)}, bf16[32,8192]{1,0:T(8,128)(2,1)S(1)}, u32[]{:S(2)}, u32[]{:S(2)}) collective-permute-start(bf16[32,8192]{1,0:T(8,128)(2,1)S(1)} %get-tuple-element.58), channel_id=1, source_target_pairs={{32,0},{136,8},{56,24},{144,16},{0,32},{168,40},{24,56},{176,48},{... | collective-permute-start | bytes 1572872 | tf_op jit(solution)/shard_map/ppermute | solution.py:80
  62.9 26.3 %collective-permute-start.10 = (bf16[32,8192]{1,0:T(8,128)(2,1)S(1)}, bf16[32,8192]{1,0:T(8,128)(2,1)S(1)}, u32[]{:S(2)}, u32[]{:S(2)}) collective-permute-start(bf16[32,8192]{1,0:T(8,128)(2,1)S(1)} %get-tuple-element.59), channel_id=1, source_target_pairs={{32,0},{136,8},{56,24},{144,16},{0,32},{168,40},{24,56},{176,48},{... | collective-permute-start | bytes 1572872 | tf_op jit(solution)/shard_map/ppermute | solution.py:80
  88.5 1.7 %collective-permute-start.12 = (f32[8,128]{1,0:T(8,128)S(1)}, f32[8,128]{1,0:T(8,128)S(1)}, u32[]{:S(2)}, u32[]{:S(2)}) collective-permute-start(f32[8,128]{1,0:T(8,128)S(1)} %get-tuple-element.61.own_part_ref), channel_id=1, source_target_pairs={{0,8},{8,0},{1,9},{9,1},{2,10},{10,2},{3,11},{11,3},{4,12},{12,4},... | collective-permute-start | bytes 12296 | tf_op jit(solution)/shard_map/ppermute | solution.py:26
